TPU v7x, 256 devices: a whole 4x4x8 slice. The times are simulated.
256 devices in a mesh: pipe: 8 (over y, core), dp: 16 (over x_lo, z), tensor: 2 (over x_hi).
Axes of the slice: x: 4 (x_hi: 2, x_lo: 2; x = x_hi * 2 + x_lo), y: 4, z: 8, core: 2. Of those that a mesh axis runs over, the one named last changes fastest.
Arguments:
- codes_in: bfloat16 [4, 2048, 512], P(None, 'dp'), may hold values from -6 to 6
- lengths: int32 [4, 32], P(None, 'dp'), may hold values from 1 to 64, as said below
- dec_weight: bfloat16 [8, 512, 8192], P('pipe', 'dp', 'tensor'), may hold values from -0.25 to 0.25
- enc_weight: bfloat16 [8, 512, 8192], P('pipe', 'dp', 'tensor'), may hold values from -0.0625 to 0.0625
- head: bfloat16 [512], replicated, may hold values from -0.25 to 0.25
Outputs:
- code_grads: float32 [8, 4, 2048, 512], P('pipe', None, ('dp', 'tensor'))
- dec_grad: float32 [8, 512, 8192], P('pipe', 'dp', 'tensor')
- enc_grad: float32 [8, 512, 8192], P('pipe', 'dp', 'tensor')
Inputs may be any that keep to these rules, and one draw needn't show every extreme that they name: `lengths`: positions from a sequence's length to 63 are padding; some sequence is full and some holds one token.
All inputs are finite; a program needn't handle non-finite values.
Results may differ from a plain program's by a relative error of at most 0.04.
Values may be sent and summed in bfloat16 or wider, within the bound.
No kernel may reach another device: no remote copies, remote signals or barrier semaphores. Data moves between devices by JAX's collectives and lax.ppermute only.
A program may use at most 128 MiB of HBM per device.

v0:
```python
import jax
import jax.numpy as jnp
from jax import lax
from jax.sharding import PartitionSpec as P

eps = 1e-05
loss_scale = 512.0


def shifted(value, axis, steps):
    count = lax.axis_size(axis)
    initial, last = (max(0, -steps), min(count, count - steps))
    return lax.ppermute(value, axis, [(source, source + steps) for source in range(initial, last)])


def code_norm(codes):
    values = codes.astype(jnp.float32)
    scales = lax.rsqrt(jnp.mean(values * values, axis=-1, keepdims=True) + eps)
    return (values, scales, (values * scales).astype(jnp.bfloat16))


def silu_slope(hidden):
    sigmoid = jax.nn.sigmoid(hidden)
    return sigmoid * (1.0 + hidden * (1.0 - sigmoid))


def contract_last(left, right):
    return lax.dot_general(
        left, right, (((1,), (1,)), ((), ())), preferred_element_type=jnp.float32
    )


def contract_first(left, right):
    return lax.dot_general(
        left, right, (((0,), (0,)), ((), ())), preferred_element_type=jnp.float32
    )


def input_grad(grad_out, values, scales, summed):
    inner = jnp.mean(summed * values, axis=-1, keepdims=True)
    return (
        grad_out.astype(jnp.float32) + scales * summed - values * (scales * scales * scales) * inner
    )


def reward_seed(final_codes, head, lengths):
    micro_count, row_count, width = final_codes.shape
    seq_count = lengths.shape[1]
    seq_len = row_count // seq_count
    scores = jnp.dot(final_codes.reshape(-1, width), head, preferred_element_type=jnp.float32)
    scores = scores.reshape(micro_count, seq_count, seq_len)
    positions = jnp.arange(seq_len, dtype=jnp.int32)
    valid_mask = (positions[None, None, :] < lengths[:, :, None]).astype(jnp.float32)
    counts = lengths.astype(jnp.float32)
    rewards = jnp.sum(scores * valid_mask, axis=-1) / counts
    paired = rewards.reshape(micro_count, seq_count // 2, 2)
    weight = loss_scale * jax.nn.sigmoid(paired[..., 1] - paired[..., 0])
    reward_grad = jnp.stack([-weight, weight], axis=-1).reshape(micro_count, seq_count)
    token_grad = (reward_grad / counts)[:, :, None] * valid_mask
    token_grad = token_grad.reshape(micro_count, row_count)
    return (token_grad[:, :, None] * head.astype(jnp.float32)).astype(jnp.bfloat16)


def store_slot(store, slot_index, update, is_active):
    previous = lax.dynamic_index_in_dim(store, slot_index, 0, keepdims=False)
    return lax.dynamic_update_index_in_dim(
        store, jnp.where(is_active, update, previous), slot_index, 0
    )


def on_device(codes_in, lengths, dec_weight, enc_weight, head):
    section_count = lax.axis_size("pipe")
    section_index = lax.axis_index("pipe")
    split_count = lax.axis_size("tensor")
    tensor_index = lax.axis_index("tensor")
    micro_count, row_count, width = codes_in.shape
    share_rows = row_count // split_count
    last_section = section_count - 1
    tick_count = micro_count + section_count - 1
    decoder, encoder = (
        lax.all_gather(dec_weight[0], "dp", axis=0, tiled=True),
        lax.all_gather(enc_weight[0], "dp", axis=0, tiled=True),
    )
    columns = decoder.shape[1]

    def forward_branch(in_codes):
        values, scales, normed = code_norm(in_codes)
        hidden = jnp.dot(normed, decoder, preferred_element_type=jnp.float32)
        gated = jax.nn.silu(hidden).astype(jnp.bfloat16)
        return (hidden, contract_last(gated, encoder))

    def forward_empty(in_codes):
        return (
            jnp.zeros((row_count, columns), jnp.float32),
            jnp.zeros((row_count, width), jnp.float32),
        )

    def forward_tick(state_tuple, tick_index):
        received, code_store, hidden_store, final_store = state_tuple
        micro_index = tick_index - section_index
        is_active = (micro_index >= 0) & (micro_index < micro_count)
        slot_index = jnp.clip(micro_index, 0, micro_count - 1)
        first_codes = lax.dynamic_index_in_dim(codes_in, slot_index, 0, keepdims=False)
        in_codes = jnp.where(section_index == 0, first_codes, received)
        hidden, partial_value = lax.cond(is_active, forward_branch, forward_empty, in_codes)
        summed = lax.psum(partial_value.astype(jnp.bfloat16), "tensor").astype(jnp.float32)
        result = (in_codes.astype(jnp.float32) + summed).astype(jnp.bfloat16)
        outgoing = shifted(result, "pipe", 1)
        code_store = store_slot(code_store, slot_index, in_codes, is_active)
        hidden_store = store_slot(hidden_store, slot_index, hidden, is_active)
        final_store = store_slot(
            final_store, slot_index, result, is_active & (section_index == last_section)
        )
        return ((outgoing, code_store, hidden_store, final_store), None)

    forward_start = (
        jnp.zeros((row_count, width), jnp.bfloat16),
        jnp.zeros((micro_count, row_count, width), jnp.bfloat16),
        jnp.zeros((micro_count, row_count, columns), jnp.float32),
        jnp.zeros((micro_count, row_count, width), jnp.bfloat16),
    )
    forward_state, unused_out = lax.scan(
        forward_tick, forward_start, jnp.arange(tick_count, dtype=jnp.int32)
    )
    code_store = forward_state[1]
    hidden_store = forward_state[2]
    final_codes = forward_state[3]
    seed_grads = reward_seed(final_codes, head, lengths)

    def backward_branch(grad_out, in_codes, hidden, dec_sum, enc_sum):
        values, scales, normed = code_norm(in_codes)
        gated = jax.nn.silu(hidden).astype(jnp.bfloat16)
        gated_grad = jnp.dot(grad_out, encoder, preferred_element_type=jnp.float32)
        hidden_grad = (gated_grad * silu_slope(hidden)).astype(jnp.bfloat16)
        partial_value = contract_last(hidden_grad, decoder)
        enc_sum = enc_sum + contract_first(grad_out, gated)
        dec_sum = dec_sum + contract_first(normed, hidden_grad)
        return (partial_value, dec_sum, enc_sum)

    def backward_empty(grad_out, in_codes, hidden, dec_sum, enc_sum):
        return (jnp.zeros((row_count, width), jnp.float32), dec_sum, enc_sum)

    def backward_tick(state_tuple, tick_index):
        received, dec_sum, enc_sum, grad_store = state_tuple
        micro_index = tick_index - (last_section - section_index)
        is_active = (micro_index >= 0) & (micro_index < micro_count)
        slot_index = jnp.clip(micro_index, 0, micro_count - 1)
        seed_rows = lax.dynamic_index_in_dim(seed_grads, slot_index, 0, keepdims=False)
        grad_out = jnp.where(section_index == last_section, seed_rows, received)
        in_codes = lax.dynamic_index_in_dim(code_store, slot_index, 0, keepdims=False)
        hidden = lax.dynamic_index_in_dim(hidden_store, slot_index, 0, keepdims=False)
        partial_value, dec_sum, enc_sum = lax.cond(
            is_active, backward_branch, backward_empty, grad_out, in_codes, hidden, dec_sum, enc_sum
        )
        values, scales, normed = code_norm(in_codes)
        summed = lax.psum(partial_value.astype(jnp.bfloat16), "tensor").astype(jnp.float32)
        grad_full = input_grad(grad_out, values, scales, summed)
        outgoing = shifted(grad_full.astype(jnp.bfloat16), "pipe", -1)
        piece = lax.dynamic_slice_in_dim(grad_full, tensor_index * share_rows, share_rows, 0)
        grad_store = store_slot(grad_store, slot_index, piece, is_active)
        return ((outgoing, dec_sum, enc_sum, grad_store), None)

    backward_start = (
        jnp.zeros((row_count, width), jnp.bfloat16),
        jnp.zeros((width, columns), jnp.float32),
        jnp.zeros((width, columns), jnp.float32),
        jnp.zeros((micro_count, share_rows, width), jnp.float32),
    )
    backward_state, unused_back = lax.scan(
        backward_tick, backward_start, jnp.arange(tick_count, dtype=jnp.int32)
    )
    dec_term = backward_state[1].astype(jnp.bfloat16).astype(jnp.float32)
    enc_term = backward_state[2].astype(jnp.bfloat16).astype(jnp.float32)
    dec_grad, enc_grad = (
        lax.psum_scatter(
            dec_term.astype(jnp.bfloat16), "dp", scatter_dimension=0, tiled=True
        ).astype(jnp.float32),
        lax.psum_scatter(
            enc_term.astype(jnp.bfloat16), "dp", scatter_dimension=0, tiled=True
        ).astype(jnp.float32),
    )
    return (backward_state[3][None], dec_grad[None], enc_grad[None])


def solution(mesh):
    in_specs = (
        P(None, "dp", None),
        P(None, "dp"),
        P("pipe", "dp", "tensor"),
        P("pipe", "dp", "tensor"),
        P(),
    )
    out_specs = (
        P("pipe", None, ("dp", "tensor"), None),
        P("pipe", "dp", "tensor"),
        P("pipe", "dp", "tensor"),
    )
    return jax.shard_map(
        on_device, mesh=mesh, in_specs=in_specs, out_specs=out_specs, check_vma=False
    )
```

profile of v0, /device:TPU:1, one launch (start us, length us, event | category | flops | bytes accessed | tf_op | source)
XLA Modules:
  0.0 1569.3 jit_solution(14353121129989085273)
XLA Ops:
  11.6 70.0 %all-gather.5.cloned.1.call-done = bf16[1,512,4096]{2,1,0:T(8,128)(2,1)} async-done(((bf16[1,32,4096]{2,1,0:T(8,128)(2,1)}), bf16[1,512,4096]{2,1,0:T(8,128)(2,1)}) %all-gather.5.cloned.1.call-update) | async-done | bytes 4194320 | tf_op jit(solution)/shard_map/all_gather | solution.py:81
  81.7 76.1 %all-gather.7.cloned.1.call-done = bf16[1,512,4096]{2,1,0:T(8,128)(2,1)} async-done(((bf16[1,32,4096]{2,1,0:T(8,128)(2,1)}), bf16[1,512,4096]{2,1,0:T(8,128)(2,1)}) %all-gather.7.cloned.1.call-update) | async-done | bytes 4194320 | tf_op jit(solution)/shard_map/all_gather | solution.py:82
  162.6 574.1 %while.35 = (s32[]{:T(128)}, bf16[128,512]{1,0:T(8,128)(2,1)S(1)}, bf16[4,128,512]{2,1,0:T(8,128)(2,1)S(1)}, f32[4,128,4096]{2,1,0:T(8,128)}, bf16[4,128,512]{2,...) while((s32[]{:T(128)}, bf16[128,512]{1,0:T(8,128)(2,1)S(1)}, ...), condition=%wide.region_5.6_spmd, body=%wide.region_0.5_spmd.sunk | while | flops 1077805184 | bytes 43911596 | solution.py:122
  169.5 42.5 %all-reduce.3.cloned.1.call-done = bf16[128,512]{1,0:T(8,128)(2,1)} async-done(((bf16[128,512]{1,0:T(8,128)(2,1)}), bf16[128,512]{1,0:T(8,128)(2,1)}) %all-reduce.3.cloned.1.call-update) | async-done | bytes 131088 | tf_op jit(solution)/shard_map/while/body/eval_jaxpr/psum | solution.py:106
  385.1 31.5 %all-reduce.3.cloned.1.call-done = bf16[128,512]{1,0:T(8,128)(2,1)} async-done(((bf16[128,512]{1,0:T(8,128)(2,1)}), bf16[128,512]{1,0:T(8,128)(2,1)}) %all-reduce.3.cloned.1.call-update) | async-done | bytes 131088 | tf_op jit(solution)/shard_map/while/body/eval_jaxpr/psum | solution.py:106
  431.7 37.6 %all-reduce.3.cloned.1.call-done = bf16[128,512]{1,0:T(8,128)(2,1)} async-done(((bf16[128,512]{1,0:T(8,128)(2,1)}), bf16[128,512]{1,0:T(8,128)(2,1)}) %all-reduce.3.cloned.1.call-update) | async-done | bytes 131088 | tf_op jit(solution)/shard_map/while/body/eval_jaxpr/psum | solution.py:106
  483.2 38.9 %all-reduce.3.cloned.1.call-done = bf16[128,512]{1,0:T(8,128)(2,1)} async-done(((bf16[128,512]{1,0:T(8,128)(2,1)}), bf16[128,512]{1,0:T(8,128)(2,1)}) %all-reduce.3.cloned.1.call-update) | async-done | bytes 131088 | tf_op jit(solution)/shard_map/while/body/eval_jaxpr/psum | solution.py:106
  536.0 38.9 %all-reduce.3.cloned.1.call-done = bf16[128,512]{1,0:T(8,128)(2,1)} async-done(((bf16[128,512]{1,0:T(8,128)(2,1)}), bf16[128,512]{1,0:T(8,128)(2,1)}) %all-reduce.3.cloned.1.call-update) | async-done | bytes 131088 | tf_op jit(solution)/shard_map/while/body/eval_jaxpr/psum | solution.py:106
  588.8 38.6 %all-reduce.3.cloned.1.call-done = bf16[128,512]{1,0:T(8,128)(2,1)} async-done(((bf16[128,512]{1,0:T(8,128)(2,1)}), bf16[128,512]{1,0:T(8,128)(2,1)}) %all-reduce.3.cloned.1.call-update) | async-done | bytes 131088 | tf_op jit(solution)/shard_map/while/body/eval_jaxpr/psum | solution.py:106
  641.3 38.6 %all-reduce.3.cloned.1.call-done = bf16[128,512]{1,0:T(8,128)(2,1)} async-done(((bf16[128,512]{1,0:T(8,128)(2,1)}), bf16[128,512]{1,0:T(8,128)(2,1)}) %all-reduce.3.cloned.1.call-update) | async-done | bytes 131088 | tf_op jit(solution)/shard_map/while/body/eval_jaxpr/psum | solution.py:106
  693.9 35.8 %all-reduce.3.cloned.1.call-done = bf16[128,512]{1,0:T(8,128)(2,1)} async-done(((bf16[128,512]{1,0:T(8,128)(2,1)}), bf16[128,512]{1,0:T(8,128)(2,1)}) %all-reduce.3.cloned.1.call-update) | async-done | bytes 131088 | tf_op jit(solution)/shard_map/while/body/eval_jaxpr/psum | solution.py:106
  747.1 658.3 %while.36 = (s32[]{:T(128)}, bf16[128,512]{1,0:T(8,128)(2,1)S(1)}, f32[512,4096]{1,0:T(8,128)}, f32[512,4096]{0,1:T(8,128)}, f32[4,64,512]{2,1,0:T(8,128)S(1)}, ...) while((s32[]{:T(128)}, bf16[128,512]{1,0:T(8,128)(2,1)S(1)}, ...), condition=%wide.region_14.15_spmd, body=%wide.region_7.14_spmd.sunk | while | flops 2160558592 | bytes 196747408 | solution.py:169
  749.1 48.6 %all-reduce.5.cloned.1.call-done = bf16[128,512]{1,0:T(8,128)(2,1)} async-done(((bf16[128,512]{1,0:T(8,128)(2,1)}), bf16[128,512]{1,0:T(8,128)(2,1)}) %all-reduce.5.cloned.1.call-update) | async-done | bytes 131088 | tf_op jit(solution)/shard_map/while/body/eval_jaxpr/psum | solution.py:156
  808.7 48.8 %all-reduce.5.cloned.1.call-done = bf16[128,512]{1,0:T(8,128)(2,1)} async-done(((bf16[128,512]{1,0:T(8,128)(2,1)}), bf16[128,512]{1,0:T(8,128)(2,1)}) %all-reduce.5.cloned.1.call-update) | async-done | bytes 131088 | tf_op jit(solution)/shard_map/while/body/eval_jaxpr/psum | solution.py:156
  868.5 50.2 %all-reduce.5.cloned.1.call-done = bf16[128,512]{1,0:T(8,128)(2,1)} async-done(((bf16[128,512]{1,0:T(8,128)(2,1)}), bf16[128,512]{1,0:T(8,128)(2,1)}) %all-reduce.5.cloned.1.call-update) | async-done | bytes 131088 | tf_op jit(solution)/shard_map/while/body/eval_jaxpr/psum | solution.py:156
  929.7 50.2 %all-reduce.5.cloned.1.call-done = bf16[128,512]{1,0:T(8,128)(2,1)} async-done(((bf16[128,512]{1,0:T(8,128)(2,1)}), bf16[128,512]{1,0:T(8,128)(2,1)}) %all-reduce.5.cloned.1.call-update) | async-done | bytes 131088 | tf_op jit(solution)/shard_map/while/body/eval_jaxpr/psum | solution.py:156
  990.8 50.2 %all-reduce.5.cloned.1.call-done = bf16[128,512]{1,0:T(8,128)(2,1)} async-done(((bf16[128,512]{1,0:T(8,128)(2,1)}), bf16[128,512]{1,0:T(8,128)(2,1)}) %all-reduce.5.cloned.1.call-update) | async-done | bytes 131088 | tf_op jit(solution)/shard_map/while/body/eval_jaxpr/psum | solution.py:156
  1051.9 50.2 %all-reduce.5.cloned.1.call-done = bf16[128,512]{1,0:T(8,128)(2,1)} async-done(((bf16[128,512]{1,0:T(8,128)(2,1)}), bf16[128,512]{1,0:T(8,128)(2,1)}) %all-reduce.5.cloned.1.call-update) | async-done | bytes 131088 | tf_op jit(solution)/shard_map/while/body/eval_jaxpr/psum | solution.py:156
  1130.3 31.9 %all-reduce.5.cloned.1.call-done = bf16[128,512]{1,0:T(8,128)(2,1)} async-done(((bf16[128,512]{1,0:T(8,128)(2,1)}), bf16[128,512]{1,0:T(8,128)(2,1)}) %all-reduce.5.cloned.1.call-update) | async-done | bytes 131088 | tf_op jit(solution)/shard_map/while/body/eval_jaxpr/psum | solution.py:156
  1190.3 31.8 %all-reduce.5.cloned.1.call-done = bf16[128,512]{1,0:T(8,128)(2,1)} async-done(((bf16[128,512]{1,0:T(8,128)(2,1)}), bf16[128,512]{1,0:T(8,128)(2,1)}) %all-reduce.5.cloned.1.call-update) | async-done | bytes 131088 | tf_op jit(solution)/shard_map/while/body/eval_jaxpr/psum | solution.py:156
  1250.2 30.8 %all-reduce.5.cloned.1.call-done = bf16[128,512]{1,0:T(8,128)(2,1)} async-done(((bf16[128,512]{1,0:T(8,128)(2,1)}), bf16[128,512]{1,0:T(8,128)(2,1)}) %all-reduce.5.cloned.1.call-update) | async-done | bytes 131088 | tf_op jit(solution)/shard_map/while/body/eval_jaxpr/psum | solution.py:156
  1351.0 45.5 %all-reduce.5.cloned.1.call-done = bf16[128,512]{1,0:T(8,128)(2,1)} async-done(((bf16[128,512]{1,0:T(8,128)(2,1)}), bf16[128,512]{1,0:T(8,128)(2,1)}) %all-reduce.5.cloned.1.call-update) | async-done | bytes 131088 | tf_op jit(solution)/shard_map/while/body/eval_jaxpr/psum | solution.py:156
  1418.9 62.3 %reduce-scatter.5.cloned.1.call-done = bf16[32,4096]{1,0:T(8,128)(2,1)} async-done(((bf16[512,4096]{1,0:T(8,128)(2,1)}), bf16[32,4096]{1,0:T(8,128)(2,1)}) %reduce-scatter.5.cloned.1.call-update) | async-done | bytes 262160 | tf_op jit(solution)/shard_map/reduce_scatter | solution.py:178
  1483.0 78.0 %reduce-scatter.3.cloned.1.call-done = bf16[32,4096]{1,0:T(8,128)(2,1)} async-done(((bf16[512,4096]{1,0:T(8,128)(2,1)}), bf16[32,4096]{1,0:T(8,128)(2,1)}) %reduce-scatter.3.cloned.1.call-update) | async-done | bytes 262160 | tf_op jit(solution)/shard_map/reduce_scatter | solution.py:175
  (487 shorter events, 622.8 us)
Async XLA Ops:
  7.2 74.5 %all-gather.5.cloned.1.call-start = ((), (), s32[]{:S(2)}) async-start(), calls=%async_computation.4 | async-start | bytes 4456448 | tf_op jit(solution)/shard_map/all_gather | solution.py:81
  7.9 149.9 %all-gather.7.cloned.1.call-start = ((), (), s32[]{:S(2)}) async-start(), calls=%async_computation.5 | async-start | bytes 4456448 | tf_op jit(solution)/shard_map/all_gather | solution.py:82
  162.6 49.4 %all-reduce.3.cloned.1.call-start = ((), (), s32[]{:S(2)}) async-start(), calls=%async_computation.6 | async-start | bytes 262144 | tf_op jit(solution)/shard_map/while/body/eval_jaxpr/psum | solution.py:106
  269.5 43.0 %all-reduce.3.cloned.1.call-start = ((), (), s32[]{:S(2)}) async-start(), calls=%async_computation.6 | async-start | bytes 262144 | tf_op jit(solution)/shard_map/while/body/eval_jaxpr/psum | solution.py:106
  320.7 43.0 %all-reduce.3.cloned.1.call-start = ((), (), s32[]{:S(2)}) async-start(), calls=%async_computation.6 | async-start | bytes 262144 | tf_op jit(solution)/shard_map/while/body/eval_jaxpr/psum | solution.py:106
  372.0 44.5 %all-reduce.3.cloned.1.call-start = ((), (), s32[]{:S(2)}) async-start(), calls=%async_computation.6 | async-start | bytes 262144 | tf_op jit(solution)/shard_map/while/body/eval_jaxpr/psum | solution.py:106
  424.8 44.5 %all-reduce.3.cloned.1.call-start = ((), (), s32[]{:S(2)}) async-start(), calls=%async_computation.6 | async-start | bytes 262144 | tf_op jit(solution)/shard_map/while/body/eval_jaxpr/psum | solution.py:106
  476.3 45.8 %all-reduce.3.cloned.1.call-start = ((), (), s32[]{:S(2)}) async-start(), calls=%async_computation.6 | async-start | bytes 262144 | tf_op jit(solution)/shard_map/while/body/eval_jaxpr/psum | solution.py:106
  529.1 45.8 %all-reduce.3.cloned.1.call-start = ((), (), s32[]{:S(2)}) async-start(), calls=%async_computation.6 | async-start | bytes 262144 | tf_op jit(solution)/shard_map/while/body/eval_jaxpr/psum | solution.py:106
  581.9 45.5 %all-reduce.3.cloned.1.call-start = ((), (), s32[]{:S(2)}) async-start(), calls=%async_computation.6 | async-start | bytes 262144 | tf_op jit(solution)/shard_map/while/body/eval_jaxpr/psum | solution.py:106
  634.4 45.5 %all-reduce.3.cloned.1.call-start = ((), (), s32[]{:S(2)}) async-start(), calls=%async_computation.6 | async-start | bytes 262144 | tf_op jit(solution)/shard_map/while/body/eval_jaxpr/psum | solution.py:106
  747.1 50.7 %all-reduce.5.cloned.1.call-start = ((), (), s32[]{:S(2)}) async-start(), calls=%async_computation.7 | async-start | bytes 262144 | tf_op jit(solution)/shard_map/while/body/eval_jaxpr/psum | solution.py:156
  806.7 50.9 %all-reduce.5.cloned.1.call-start = ((), (), s32[]{:S(2)}) async-start(), calls=%async_computation.7 | async-start | bytes 262144 | tf_op jit(solution)/shard_map/while/body/eval_jaxpr/psum | solution.py:156
  866.5 52.2 %all-reduce.5.cloned.1.call-start = ((), (), s32[]{:S(2)}) async-start(), calls=%async_computation.7 | async-start | bytes 262144 | tf_op jit(solution)/shard_map/while/body/eval_jaxpr/psum | solution.py:156
  927.6 52.2 %all-reduce.5.cloned.1.call-start = ((), (), s32[]{:S(2)}) async-start(), calls=%async_computation.7 | async-start | bytes 262144 | tf_op jit(solution)/shard_map/while/body/eval_jaxpr/psum | solution.py:156
  988.7 52.2 %all-reduce.5.cloned.1.call-start = ((), (), s32[]{:S(2)}) async-start(), calls=%async_computation.7 | async-start | bytes 262144 | tf_op jit(solution)/shard_map/while/body/eval_jaxpr/psum | solution.py:156
  1049.9 52.2 %all-reduce.5.cloned.1.call-start = ((), (), s32[]{:S(2)}) async-start(), calls=%async_computation.7 | async-start | bytes 262144 | tf_op jit(solution)/shard_map/while/body/eval_jaxpr/psum | solution.py:156
  1111.0 51.2 %all-reduce.5.cloned.1.call-start = ((), (), s32[]{:S(2)}) async-start(), calls=%async_computation.7 | async-start | bytes 262144 | tf_op jit(solution)/shard_map/while/body/eval_jaxpr/psum | solution.py:156
  1171.1 51.0 %all-reduce.5.cloned.1.call-start = ((), (), s32[]{:S(2)}) async-start(), calls=%async_computation.7 | async-start | bytes 262144 | tf_op jit(solution)/shard_map/while/body/eval_jaxpr/psum | solution.py:156
  1231.0 50.1 %all-reduce.5.cloned.1.call-start = ((), (), s32[]{:S(2)}) async-start(), calls=%async_computation.7 | async-start | bytes 262144 | tf_op jit(solution)/shard_map/while/body/eval_jaxpr/psum | solution.py:156
  1289.9 50.1 %all-reduce.5.cloned.1.call-start = ((), (), s32[]{:S(2)}) async-start(), calls=%async_computation.7 | async-start | bytes 262144 | tf_op jit(solution)/shard_map/while/body/eval_jaxpr/psum | solution.py:156
  1348.9 47.5 %all-reduce.5.cloned.1.call-start = ((), (), s32[]{:S(2)}) async-start(), calls=%async_computation.7 | async-start | bytes 262144 | tf_op jit(solution)/shard_map/while/body/eval_jaxpr/psum | solution.py:156
  1405.3 75.9 %reduce-scatter.5.cloned.1.call-start = ((), (), s32[]{:S(2)}) async-start(), calls=%async_computation.3 | async-start | bytes 4456448 | tf_op jit(solution)/shard_map/reduce_scatter | solution.py:178
  1412.9 148.1 %reduce-scatter.3.cloned.1.call-start = ((), (), s32[]{:S(2)}) async-start(), calls=%async_computation.2 | async-start | bytes 4456448 | tf_op jit(solution)/shard_map/reduce_scatter | solution.py:175
  (75 other events, 384.0 us)
Sparse Core Ops, SparseCore 0:
  9.8 71.8 all-gather.4
  83.4 74.2 all-gather.6
  167.9 44.1 all-reduce.2
  280.9 31.5 all-reduce.2
  332.1 31.5 all-reduce.2
  383.4 33.0 all-reduce.2
  430.0 39.2 all-reduce.2
  481.6 40.4 all-reduce.2
  534.3 40.4 all-reduce.2
  587.1 40.2 all-reduce.2
  639.7 40.2 all-reduce.2
  692.2 37.4 all-reduce.2
  750.7 46.9 all-reduce.4
  810.3 47.1 all-reduce.4
  870.1 48.5 all-reduce.4
  931.2 48.5 all-reduce.4
  992.4 48.5 all-reduce.4
  1053.8 48.2 all-reduce.4
  1130.4 31.7 all-reduce.4
  1190.4 31.6 all-reduce.4
  1250.3 30.6 all-reduce.4
  1352.6 43.8 all-reduce.4
  1413.0 68.1 reduce-scatter.4
  1483.6 77.2 reduce-scatter.2
  (2 shorter events, 61.3 us)
where the time goes:
time: 1580 us; the launch traced here: 1570 us
  waiting for transfers between devices  1190 us (75%)
  local copies, waits for them, and re-layouts  109 us (7%)
  other arithmetic  81 us (5%)
  starting transfers between devices  78.7 us (5%)
  matrix products  78.4 us (5%)
  loops' own time  17.1 us (1%)
    psum x11, waiting for transfers between devices, backward_tick(): lax.psum(partial_value.astype(jnp.bfloat16), 'tensor').astype(jnp.float32)  469 us
    psum x11, waiting for transfers between devices, forward_tick(): lax.psum(partial_value.astype(jnp.bfloat16), 'tensor').astype(jnp.float32)  391 us
    ppermute x22, starting transfers between devices, shifted(): lax.ppermute(value, axis, [(source, source + steps) for source in range(i...  78.6 us
    reduce_scatter x1, waiting for transfers between devices, on_device(): lax.psum_scatter(dec_term.astype(jnp.bfloat16), 'dp', scatter_dimension=0...  78 us
    all_gather x1, waiting for transfers between devices, on_device(): lax.all_gather(enc_weight[0], 'dp', axis=0, tiled=True)  76.1 us
    all_gather x1, waiting for transfers between devices, on_device(): lax.all_gather(dec_weight[0], 'dp', axis=0, tiled=True)  70 us
    reduce_scatter x1, waiting for transfers between devices, on_device(): lax.psum_scatter(enc_term.astype(jnp.bfloat16), 'dp', scatter_dimension=0...  62.3 us
    dynamic_update_slice x44, other arithmetic, store_slot(): lax.dynamic_update_index_in_dim(store, jnp.where(is_active, update, previ...  45.3 us
  transfers between devices with their start and end apart: 48, of which 44 were waited for; matrix products, arithmetic and copies ran while one was open for 3% of the time, Pallas kernels for 0%

commit v1 on v0

v1 whole, which is shorter than its diff:
```python
import functools

import jax
import jax.numpy as jnp
from jax import lax
from jax.experimental import pallas as pl
from jax.experimental.pallas import tpu as pltpu
from jax.sharding import PartitionSpec as P

eps = 1e-05
loss_scale = 512.0
f32 = jnp.float32
bf16 = jnp.bfloat16

Z = 8
SUB = 32
WIDTH = 512
SPAN = 2048
COLS = 4096
XPART = 768
ZPART = SPAN - XPART
TILE = 1024
CHUNKS = 2
STAGES = 4


def core_swap(value):
    return lax.ppermute(value, "pipe", [(i, i ^ 1) for i in range(8)])


def y_shift(value, steps):
    return lax.ppermute(
        value, "pipe", [(i, i + 2 * steps) for i in range(8) if 0 <= i + 2 * steps < 8]
    )


def z_shift(value, steps):
    return lax.ppermute(
        value, "dp", [(x * Z + z, x * Z + (z + steps) % Z) for x in range(2) for z in range(Z)]
    )


def swap_a(value):
    return lax.ppermute(value, "dp", [(x * Z + z, (1 - x) * Z + z) for x in range(2) for z in range(Z)])


def swap_b(value):
    pairs = [
        ((x * Z + z) * 2 + t, ((1 - x) * Z + z) * 2 + 1 - t)
        for x in range(2)
        for z in range(Z)
        for t in range(2)
    ]
    return lax.ppermute(value, ("dp", "tensor"), pairs)


def gather_x(block):
    half = block.shape[0] // 2
    a = swap_a(block)
    b = swap_b(block)
    d = jnp.concatenate([swap_a(b[:half]), swap_b(a[half:])], axis=0)
    return {(0, 0): block, (0, 1): a, (1, 1): b, (1, 0): d}


def gather_z(block):
    half = block.shape[0] // 2
    out = {0: block}
    up, down = block, block
    for step in (1, 2, 3):
        up = z_shift(up, 1)
        down = z_shift(down, -1)
        out[Z - step] = up
        out[step] = down
    out[4] = (z_shift(up[:half], 1), z_shift(down[half:], -1))
    return out


def copy_kernel(moves, n_in, *refs):
    sources, target, sems = refs[:n_in], refs[n_in + 1], refs[n_in + 2]
    copies = []
    for k, (which, src, dst) in enumerate(moves):
        copy = pltpu.make_async_copy(sources[which].at[src], target.at[dst], sems.at[k])
        copy.start()
        copies.append(copy)
    for copy in copies:
        copy.wait()


def place(buffer, pieces, moves):
    n_in = len(pieces)
    return pl.pallas_call(
        functools.partial(copy_kernel, moves, n_in),
        out_shape=jax.ShapeDtypeStruct(buffer.shape, buffer.dtype),
        in_specs=[pl.BlockSpec(memory_space=pl.ANY)] * (n_in + 1),
        out_specs=pl.BlockSpec(memory_space=pl.ANY),
        scratch_shapes=[pltpu.SemaphoreType.DMA((len(moves),))],
        input_output_aliases={n_in: 0},
    )(*pieces, buffer)


def spot(xr, dz, tr, low, high):
    row = xr * Z * SUB + dz * SUB
    return (slice(None), slice(None), slice(row, row + SUB), slice(tr * SPAN + low, tr * SPAN + high))


def gather_weights(dec_weight, enc_weight, core):
    own = jnp.stack([dec_weight[0], enc_weight[0]])
    mine = lax.dynamic_slice_in_dim(own, core * SPAN, SPAN, 2)
    other = core_swap(lax.dynamic_slice_in_dim(own, (1 - core) * SPAN, SPAN, 2))
    first = core == 0
    block = jnp.stack([jnp.where(first, mine, other), jnp.where(first, other, mine)])
    part_x, part_z = block[..., :XPART], block[..., XPART:]

    part_x = gather_x(part_x)
    stacked = jnp.stack(
        [
            jnp.stack([part_x[0, 0], part_x[0, 1]]),
            jnp.stack([part_x[1, 0], part_x[1, 1]]),
        ]
    )
    rings = gather_z(stacked)
    flat = gather_z(part_z)
    flat[4] = jnp.concatenate([flat[4][0], flat[4][1]], axis=0)

    buffer = jnp.zeros((2, 2, WIDTH, COLS), bf16)
    groups = ((7, 0, 1, 2), (3, 4, 5, 6))
    pieces, moves = [], []
    for group in groups:
        wide = gather_x(jnp.stack([flat[dz] for dz in group]))
        for (tr, xr), piece in wide.items():
            for k, dz in enumerate(group):
                moves.append((len(pieces), (k,), spot(xr, dz, tr, XPART, SPAN)))
            pieces.append(piece)
    for dz in range(Z):
        for tr in range(2):
            for xr in range(2):
                if dz == 4:
                    moves.append((len(pieces) + tr, (0, xr), spot(xr, dz, tr, 0, XPART)))
                else:
                    moves.append((len(pieces), (tr, xr), spot(xr, dz, tr, 0, XPART)))
        if dz == 4:
            pieces += [rings[dz][0], rings[dz][1]]
        else:
            pieces.append(rings[dz])
    return place(buffer, pieces, moves)


def add(*terms):
    return functools.reduce(lambda a, b: a + b, [t.astype(f32) for t in terms])


def reduce_x(parts):
    far = parts[1, 0]
    half = far.shape[0] // 2
    from_a = swap_a(far[:half])
    from_b = swap_b(far[half:])
    to_b = jnp.concatenate(
        [add(parts[1, 1][:half], from_a).astype(bf16), parts[1, 1][half:]], axis=0
    )
    to_a = jnp.concatenate(
        [parts[0, 1][:half], add(parts[0, 1][half:], from_b).astype(bf16)], axis=0
    )
    return add(parts[0, 0], swap_a(to_a), swap_b(to_b))


def reduce_z(parts):
    far = parts[4]
    half = far.shape[0] // 2
    up = z_shift(far[:half], 1)
    down = z_shift(far[half:], -1)
    up = jnp.concatenate([add(parts[3][:half], up).astype(bf16), parts[3][half:]], axis=0)
    down = jnp.concatenate([parts[5][:half], add(parts[5][half:], down).astype(bf16)], axis=0)
    up = z_shift(up, 1)
    down = z_shift(down, -1)
    for step in (2, 1):
        up = z_shift(add(parts[step], up).astype(bf16), 1)
        down = z_shift(add(parts[Z - step], down).astype(bf16), -1)
    return add(parts[0], up, down)


def norm_of(codes):
    values = codes.astype(f32)
    scales = lax.rsqrt(jnp.mean(values * values, axis=-1, keepdims=True) + eps)
    return values, scales


def grad_through_norm(grad_out, codes, left, right):
    values, scales = norm_of(codes)
    summed = left.astype(f32) + right.astype(f32)
    inner = jnp.mean(summed * values, axis=-1, keepdims=True)
    return (
        grad_out.astype(f32) + scales * summed - values * (scales * scales * scales) * inner
    )


def dot_rows(left, right):
    return lax.dot_general(left, right, (((1,), (0,)), ((), ())), preferred_element_type=f32)


def dot_last(left, right):
    return lax.dot_general(left, right, (((1,), (1,)), ((), ())), preferred_element_type=f32)


def dot_first(left, right):
    return lax.dot_general(left, right, (((0,), (0,)), ((), ())), preferred_element_type=f32)


def forward_kernel(n_terms, keep, *refs):
    terms, (dec_ref, enc_ref) = refs[:n_terms], refs[n_terms : n_terms + 2]
    outs = refs[n_terms + 2 :]
    code_ref, part_ref = outs[:2]
    normed_ref, total_ref = outs[-2:]
    step = pl.program_id(0)

    @pl.when(step == 0)
    def _():
        codes = terms[1][...].astype(f32)
        if n_terms == 3:
            codes = codes + terms[2][...].astype(f32)
        codes = (terms[0][...].astype(f32) + codes).astype(bf16)
        code_ref[...] = codes
        values, scales = norm_of(codes)
        normed_ref[...] = (values * scales).astype(bf16)
        total_ref[...] = jnp.zeros_like(total_ref)

    half = 0.5 * dot_rows(normed_ref[...], dec_ref[0, 0])
    bend = jnp.tanh(half)
    gated = (half + half * bend).astype(bf16)
    if keep:
        gated_ref, slope_ref = outs[2:4]
        gated_ref[...] = gated
        slope_ref[...] = (0.5 * (1.0 + bend) * (1.0 + half * (1.0 - bend))).astype(bf16)
    total_ref[...] += dot_last(gated, enc_ref[0, 0])

    @pl.when(step == pl.num_programs(0) - 1)
    def _():
        part_ref[...] = total_ref[...].astype(bf16)


def weight_specs(section):
    return [
        pl.BlockSpec((1, 1, WIDTH, TILE), lambda i: (section, 0, 0, i)),
        pl.BlockSpec((1, 1, WIDTH, TILE), lambda i: (section, 1, 0, i)),
    ]


def section_cost(rows):
    return pl.CostEstimate(
        flops=4 * rows * WIDTH * COLS,
        bytes_accessed=4 * WIDTH * COLS + 8 * rows * WIDTH,
        transcendentals=rows * COLS,
    )


def section_forward(terms, weights, section, keep):
    rows = terms[0].shape[0]
    narrow = pl.BlockSpec((rows, WIDTH), lambda i: (0, 0))
    wide = pl.BlockSpec((rows, TILE), lambda i: (0, i))
    out_shape = [jax.ShapeDtypeStruct((rows, WIDTH), bf16)] * 2
    out_specs = [narrow, narrow]
    if keep:
        out_shape += [jax.ShapeDtypeStruct((rows, COLS), bf16)] * 2
        out_specs += [wide, wide]
    return pl.pallas_call(
        functools.partial(forward_kernel, len(terms), keep),
        grid=(COLS // TILE,),
        in_specs=[narrow] * len(terms) + weight_specs(section),
        out_specs=out_specs,
        out_shape=out_shape,
        scratch_shapes=[pltpu.VMEM((rows, WIDTH), bf16), pltpu.VMEM((rows, WIDTH), f32)],
        compiler_params=pltpu.CompilerParams(vmem_limit_bytes=24 * 1024 * 1024),
        cost_estimate=section_cost(rows),
    )(*terms, weights, weights)


def backward_kernel(n_terms, keep, *refs):
    terms, (slope_ref, dec_ref, enc_ref) = refs[:n_terms], refs[n_terms : n_terms + 3]
    outs = refs[n_terms + 3 :]
    grad_ref, part_ref = outs[:2]
    total_ref = outs[-1]
    step = pl.program_id(0)

    @pl.when(step == 0)
    def _():
        if n_terms == 2:
            grad = terms[0][...].astype(f32) + terms[1][...].astype(f32)
        else:
            grad = grad_through_norm(*[t[...] for t in terms])
        grad_ref[...] = grad.astype(bf16)
        total_ref[...] = jnp.zeros_like(total_ref)

    gated_grad = dot_rows(grad_ref[...], enc_ref[0, 0])
    hidden_grad = (gated_grad * slope_ref[...].astype(f32)).astype(bf16)
    if keep:
        outs[2][...] = hidden_grad
    total_ref[...] += dot_last(hidden_grad, dec_ref[0, 0])

    @pl.when(step == pl.num_programs(0) - 1)
    def _():
        part_ref[...] = total_ref[...].astype(bf16)


def section_backward(terms, slope, weights, section, keep):
    rows = terms[0].shape[0]
    narrow = pl.BlockSpec((rows, WIDTH), lambda i: (0, 0))
    wide = pl.BlockSpec((rows, TILE), lambda i: (0, i))
    out_shape = [jax.ShapeDtypeStruct((rows, WIDTH), bf16)] * 2
    out_specs = [narrow, narrow]
    if keep:
        out_shape += [jax.ShapeDtypeStruct((rows, COLS), bf16)]
        out_specs += [wide]
    return pl.pallas_call(
        functools.partial(backward_kernel, len(terms), keep),
        grid=(COLS // TILE,),
        in_specs=[narrow] * len(terms) + [wide] + weight_specs(section),
        out_specs=out_specs,
        out_shape=out_shape,
        scratch_shapes=[pltpu.VMEM((rows, WIDTH), f32)],
        compiler_params=pltpu.CompilerParams(vmem_limit_bytes=24 * 1024 * 1024),
        cost_estimate=section_cost(rows),
    )(*terms, slope, weights, weights)


def norm_grad_kernel(grad_ref, code_ref, left_ref, right_ref, out_ref):
    out_ref[...] = grad_through_norm(
        grad_ref[...], code_ref[...], left_ref[...], right_ref[...]
    ).astype(out_ref.dtype)


def norm_grad(grad, codes, left, right, dtype):
    return pl.pallas_call(
        norm_grad_kernel, out_shape=jax.ShapeDtypeStruct(grad.shape, dtype)
    )(grad, codes, left, right)


def seed_kernel(flag_ref, lengths_ref, code_ref, left_ref, right_ref, head_ref, out_ref):
    codes = (
        code_ref[...].astype(f32) + (left_ref[...].astype(f32) + right_ref[...].astype(f32))
    ).astype(bf16)
    head = head_ref[...].astype(f32)
    scores = jnp.sum(codes.astype(f32) * head, axis=-1, keepdims=True)
    rows = scores.shape[0]
    seq_len = rows // 2
    position = lax.broadcasted_iota(jnp.int32, (rows, 1), 0)
    chosen_length, other_length = lengths_ref[0], lengths_ref[1]
    chosen = jnp.where(position < seq_len, 1.0, 0.0)
    limit = jnp.where(position < seq_len, chosen_length, other_length + seq_len)
    valid = jnp.where(position < limit, 1.0, 0.0)
    chosen_count = jnp.full((1, 1), chosen_length, jnp.int32).astype(f32)
    other_count = jnp.full((1, 1), other_length, jnp.int32).astype(f32)
    chosen_sum = jnp.sum(scores * valid * chosen, axis=0, keepdims=True)
    other_sum = jnp.sum(scores * valid * (1.0 - chosen), axis=0, keepdims=True)
    gap = other_sum / other_count - chosen_sum / chosen_count
    weight = loss_scale * jax.nn.sigmoid(gap)
    token = (1.0 - chosen) * (weight / other_count) - chosen * (weight / chosen_count)
    token = token * valid * jnp.full((1, 1), flag_ref[0], jnp.int32).astype(f32)
    out_ref[...] = (token * head).astype(bf16)


def reward_seed(flag, lengths, codes, left, right, head):
    vmem = pl.BlockSpec(memory_space=pltpu.VMEM)
    smem = pl.BlockSpec(memory_space=pltpu.SMEM)
    return pl.pallas_call(
        seed_kernel,
        in_specs=[smem, smem, vmem, vmem, vmem, vmem],
        out_specs=vmem,
        out_shape=jax.ShapeDtypeStruct(codes.shape, bf16),
    )(flag, lengths, codes, left, right, head)


def weight_grad_kernel(*refs):
    grads, codes = refs[0:CHUNKS], refs[CHUNKS : 2 * CHUNKS]
    gated, hidden = refs[2 * CHUNKS : 3 * CHUNKS], refs[3 * CHUNKS : 4 * CHUNKS]
    x_ref, z_ref = refs[4 * CHUNKS :]

    def joined(group):
        return jnp.concatenate([ref[0] for ref in group], axis=0)

    values, scales = norm_of(joined(codes))
    normed = (values * scales).astype(bf16)
    for mat, (left, group) in enumerate(((normed, hidden), (joined(grads), gated))):
        for low, high, is_x in ((0, XPART, True), (XPART, SPAN, False)):
            right = jnp.concatenate([ref[0, :, low:high] for ref in group], axis=0)
            result = dot_first(left, right).astype(bf16)
            for xr in range(2):
                for dz in range(Z):
                    row = (xr * Z + dz) * SUB
                    piece = result[row : row + SUB]
                    if is_x:
                        x_ref[dz, 0, xr, 0, mat] = piece
                    else:
                        z_ref[0, xr, dz, 0, mat] = piece


def weight_grads(grads, codes, gated, hidden):
    rows = grads[0].shape[1]
    narrow = pl.BlockSpec((1, rows, WIDTH), lambda s, t: (s, 0, 0))
    wide = pl.BlockSpec((1, rows, SPAN), lambda s, t: (s, 0, t))
    return pl.pallas_call(
        weight_grad_kernel,
        grid=(2, 2),
        in_specs=[narrow] * (2 * CHUNKS) + [wide] * (2 * CHUNKS),
        out_specs=[
            pl.BlockSpec((Z, 1, 2, 1, 2, SUB, XPART), lambda s, t: (0, t, 0, s, 0, 0, 0)),
            pl.BlockSpec((1, 2, Z, 1, 2, SUB, ZPART), lambda s, t: (t, 0, 0, s, 0, 0, 0)),
        ],
        out_shape=[
            jax.ShapeDtypeStruct((Z, 2, 2, 2, 2, SUB, XPART), bf16),
            jax.ShapeDtypeStruct((2, 2, Z, 2, 2, SUB, ZPART), bf16),
        ],
        compiler_params=pltpu.CompilerParams(vmem_limit_bytes=40 * 1024 * 1024),
    )(*grads, *codes, *gated, *hidden)


def to_local(value, pair, z_index):
    lead = value.shape[:-1]
    value = value.reshape(lead + (2, Z, SUB))
    axis = len(lead)
    value = jnp.where(pair == 0, value, jnp.flip(value, axis))
    doubled = jnp.concatenate([value, value], axis=axis + 1)
    return lax.dynamic_slice_in_dim(doubled, z_index, Z, axis + 1).reshape(lead + (WIDTH,))


def to_global(value, pair, z_index):
    return to_local(value, pair, (Z - z_index) % Z)


def on_device(codes_in, lengths, dec_weight, enc_weight, head):
    pipe = lax.axis_index("pipe")
    core, stage = pipe % 2, pipe // 2
    tensor = lax.axis_index("tensor")
    dp = lax.axis_index("dp")
    pair, z_index = dp // Z, dp % Z

    weights = gather_weights(dec_weight, enc_weight, core)

    codes_in = lax.dynamic_slice_in_dim(codes_in, tensor * CHUNKS, CHUNKS, 0)
    lengths = lax.dynamic_slice_in_dim(lengths, tensor * CHUNKS, CHUNKS, 0)
    codes_in = to_local(codes_in, pair, z_index)
    codes_in = jnp.where(stage == 0, codes_in, jnp.zeros_like(codes_in))
    head = to_local(head[None], pair, z_index)
    is_last = (stage == STAGES - 1).astype(jnp.int32)[None]

    rows = codes_in.shape[1]
    blank = jnp.zeros((rows, WIDTH), bf16)
    chunks = range(CHUNKS)
    received = [blank] * CHUNKS
    codes = [[None, None] for _ in chunks]
    gated = [[None, None] for _ in chunks]
    slope = [[None, None] for _ in chunks]
    seeds = [None] * CHUNKS
    for step in range(STAGES):
        keep = step == STAGES - 1
        for m in chunks:
            first = section_forward([received[m], codes_in[m]], weights, 0, keep)
            second = section_forward([first[0], first[1], core_swap(first[1])], weights, 1, keep)
            across = core_swap(second[1])
            if keep:
                codes[m] = [first[0], second[0]]
                gated[m] = [first[2], second[2]]
                slope[m] = [first[3], second[3]]
                seeds[m] = reward_seed(is_last, lengths[m], second[0], second[1], across, head)
            else:
                received[m] = y_shift(add(second[0], add(second[1], across)).astype(bf16), 1)

    received = [blank] * CHUNKS
    grads = [[None, None] for _ in chunks]
    hidden = [[None, None] for _ in chunks]
    parts = [[None, None] for _ in chunks]
    for step in range(STAGES):
        keep = step == STAGES - 1
        for m in chunks:
            second = section_backward([received[m], seeds[m]], slope[m][1], weights, 1, keep)
            second_across = core_swap(second[1])
            first = section_backward(
                [second[0], codes[m][1], second[1], second_across], slope[m][0], weights, 0, keep
            )
            first_across = core_swap(first[1])
            if keep:
                grads[m] = [first[0], second[0]]
                hidden[m] = [first[2], second[2]]
                parts[m] = [(first[1], first_across), (second[1], second_across)]
            else:
                received[m] = y_shift(
                    norm_grad(first[0], codes[m][0], first[1], first_across, bf16), -1
                )

    by_x, by_z = weight_grads(
        [jnp.stack(grads[m]) for m in chunks],
        [jnp.stack(codes[m]) for m in chunks],
        [jnp.stack(gated[m]) for m in chunks],
        [jnp.stack(hidden[m]) for m in chunks],
    )
    summed_x = reduce_z([by_x[dz] for dz in range(Z)]).astype(bf16)
    summed_x = reduce_x({(tr, xr): summed_x[tr, xr] for tr in range(2) for xr in range(2)})
    summed_z = reduce_x({(tr, xr): by_z[tr, xr] for tr in range(2) for xr in range(2)})
    summed_z = reduce_z([summed_z[dz].astype(bf16) for dz in range(Z)])
    summed = jnp.concatenate([summed_x, summed_z], axis=-1)
    mine = lax.dynamic_index_in_dim(summed, core, 0, keepdims=False)
    other = core_swap(lax.dynamic_index_in_dim(summed, 1 - core, 0, keepdims=False))
    full = jnp.where(
        core == 0,
        jnp.concatenate([mine, other], axis=-1),
        jnp.concatenate([other, mine], axis=-1),
    )

    def pick(pairs):
        return jnp.where(core == 0, pairs[0], pairs[1])

    code_grads = []
    for m in chunks:
        code_grads.append(
            norm_grad(
                pick(grads[m]),
                pick(codes[m]),
                pick([parts[m][0][0], parts[m][1][0]]),
                pick([parts[m][0][1], parts[m][1][1]]),
                f32,
            )
        )
    code_grads = to_global(jnp.stack(code_grads), pair, z_index)
    share = rows // 2
    kept = lax.dynamic_slice_in_dim(code_grads, tensor * share, share, 1)
    sent = lax.dynamic_slice_in_dim(code_grads, (1 - tensor) * share, share, 1)
    got = lax.ppermute(sent, "tensor", [(0, 1), (1, 0)])
    code_out = jnp.where(
        tensor == 0, jnp.concatenate([kept, got], axis=0), jnp.concatenate([got, kept], axis=0)
    )
    return (code_out[None], full[0][None], full[1][None])


def solution(mesh):
    in_specs = (
        P(None, "dp", None),
        P(None, "dp"),
        P("pipe", "dp", "tensor"),
        P("pipe", "dp", "tensor"),
        P(),
    )
    out_specs = (
        P("pipe", None, ("dp", "tensor"), None),
        P("pipe", "dp", "tensor"),
        P("pipe", "dp", "tensor"),
    )
    return jax.shard_map(
        on_device, mesh=mesh, in_specs=in_specs, out_specs=out_specs, check_vma=False
    )
```

time: 1580 us -> 1120 us (0.71)
  waiting for transfers between devices: 1190 us -> 185 us
  Pallas kernels: 0 us -> 660 us
  matrix products: 78.4 us -> 0 us
  starting transfers between devices: 78.7 us -> 124 us
  other arithmetic: 81 us -> 38.9 us
  loops' own time: 17.1 us -> 0 us
    psum x22 -> x0, waiting for transfers between devices: 860 us -> none  [the longest x11 469 us: backward_tick(): lax.psum(partial_value.astype(jnp.bfloat16), 'tensor').astype(jnp.float32)]
    pallas_call x0 -> x44, Pallas kernels: none -> 660 us  [the longest x1 510 us: place(): pl.pallas_call(functools.partial(copy_kernel, moves, n_in), out_shape=jax...]
    all_gather x2 -> x0, waiting for transfers between devices: 146 us -> none  [the longest x1 76.1 us: on_device(): lax.all_gather(enc_weight[0], 'dp', axis=0, tiled=True)]
    ppermute x22 -> x99, waiting for transfers between devices: 43 us -> 185 us  [the longest x32 79.3 us: z_shift(): lax.ppermute(value, 'dp', [(x * Z + z, x * Z + (z + steps) % Z) for x in...]
    reduce_scatter x2 -> x0, waiting for transfers between devices: 140 us -> none  [the longest x1 78 us: on_device(): lax.psum_scatter(dec_term.astype(jnp.bfloat16), 'dp', scatter_dimension=0...]
    dot_general x25 -> x0, matrix products: 78.4 us -> none  [the longest x8 24.5 us: contract_first(): lax.dot_general(left, right, (((0,), (0,)), ((), ())), preferred_element_...]
    unnamed x4 -> x141, local copies, waits for them, and re-layouts: 1.45 us -> 74 us
    ppermute x22 -> x99, starting transfers between devices: 78.6 us -> 124 us  [the longest x32 48 us: z_shift(): lax.ppermute(value, 'dp', [(x * Z + z, x * Z + (z + steps) % Z) for x in...]
  transfers between devices with their start and end apart: 48 -> 99, of which waited for: 44 -> 28; matrix products, arithmetic and copies ran while one was open for 3% -> 5% of each run, Pallas kernels for 0% -> 12%
where the time goes in v1:
time: 1120 us; the launch traced here: 1110 us
  Pallas kernels  660 us (59%)
  waiting for transfers between devices  185 us (17%)
  starting transfers between devices  124 us (11%)
  local copies, waits for them, and re-layouts  99.8 us (9%)
  other arithmetic  38.9 us (3%)
    pallas_call x1, Pallas kernels, place(): pl.pallas_call(functools.partial(copy_kernel, moves, n_in), out_shape=jax...  510 us
    ppermute x32, waiting for transfers between devices, z_shift(): lax.ppermute(value, 'dp', [(x * Z + z, x * Z + (z + steps) % Z) for x in...  79.3 us
    unnamed x141, local copies, waits for them, and re-layouts  74 us
    pallas_call x16, Pallas kernels, section_forward(): pl.pallas_call(functools.partial(forward_kernel, len(terms), keep), grid=...  61.9 us
    pallas_call x16, Pallas kernels, section_backward(): pl.pallas_call(functools.partial(backward_kernel, len(terms), keep), grid...  60.5 us
    ppermute x10, waiting for transfers between devices, swap_b(): return lax.ppermute(value, ('dp', 'tensor'), pairs)  58.7 us
    ppermute x32, starting transfers between devices, z_shift(): lax.ppermute(value, 'dp', [(x * Z + z, x * Z + (z + steps) % Z) for x in...  48 us
    ppermute x34, starting transfers between devices, core_swap(): return lax.ppermute(value, 'pipe', [(i, i ^ 1) for i in range(8)])  32 us
  transfers between devices with their start and end apart: 99, of which 28 were waited for; matrix products, arithmetic and copies ran while one was open for 5% of the time, Pallas kernels for 12%

profile of v1, /device:TPU:1, one launch (start us, length us, event | category | flops | bytes accessed | tf_op | source)
XLA Modules:
  0.0 1110.3 jit_solution(15726063700875877200)
XLA Ops:
  26.4 20.9 %collective-permute-done.9 = bf16[2,2,32,1280]{3,2,1,0:T(8,128)(2,1)S(1)} collective-permute-done((bf16[2,2,32,1280]{3,2,1,0:T(8,128)(2,1)S(1)}, bf16[2,2,32,1280]{3,2,1,0:T(8,128)(2,1)S(1)}, u32[]{:S(2)}, u32[]{:S(2)}) %collective-permute-start.9) | collective-permute-done | bytes 327712 | tf_op jit(solution)/shard_map/ppermute | solution.py:38
  64.6 11.6 %collective-permute-done.25.refs_15_ = bf16[2,2,2,2,32,768]{5,4,3,2,1,0:T(8,128)(2,1)} collective-permute-done((bf16[2,2,2,2,32,768]{5,4,3,2,1,0:T(8,128)(2,1)S(1)}, bf16[2,2,2,2,32,768]{5,4,3,2,1,0:T(8,128)(2,1)}, u32[]{:S(2)}, u32[]{:S(2)}) %collective-permute-start.25) | collective-permute-done | bytes 786464 | tf_op jit(solution)/shard_map/ppermute | solution.py:38
  77.6 6.9 collective-permute-done.5.refs_2_
  92.1 20.6 %collective-permute-done.14.refs_6_ = bf16[4,2,2,32,1280]{4,3,2,1,0:T(8,128)(2,1)} collective-permute-done((bf16[4,2,2,32,1280]{4,3,2,1,0:T(8,128)(2,1)}, bf16[4,2,2,32,1280]{4,3,2,1,0:T(8,128)(2,1)}, u32[]{:S(2)}, u32[]{:S(2)}) %collective-permute-start.14) | collective-permute-done | bytes 1310752 | tf_op jit(solution)/shard_map/ppermute | solution.py:54
  130.1 10.6 collective-permute-done.15
  143.3 6.1 broadcast_in_dim.19.refs_17_
  149.4 509.9 %shard_map.76.refs_2_.refs_3_.refs_4_.refs_5_.refs_6_ = bf16[2,2,512,4096]{3,2,1,0:T(8,128)(2,1)} custom-call(bf16[4,2,2,32,1280]{4,3,2,1,0:T(8,128)(2,1)} %copy-done.55, bf16[4,2,2,32,1280]{4,3,2,1,0:T(8,128)(2,1)} %collective-permute-done.4.refs_1_, bf16[4,2,2,32,1280]{4,3,2,1,0:T(8,128)(2,1)} %copy-done.57, ...), custom_call_target="tpu_custom_call", output_to_operand_aliasing={{}: (17, {})} | custom-call | tf_op jit(solution)/shard_map/pallas_call | solution.py:91
  659.3 5.8 copy-done.2
  668.7 6.0 collective-permute-start.51
  674.9 5.8 copy-done.3
  711.8 5.8 copy-done.4
  770.9 5.8 copy-done.5
  787.7 5.8 copy-done.6
  800.5 5.8 copy-done.7
  832.7 5.8 copy-done.8
  866.2 5.8 copy-done.9
  903.7 5.8 copy-done.10
  929.0 8.8 shard_map.119
  946.4 25.4 %collective-permute-done.86 = bf16[4,2,2,32,1280]{4,3,2,1,0:T(8,128)(2,1)S(1)} collective-permute-done((bf16[4,2,2,32,1280]{4,3,2,1,0:T(8,128)(2,1)S(1)}, bf16[4,2,2,32,1280]{4,3,2,1,0:T(8,128)(2,1)S(1)}, u32[]{:S(2)}, u32[]{:S(2)}) %collective-permute-start.86) | collective-permute-done | bytes 1310752 | tf_op jit(solution)/shard_map/ppermute | solution.py:54
  989.2 11.6 %collective-permute-done.75 = bf16[2,2,2,2,32,768]{5,4,3,2,1,0:T(8,128)(2,1)} collective-permute-done((bf16[2,2,2,2,32,768]{5,4,3,2,1,0:T(8,128)(2,1)}, bf16[2,2,2,2,32,768]{5,4,3,2,1,0:T(8,128)(2,1)}, u32[]{:S(2)}, u32[]{:S(2)}) %collective-permute-start.75) | collective-permute-done | bytes 786464 | tf_op jit(solution)/shard_map/ppermute | solution.py:38
  1014.9 6.1 collective-permute-done.76
  1024.5 9.2 collective-permute-done.87
  1055.9 9.0 collective-permute-done.81
  1093.5 14.2 %collective-permute-done.73 = f32[2,64,512]{1,2,0:T(8,128)S(1)} collective-permute-done((f32[2,64,512]{1,2,0:T(8,128)S(1)}, f32[2,64,512]{1,2,0:T(8,128)S(1)}, u32[]{:S(2)}, u32[]{:S(2)}) %collective-permute-start.73) | collective-permute-done | bytes 262176 | tf_op jit(solution)/shard_map/ppermute | solution.py:525
  (452 shorter events, 379.1 us)
Async XLA Ops:
  20.8 36.6 %collective-permute-start.24 = (bf16[2,2,2,2,32,768]{5,4,3,2,1,0:T(8,128)(2,1)S(1)}, bf16[2,2,2,2,32,768]{5,4,3,2,1,0:T(8,128)(2,1)S(1)}, u32[]{:S(2)}, u32[]{:S(2)}) collective-permute-start(bf16[2,2,2,2,32,768]{5,4,3,2,1,0:T(8,128)(2,1)S(1)} %pad_maximum_fusion.10.refs_8_), channel_id=1, source_target_pairs={{0,2},{2,4},{4,6},{6,8},{8,10},{10,12},{12,14},{14,0},{16,18},{18,... | collective-permute-start | bytes 2359304 | tf_op jit(solution)/shard_map/ppermute | solution.py:38
  21.1 26.3 %collective-permute-start.9 = (bf16[2,2,32,1280]{3,2,1,0:T(8,128)(2,1)S(1)}, bf16[2,2,32,1280]{3,2,1,0:T(8,128)(2,1)S(1)}, u32[]{:S(2)}, u32[]{:S(2)}) collective-permute-start(bf16[2,2,32,1280]{3,2,1,0:T(8,128)(2,1)S(1)} %collective-permute-done.1), channel_id=1, source_target_pairs={{0,2},{2,4},{4,6},{6,8},{8,10},{10,12},{12,14},{14,0},{16,18},{18,... | collective-permute-start | bytes 983048 | tf_op jit(solution)/shard_map/ppermute | solution.py:38
  22.3 25.1 %collective-permute-start.3 = (bf16[2,2,32,1280]{3,2,1,0:T(8,128)(2,1)S(1)}, bf16[2,2,32,1280]{3,2,1,0:T(8,128)(2,1)S(1)}, u32[]{:S(2)}, u32[]{:S(2)}) collective-permute-start(bf16[2,2,32,1280]{3,2,1,0:T(8,128)(2,1)S(1)} %collective-permute-done.2), channel_id=1, source_target_pairs={{0,14},{2,0},{4,2},{6,4},{8,6},{10,8},{12,10},{14,12},{16,30},{18,... | collective-permute-start | bytes 983048 | tf_op jit(solution)/shard_map/ppermute | solution.py:38
  25.0 34.2 %collective-permute-start.21 = (bf16[2,2,2,2,32,768]{5,4,3,2,1,0:T(8,128)(2,1)S(1)}, bf16[2,2,2,2,32,768]{5,4,3,2,1,0:T(8,128)(2,1)S(1)}, u32[]{:S(2)}, u32[]{:S(2)}) collective-permute-start(bf16[2,2,2,2,32,768]{5,4,3,2,1,0:T(8,128)(2,1)S(1)} %pad_maximum_fusion.10.refs_8_), channel_id=1, source_target_pairs={{0,14},{2,0},{4,2},{6,4},{8,6},{10,8},{12,10},{14,12},{16,30},{18,... | collective-permute-start | bytes 2359304 | tf_op jit(solution)/shard_map/ppermute | solution.py:38
  57.5 27.0 %collective-permute-start.5 = (bf16[4,2,2,32,1280]{4,3,2,1,0:T(8,128)(2,1)S(1)}, bf16[4,2,2,32,1280]{4,3,2,1,0:T(8,128)(2,1)S(1)}, u32[]{:S(2)}, u32[]{:S(2)}) collective-permute-start(bf16[4,2,2,32,1280]{4,3,2,1,0:T(8,128)(2,1)S(1)} %pad_maximum_fusion.6.refs_0_), channel_id=1, source_target_pairs={{0,17},{1,16},{2,19},{3,18},{4,21},{5,20},{6,23},{7,22},{8,25},{9,... | collective-permute-start | bytes 3932168 | tf_op jit(solution)/shard_map/ppermute | solution.py:54
  59.2 30.7 %collective-permute-start.4 = (bf16[4,2,2,32,1280]{4,3,2,1,0:T(8,128)(2,1)S(1)}, bf16[4,2,2,32,1280]{4,3,2,1,0:T(8,128)(2,1)}, u32[]{:S(2)}, u32[]{:S(2)}) collective-permute-start(bf16[4,2,2,32,1280]{4,3,2,1,0:T(8,128)(2,1)S(1)} %pad_maximum_fusion.6.refs_0_), channel_id=1, source_target_pairs={{0,16},{2,18},{4,20},{6,22},{8,24},{10,26},{12,28},{14,30},{16,0},... | collective-permute-start | bytes 3932168 | tf_op jit(solution)/shard_map/ppermute | solution.py:44
  63.5 49.3 %collective-permute-start.14 = (bf16[4,2,2,32,1280]{4,3,2,1,0:T(8,128)(2,1)}, bf16[4,2,2,32,1280]{4,3,2,1,0:T(8,128)(2,1)}, u32[]{:S(2)}, u32[]{:S(2)}) collective-permute-start(bf16[4,2,2,32,1280]{4,3,2,1,0:T(8,128)(2,1)} %pad_maximum_fusion.8.refs_4_), channel_id=1, source_target_pairs={{0,17},{1,16},{2,19},{3,18},{4,21},{5,20},{6,23},{7,22},{8,25},{9,... | collective-permute-start | bytes 3932168 | tf_op jit(solution)/shard_map/ppermute | solution.py:54
  76.3 40.1 %collective-permute-start.13 = (bf16[4,2,2,32,1280]{4,3,2,1,0:T(8,128)(2,1)}, bf16[4,2,2,32,1280]{4,3,2,1,0:T(8,128)(2,1)}, u32[]{:S(2)}, u32[]{:S(2)}) collective-permute-start(bf16[4,2,2,32,1280]{4,3,2,1,0:T(8,128)(2,1)} %pad_maximum_fusion.8.refs_4_), channel_id=1, source_target_pairs={{0,16},{2,18},{4,20},{6,22},{8,24},{10,26},{12,28},{14,30},{16,0},... | collective-permute-start | bytes 3932168 | tf_op jit(solution)/shard_map/ppermute | solution.py:44
  77.6 40.7 %collective-permute-start.26 = (bf16[2,2,2,2,32,768]{5,4,3,2,1,0:T(8,128)(2,1)}, bf16[2,2,2,2,32,768]{5,4,3,2,1,0:T(8,128)(2,1)S(1)}, u32[]{:S(2)}, u32[]{:S(2)}) collective-permute-start(bf16[2,2,2,2,32,768]{5,4,3,2,1,0:T(8,128)(2,1)} %collective-permute-done.25.refs_15_), channel_id=1, source_target_pairs={{0,2},{2,4},{4,6},{6,8},{8,10},{10,12},{12,14},{14,0},{16,18},{18,... | collective-permute-start | bytes 2359304 | tf_op jit(solution)/shard_map/ppermute | solution.py:38
  85.6 34.4 %collective-permute-start.23 = (bf16[2,2,2,2,32,768]{5,4,3,2,1,0:T(8,128)(2,1)}, bf16[2,2,2,2,32,768]{5,4,3,2,1,0:T(8,128)(2,1)}, u32[]{:S(2)}, u32[]{:S(2)}) collective-permute-start(bf16[2,2,2,2,32,768]{5,4,3,2,1,0:T(8,128)(2,1)} %collective-permute-done.22.refs_10_), channel_id=1, source_target_pairs={{0,14},{2,0},{4,2},{6,4},{8,6},{10,8},{12,10},{14,12},{16,30},{18,... | collective-permute-start | bytes 2359304 | tf_op jit(solution)/shard_map/ppermute | solution.py:38
  90.0 36.6 %collective-permute-start.6 = (bf16[2,2,2,32,1280]{4,3,2,1,0:T(8,128)(2,1)}, bf16[2,2,2,32,1280]{4,3,2,1,0:T(8,128)(2,1)S(1)}, u32[]{:S(2)}, u32[]{:S(2)}) collective-permute-start(bf16[2,2,2,32,1280]{4,3,2,1,0:T(8,128)(2,1)} %slice.343), channel_id=1, source_target_pairs={{0,16},{2,18},{4,20},{6,22},{8,24},{10,26},{12,28},{14,30},{16,0},... | collective-permute-start | bytes 1966088 | tf_op jit(solution)/shard_map/ppermute | solution.py:44
  116.3 24.4 %collective-permute-start.15 = (bf16[2,2,2,32,1280]{4,3,2,1,0:T(8,128)(2,1)}, bf16[2,2,2,32,1280]{4,3,2,1,0:T(8,128)(2,1)}, u32[]{:S(2)}, u32[]{:S(2)}) collective-permute-start(bf16[2,2,2,32,1280]{4,3,2,1,0:T(8,128)(2,1)} %slice.347), channel_id=1, source_target_pairs={{0,16},{2,18},{4,20},{6,22},{8,24},{10,26},{12,28},{14,30},{16,0},... | collective-permute-start | bytes 1966088 | tf_op jit(solution)/shard_map/ppermute | solution.py:44
  118.3 22.4 %collective-permute-start.16 = (bf16[2,2,2,32,1280]{4,3,2,1,0:T(8,128)(2,1)}, bf16[2,2,2,32,1280]{4,3,2,1,0:T(8,128)(2,1)}, u32[]{:S(2)}, u32[]{:S(2)}) collective-permute-start(bf16[2,2,2,32,1280]{4,3,2,1,0:T(8,128)(2,1)} %slice.348), channel_id=1, source_target_pairs={{0,17},{1,16},{2,19},{3,18},{4,21},{5,20},{6,23},{7,22},{8,25},{9,... | collective-permute-start | bytes 1966088 | tf_op jit(solution)/shard_map/ppermute | solution.py:54
  120.0 23.2 %collective-permute-start.27 = (bf16[1,2,2,2,32,768]{5,4,3,2,1,0:T(8,128)(2,1)S(1)}, bf16[1,2,2,2,32,768]{5,4,3,2,1,0:T(8,128)(2,1)S(1)}, u32[]{:S(2)}, u32[]{:S(2)}) collective-permute-start(bf16[1,2,2,2,32,768]{5,4,3,2,1,0:T(8,128)(2,1)S(1)} %slice.351), channel_id=1, source_target_pairs={{0,2},{2,4},{4,6},{6,8},{8,10},{10,12},{12,14},{14,0},{16,18},{18,... | collective-permute-start | bytes 1179656 | tf_op jit(solution)/shard_map/ppermute | solution.py:38
  940.7 31.1 %collective-permute-start.86 = (bf16[4,2,2,32,1280]{4,3,2,1,0:T(8,128)(2,1)S(1)}, bf16[4,2,2,32,1280]{4,3,2,1,0:T(8,128)(2,1)S(1)}, u32[]{:S(2)}, u32[]{:S(2)}) collective-permute-start(bf16[4,2,2,32,1280]{4,3,2,1,0:T(8,128)(2,1)S(1)} %get-tuple-element.167), channel_id=1, source_target_pairs={{0,17},{1,16},{2,19},{3,18},{4,21},{5,20},{6,23},{7,22},{8,25},{9,... | collective-permute-start | bytes 3932168 | tf_op jit(solution)/shard_map/ppermute | solution.py:54
  942.1 29.8 %collective-permute-start.88 = (bf16[4,2,2,32,1280]{4,3,2,1,0:T(8,128)(2,1)S(1)}, bf16[4,2,2,32,1280]{4,3,2,1,0:T(8,128)(2,1)S(1)}, u32[]{:S(2)}, u32[]{:S(2)}) collective-permute-start(bf16[4,2,2,32,1280]{4,3,2,1,0:T(8,128)(2,1)S(1)} %get-tuple-element.166), channel_id=1, source_target_pairs={{0,16},{2,18},{4,20},{6,22},{8,24},{10,26},{12,28},{14,30},{16,0},... | collective-permute-start | bytes 3932168 | tf_op jit(solution)/shard_map/ppermute | solution.py:44
  943.5 36.2 %collective-permute-start.74 = (bf16[1,2,2,2,32,768]{5,4,3,2,1,0:T(8,128)(2,1)S(1)}, bf16[1,2,2,2,32,768]{5,4,3,2,1,0:T(8,128)(2,1)S(1)}, u32[]{:S(2)}, u32[]{:S(2)}) collective-permute-start(bf16[1,2,2,2,32,768]{5,4,3,2,1,0:T(8,128)(2,1)S(1)} %get-tuple-element.174), channel_id=1, source_target_pairs={{0,2},{2,4},{4,6},{6,8},{8,10},{10,12},{12,14},{14,0},{16,18},{18,... | collective-permute-start | bytes 1179656 | tf_op jit(solution)/shard_map/ppermute | solution.py:38
  945.0 34.7 %collective-permute-start.78 = (bf16[1,2,2,2,32,768]{5,4,3,2,1,0:T(8,128)(2,1)S(1)}, bf16[1,2,2,2,32,768]{5,4,3,2,1,0:T(8,128)(2,1)S(1)}, u32[]{:S(2)}, u32[]{:S(2)}) collective-permute-start(bf16[1,2,2,2,32,768]{5,4,3,2,1,0:T(8,128)(2,1)S(1)} %get-tuple-element.175), channel_id=1, source_target_pairs={{0,14},{2,0},{4,2},{6,4},{8,6},{10,8},{12,10},{14,12},{16,30},{18,... | collective-permute-start | bytes 1179656 | tf_op jit(solution)/shard_map/ppermute | solution.py:38
  976.3 57.4 %collective-permute-start.87 = (bf16[8,2,2,32,1280]{4,3,2,1,0:T(8,128)(2,1)}, bf16[8,2,2,32,1280]{4,3,2,1,0:T(8,128)(2,1)}, u32[]{:S(2)}, u32[]{:S(2)}) collective-permute-start(bf16[8,2,2,32,1280]{4,3,2,1,0:T(8,128)(2,1)} %pad_maximum_fusion), channel_id=1, source_target_pairs={{0,16},{2,18},{4,20},{6,22},{8,24},{10,26},{12,28},{14,30},{16,0},... | collective-permute-start | bytes 7864328 | tf_op jit(solution)/shard_map/ppermute | solution.py:44
  978.4 58.3 %collective-permute-start.89 = (bf16[8,2,2,32,1280]{4,3,2,1,0:T(8,128)(2,1)}, bf16[8,2,2,32,1280]{4,3,2,1,0:T(8,128)(2,1)}, u32[]{:S(2)}, u32[]{:S(2)}) collective-permute-start(bf16[8,2,2,32,1280]{4,3,2,1,0:T(8,128)(2,1)} %pad_maximum_fusion.1), channel_id=1, source_target_pairs={{0,17},{1,16},{2,19},{3,18},{4,21},{5,20},{6,23},{7,22},{8,25},{9,... | collective-permute-start | bytes 7864328 | tf_op jit(solution)/shard_map/ppermute | solution.py:54
  987.8 27.1 %collective-permute-start.79 = (bf16[2,2,2,2,32,768]{5,4,3,2,1,0:T(8,128)(2,1)}, bf16[2,2,2,2,32,768]{5,4,3,2,1,0:T(8,128)(2,1)S(1)}, u32[]{:S(2)}, u32[]{:S(2)}) collective-permute-start(bf16[2,2,2,2,32,768]{5,4,3,2,1,0:T(8,128)(2,1)} %pad_maximum_fusion.12), channel_id=1, source_target_pairs={{0,14},{2,0},{4,2},{6,4},{8,6},{10,8},{12,10},{14,12},{16,30},{18,... | collective-permute-start | bytes 2359304 | tf_op jit(solution)/shard_map/ppermute | solution.py:38
  1023.0 21.3 %collective-permute-start.80 = (bf16[2,2,2,2,32,768]{5,4,3,2,1,0:T(8,128)(2,1)S(1)}, bf16[2,2,2,2,32,768]{5,4,3,2,1,0:T(8,128)(2,1)S(1)}, u32[]{:S(2)}, u32[]{:S(2)}) collective-permute-start(bf16[2,2,2,2,32,768]{5,4,3,2,1,0:T(8,128)(2,1)S(1)} %get-tuple-element.171), channel_id=1, source_target_pairs={{0,14},{2,0},{4,2},{6,4},{8,6},{10,8},{12,10},{14,12},{16,30},{18,... | collective-permute-start | bytes 2359304 | tf_op jit(solution)/shard_map/ppermute | solution.py:38
  1023.3 32.6 %collective-permute-start.77 = (bf16[2,2,2,2,32,768]{5,4,3,2,1,0:T(8,128)(2,1)S(1)}, bf16[2,2,2,2,32,768]{5,4,3,2,1,0:T(8,128)(2,1)S(1)}, u32[]{:S(2)}, u32[]{:S(2)}) collective-permute-start(bf16[2,2,2,2,32,768]{5,4,3,2,1,0:T(8,128)(2,1)S(1)} %get-tuple-element.170), channel_id=1, source_target_pairs={{0,2},{2,4},{4,6},{6,8},{8,10},{10,12},{12,14},{14,0},{16,18},{18,... | collective-permute-start | bytes 2359304 | tf_op jit(solution)/shard_map/ppermute | solution.py:38
  1049.6 22.4 %collective-permute-start.95 = (bf16[2,2,32,1280]{3,2,1,0:T(8,128)(2,1)S(1)}, bf16[2,2,32,1280]{3,2,1,0:T(8,128)(2,1)S(1)}, u32[]{:S(2)}, u32[]{:S(2)}) collective-permute-start(bf16[2,2,32,1280]{3,2,1,0:T(8,128)(2,1)S(1)} %pad_maximum_fusion.15), channel_id=1, source_target_pairs={{0,14},{2,0},{4,2},{6,4},{8,6},{10,8},{12,10},{14,12},{16,30},{18,... | collective-permute-start | bytes 983048 | tf_op jit(solution)/shard_map/ppermute | solution.py:38
  (144 other events, 1104.0 us)

commit v2 on v1

v2 whole, which is shorter than its diff:
```python
import functools

import jax
import jax.numpy as jnp
from jax import lax
from jax.experimental import pallas as pl
from jax.experimental.pallas import tpu as pltpu
from jax.sharding import PartitionSpec as P

eps = 1e-05
loss_scale = 512.0
f32 = jnp.float32
bf16 = jnp.bfloat16

Z = 8
SUB = 32
WIDTH = 512
SPAN = 2048
COLS = 4096
XPART = 896
ZPART = SPAN - XPART
TILE = 1024
NEAR = (0, 1, 2, 6, 7)
FAR = (3, 4, 5)
MIB = 1024 * 1024
CHUNKS = 2
STAGES = 4


def core_swap(value):
    return lax.ppermute(value, "pipe", [(i, i ^ 1) for i in range(8)])


def y_shift(value, steps):
    return lax.ppermute(
        value, "pipe", [(i, i + 2 * steps) for i in range(8) if 0 <= i + 2 * steps < 8]
    )


def z_shift(value, steps):
    return lax.ppermute(
        value, "dp", [(x * Z + z, x * Z + (z + steps) % Z) for x in range(2) for z in range(Z)]
    )


def swap_a(value):
    return lax.ppermute(value, "dp", [(x * Z + z, (1 - x) * Z + z) for x in range(2) for z in range(Z)])


def swap_b(value):
    pairs = [
        ((x * Z + z) * 2 + t, ((1 - x) * Z + z) * 2 + 1 - t)
        for x in range(2)
        for z in range(Z)
        for t in range(2)
    ]
    return lax.ppermute(value, ("dp", "tensor"), pairs)


def fenced(*values):
    return lax.optimization_barrier(values)


def copy_kernel(moves, n_in, *refs):
    sources, targets, sems = refs[:n_in], refs[n_in : n_in + 2], refs[n_in + 2]
    copies = []
    for k, (which, src, section, dst) in enumerate(moves):
        copy = pltpu.make_async_copy(
            sources[which].at[src], targets[section].at[dst], sems.at[k]
        )
        copy.start()
        copies.append(copy)
    for copy in copies:
        copy.wait()


def place(pieces, moves):
    vmem = pl.BlockSpec(memory_space=pltpu.VMEM)
    return pl.pallas_call(
        functools.partial(copy_kernel, moves, len(pieces)),
        out_shape=[jax.ShapeDtypeStruct((2, WIDTH, COLS), bf16)] * 2,
        in_specs=[pl.BlockSpec(memory_space=pl.ANY)] * len(pieces),
        out_specs=[vmem, vmem],
        scratch_shapes=[pltpu.SemaphoreType.DMA((len(moves),))],
        compiler_params=pltpu.CompilerParams(vmem_limit_bytes=24 * MIB),
    )(*pieces)


def spot(xr, dz, tr, low, high):
    row = (xr * Z + dz) * SUB
    return (slice(None), slice(row, row + SUB), slice(tr * SPAN + low, tr * SPAN + high))


def gather_weights(dec_weight, enc_weight, core):
    own = jnp.stack([dec_weight[0], enc_weight[0]])
    mine = lax.dynamic_slice_in_dim(own, core * SPAN, SPAN, 2)
    other = core_swap(lax.dynamic_slice_in_dim(own, (1 - core) * SPAN, SPAN, 2))
    first = core == 0
    block = jnp.stack([jnp.where(first, mine, other), jnp.where(first, other, mine)])
    part_x, part_z = block[..., :XPART], block[..., XPART:]

    a, b, u1, d1 = fenced(
        swap_a(part_x), swap_b(part_x), z_shift(part_z, 1), z_shift(part_z, -1)
    )
    da, db, u2, d2 = fenced(swap_a(b[:1]), swap_b(a[1:]), z_shift(u1, 1), z_shift(d1, -1))
    ring = jnp.stack(
        [jnp.stack([part_x, a]), jnp.stack([jnp.concatenate([da, db], axis=0), b])]
    )
    near = jnp.stack([part_z, d1, d2, u2, u1])
    near_a, near_b, w1, v1, u3, d3 = fenced(
        swap_a(near),
        swap_b(near),
        z_shift(ring, 1),
        z_shift(ring, -1),
        z_shift(u2, 1),
        z_shift(d2, -1),
    )
    near_da, near_db, w2, v2, u4, d4 = fenced(
        swap_a(near_b[:, :1]),
        swap_b(near_a[:, 1:]),
        z_shift(w1, 1),
        z_shift(v1, -1),
        z_shift(u3[:1], 1),
        z_shift(d3[1:], -1),
    )
    far = jnp.stack([d3, jnp.concatenate([u4, d4], axis=0), u3])
    far_a, far_b, w3, v3 = fenced(
        swap_a(far), swap_b(far), z_shift(w2, 1), z_shift(v2, -1)
    )
    far_da, far_db, w4, v4 = (
        swap_a(far_b[:, :1]),
        swap_b(far_a[:, 1:]),
        z_shift(w3[:1], 1),
        z_shift(v3[1:], -1),
    )

    pieces, moves = [], []
    for group, own_part, to_a, to_b, half_a, half_b in (
        (NEAR, near, near_a, near_b, near_da, near_db),
        (FAR, far, far_a, far_b, far_da, far_db),
    ):
        for k, dz in enumerate(group):
            for section in range(2):
                for n, (tr, xr) in enumerate(((0, 0), (0, 1), (1, 1))):
                    moves.append(
                        (len(pieces) + n, (k, section), section, spot(xr, dz, tr, XPART, SPAN))
                    )
                moves.append(
                    (len(pieces) + 3 + section, (k, 0), section, spot(0, dz, 1, XPART, SPAN))
                )
        pieces += [own_part, to_a, to_b, half_a, half_b]
    rings = {0: ring, 1: v1, 2: v2, 3: v3, 5: w3, 6: w2, 7: w1}
    for dz in range(Z):
        for section in range(2):
            for tr in range(2):
                for xr in range(2):
                    which, index = (len(pieces) + tr, 0) if dz == 4 else (len(pieces), tr)
                    moves.append(
                        (which, (index, xr, section), section, spot(xr, dz, tr, 0, XPART))
                    )
        pieces += [w4, v4] if dz == 4 else [rings[dz]]
    return place(pieces, moves)


def add(*terms):
    return functools.reduce(lambda a, b: a + b, [t.astype(f32) for t in terms])


def add_low(whole, part, axis):
    low, high = jnp.split(whole, 2, axis)
    return jnp.concatenate([add(low, part).astype(bf16), high], axis=axis)


def add_high(whole, part, axis):
    low, high = jnp.split(whole, 2, axis)
    return jnp.concatenate([low, add(high, part).astype(bf16)], axis=axis)


def couple(results, others):
    return lax.optimization_barrier((tuple(results), tuple(others)))[0]


def reduce_weights(ring, near, far, extra):
    z_res = (z_shift(ring[4, :1], 1), z_shift(ring[4, 1:], -1))
    x_res = (swap_a(far[1, 0, :, :1]), swap_b(far[1, 0, :, 1:]))
    w, v = z_res
    z_send = (add_low(ring[3], w, 0), add_high(ring[5], v, 0))
    x_res = couple(x_res, z_send)
    x_send = (add_high(far[0, 1], x_res[1], 1), add_low(far[1, 1], x_res[0], 1))
    z_res = couple((z_shift(z_send[0], 1), z_shift(z_send[1], -1)), x_send)
    x_res = (swap_a(x_send[0]), swap_b(x_send[1]))
    z_send = (add(ring[2], z_res[0]).astype(bf16), add(ring[6], z_res[1]).astype(bf16))
    x_res = couple(x_res, z_send + tuple(extra))
    far_sum = add(far[0, 0], *x_res).astype(bf16)
    x_send = (near[1, 0, :, :1], near[1, 0, :, 1:])
    x_send = couple(x_send, (far_sum,))
    z_res = couple((z_shift(z_send[0], 1), z_shift(z_send[1], -1)), x_send)
    n_res = (z_shift(far_sum[1, :1], 1), z_shift(far_sum[1, 1:], -1))
    x_res = (swap_a(x_send[0]), swap_b(x_send[1]))
    z_send = (add(ring[1], z_res[0]).astype(bf16), add(ring[7], z_res[1]).astype(bf16))
    n_send = (add_low(far_sum[0], n_res[0], 0), add_high(far_sum[2], n_res[1], 0))
    x_res = couple(x_res, z_send + n_send)
    x_send = (add_high(near[0, 1], x_res[1], 1), add_low(near[1, 1], x_res[0], 1))
    z_res = couple((z_shift(z_send[0], 1), z_shift(z_send[1], -1)), x_send)
    n_res = couple((z_shift(n_send[0], 1), z_shift(n_send[1], -1)), x_send)
    x_res = (swap_a(x_send[0]), swap_b(x_send[1]))
    ring_sum = add(ring[0], *z_res).astype(bf16)
    x_res = couple(x_res, (ring_sum,))
    near_sum = add(near[0, 0], *x_res).astype(bf16)
    n_send = (add(near_sum[2], n_res[0]).astype(bf16), add(near_sum[3], n_res[1]).astype(bf16))
    n_res = (z_shift(n_send[0], 1), z_shift(n_send[1], -1))
    x_res = (swap_a(ring_sum[1, 0, :1]), swap_b(ring_sum[1, 0, 1:]))
    x_send = (add_high(ring_sum[0, 1], x_res[1], 0), add_low(ring_sum[1, 1], x_res[0], 0))
    n_res = couple(n_res, x_send)
    n_send = (add(near_sum[1], n_res[0]).astype(bf16), add(near_sum[4], n_res[1]).astype(bf16))
    x_res = (swap_a(x_send[0]), swap_b(x_send[1]))
    n_res = (z_shift(n_send[0], 1), z_shift(n_send[1], -1))
    return jnp.concatenate(
        [add(ring_sum[0, 0], *x_res), add(near_sum[0], *n_res)], axis=-1
    )


def norm_of(codes):
    values = codes.astype(f32)
    scales = lax.rsqrt(jnp.mean(values * values, axis=-1, keepdims=True) + eps)
    return values, scales


def grad_through_norm(grad_out, codes, left, right):
    values, scales = norm_of(codes)
    summed = left.astype(f32) + right.astype(f32)
    inner = jnp.mean(summed * values, axis=-1, keepdims=True)
    return (
        grad_out.astype(f32) + scales * summed - values * (scales * scales * scales) * inner
    )


def dot_rows(left, right):
    return lax.dot_general(left, right, (((1,), (0,)), ((), ())), preferred_element_type=f32)


def dot_last(left, right):
    return lax.dot_general(left, right, (((1,), (1,)), ((), ())), preferred_element_type=f32)


def dot_first(left, right):
    return lax.dot_general(left, right, (((0,), (0,)), ((), ())), preferred_element_type=f32)


def forward_kernel(n_terms, keep, *refs):
    terms, weight_ref, outs = refs[:n_terms], refs[n_terms], refs[n_terms + 1 :]
    code_ref, part_ref = outs[:2]
    codes = terms[1][...].astype(f32)
    if n_terms == 3:
        codes = codes + terms[2][...].astype(f32)
    codes = (terms[0][...].astype(f32) + codes).astype(bf16)
    code_ref[...] = codes
    values, scales = norm_of(codes)
    normed = (values * scales).astype(bf16)
    total = None
    for low in range(0, COLS, TILE):
        span = slice(low, low + TILE)
        half = 0.5 * dot_rows(normed, weight_ref[0, :, span])
        bend = jnp.tanh(half)
        gated = (half + half * bend).astype(bf16)
        if keep:
            outs[2][:, span] = gated
            outs[3][:, span] = (0.5 * (1.0 + bend) * (1.0 + half * (1.0 - bend))).astype(bf16)
        part = dot_last(gated, weight_ref[1, :, span])
        total = part if total is None else total + part
    part_ref[...] = total.astype(bf16)


def section_cost(rows):
    return pl.CostEstimate(
        flops=4 * rows * WIDTH * COLS,
        bytes_accessed=4 * WIDTH * COLS + 8 * rows * WIDTH,
        transcendentals=rows * COLS,
    )


def section_forward(terms, weights, keep):
    rows = terms[0].shape[0]
    out_shape = [jax.ShapeDtypeStruct((rows, WIDTH), bf16)] * 2
    if keep:
        out_shape += [jax.ShapeDtypeStruct((rows, COLS), bf16)] * 2
    return pl.pallas_call(
        functools.partial(forward_kernel, len(terms), keep),
        out_shape=out_shape,
        compiler_params=pltpu.CompilerParams(vmem_limit_bytes=24 * MIB),
        cost_estimate=section_cost(rows),
    )(*terms, weights)


def backward_kernel(n_terms, keep, *refs):
    terms, slope_ref, weight_ref = refs[:n_terms], refs[n_terms], refs[n_terms + 1]
    outs = refs[n_terms + 2 :]
    grad_ref, part_ref = outs[:2]
    if n_terms == 2:
        grad = terms[0][...].astype(f32) + terms[1][...].astype(f32)
    else:
        grad = grad_through_norm(*[t[...] for t in terms])
        if keep:
            outs[3][...] = grad
    grad = grad.astype(bf16)
    grad_ref[...] = grad
    total = None
    for low in range(0, COLS, TILE):
        span = slice(low, low + TILE)
        gated_grad = dot_rows(grad, weight_ref[1, :, span])
        hidden_grad = (gated_grad * slope_ref[:, span].astype(f32)).astype(bf16)
        if keep:
            outs[2][:, span] = hidden_grad
        part = dot_last(hidden_grad, weight_ref[0, :, span])
        total = part if total is None else total + part
    part_ref[...] = total.astype(bf16)


def section_backward(terms, slope, weights, keep):
    rows = terms[0].shape[0]
    out_shape = [jax.ShapeDtypeStruct((rows, WIDTH), bf16)] * 2
    if keep:
        out_shape += [jax.ShapeDtypeStruct((rows, COLS), bf16)]
        if len(terms) > 2:
            out_shape += [jax.ShapeDtypeStruct((rows, WIDTH), f32)]
    return pl.pallas_call(
        functools.partial(backward_kernel, len(terms), keep),
        out_shape=out_shape,
        compiler_params=pltpu.CompilerParams(vmem_limit_bytes=24 * MIB),
        cost_estimate=section_cost(rows),
    )(*terms, slope, weights)


def norm_grad_kernel(grad_ref, code_ref, left_ref, right_ref, out_ref):
    out_ref[...] = grad_through_norm(
        grad_ref[...], code_ref[...], left_ref[...], right_ref[...]
    ).astype(out_ref.dtype)


def norm_grad(grad, codes, left, right, dtype):
    return pl.pallas_call(
        norm_grad_kernel, out_shape=jax.ShapeDtypeStruct(grad.shape, dtype)
    )(grad, codes, left, right)


def seed_kernel(flag_ref, lengths_ref, code_ref, left_ref, right_ref, head_ref, out_ref):
    codes = (
        code_ref[...].astype(f32) + (left_ref[...].astype(f32) + right_ref[...].astype(f32))
    ).astype(bf16)
    head = head_ref[...].astype(f32)
    scores = jnp.sum(codes.astype(f32) * head, axis=-1, keepdims=True)
    rows = scores.shape[0]
    seq_len = rows // 2
    position = lax.broadcasted_iota(jnp.int32, (rows, 1), 0)
    chosen_length, other_length = lengths_ref[0], lengths_ref[1]
    chosen = jnp.where(position < seq_len, 1.0, 0.0)
    limit = jnp.where(position < seq_len, chosen_length, other_length + seq_len)
    valid = jnp.where(position < limit, 1.0, 0.0)
    chosen_count = jnp.full((1, 1), chosen_length, jnp.int32).astype(f32)
    other_count = jnp.full((1, 1), other_length, jnp.int32).astype(f32)
    chosen_sum = jnp.sum(scores * valid * chosen, axis=0, keepdims=True)
    other_sum = jnp.sum(scores * valid * (1.0 - chosen), axis=0, keepdims=True)
    gap = other_sum / other_count - chosen_sum / chosen_count
    weight = loss_scale * jax.nn.sigmoid(gap)
    token = (1.0 - chosen) * (weight / other_count) - chosen * (weight / chosen_count)
    token = token * valid * jnp.full((1, 1), flag_ref[0], jnp.int32).astype(f32)
    out_ref[...] = (token * head).astype(bf16)


def reward_seed(flag, lengths, codes, left, right, head):
    vmem = pl.BlockSpec(memory_space=pltpu.VMEM)
    smem = pl.BlockSpec(memory_space=pltpu.SMEM)
    return pl.pallas_call(
        seed_kernel,
        in_specs=[smem, smem, vmem, vmem, vmem, vmem],
        out_specs=vmem,
        out_shape=jax.ShapeDtypeStruct(codes.shape, bf16),
    )(flag, lengths, codes, left, right, head)


def weight_grad_kernel(*refs):
    grads, codes = refs[0:CHUNKS], refs[CHUNKS : 2 * CHUNKS]
    gated, hidden = refs[2 * CHUNKS : 3 * CHUNKS], refs[3 * CHUNKS : 4 * CHUNKS]
    ring_ref, near_ref, far_ref = refs[-3:]

    def joined(group):
        return jnp.concatenate([ref[...] for ref in group], axis=0)

    values, scales = norm_of(joined(codes))
    normed = (values * scales).astype(bf16)
    for mat, (left, group) in enumerate(((normed, hidden), (joined(grads), gated))):
        for low, high in ((0, XPART), (XPART, SPAN)):
            right = jnp.concatenate([ref[:, low:high] for ref in group], axis=0)
            result = dot_first(left, right).astype(bf16)
            for xr in range(2):
                for dz in range(Z):
                    row = (xr * Z + dz) * SUB
                    piece = result[row : row + SUB]
                    if low == 0:
                        ring_ref[dz, 0, xr, 0, mat] = piece
                    elif dz in NEAR:
                        near_ref[0, xr, NEAR.index(dz), 0, mat] = piece
                    else:
                        far_ref[0, xr, FAR.index(dz), 0, mat] = piece


def weight_grads(section, grads, codes, gated, hidden, held):
    rows = grads[0].shape[0]
    narrow = pl.BlockSpec((rows, WIDTH), lambda t: (0, 0))
    wide = pl.BlockSpec((rows, SPAN), lambda t: (0, t))
    n_in = 4 * CHUNKS

    def group_spec(count):
        return pl.BlockSpec(
            (1, 2, count, 1, 2, SUB, ZPART), lambda t: (t, 0, 0, section, 0, 0, 0)
        )

    return pl.pallas_call(
        weight_grad_kernel,
        grid=(2,),
        in_specs=[narrow] * (2 * CHUNKS)
        + [wide] * (2 * CHUNKS)
        + [pl.BlockSpec(memory_space=pl.ANY)] * len(held),
        out_specs=[
            pl.BlockSpec((Z, 1, 2, 1, 2, SUB, XPART), lambda t: (0, t, 0, section, 0, 0, 0)),
            group_spec(len(NEAR)),
            group_spec(len(FAR)),
        ],
        out_shape=[
            jax.ShapeDtypeStruct((Z, 2, 2, 2, 2, SUB, XPART), bf16),
            jax.ShapeDtypeStruct((2, 2, len(NEAR), 2, 2, SUB, ZPART), bf16),
            jax.ShapeDtypeStruct((2, 2, len(FAR), 2, 2, SUB, ZPART), bf16),
        ],
        input_output_aliases={n_in + k: k for k in range(len(held))},
        compiler_params=pltpu.CompilerParams(vmem_limit_bytes=40 * MIB),
        cost_estimate=pl.CostEstimate(
            flops=8 * rows * CHUNKS * WIDTH * COLS // 2,
            bytes_accessed=4 * WIDTH * COLS,
            transcendentals=0,
        ),
    )(*grads, *codes, *gated, *hidden, *held)


def to_local(value, pair, z_index):
    lead = value.shape[:-1]
    value = value.reshape(lead + (2, Z, SUB))
    axis = len(lead)
    value = jnp.where(pair == 0, value, jnp.flip(value, axis))
    doubled = jnp.concatenate([value, value], axis=axis + 1)
    return lax.dynamic_slice_in_dim(doubled, z_index, Z, axis + 1).reshape(lead + (WIDTH,))


def to_global(value, pair, z_index):
    return to_local(value, pair, (Z - z_index) % Z)


def on_device(codes_in, lengths, dec_weight, enc_weight, head):
    pipe = lax.axis_index("pipe")
    core, stage = pipe % 2, pipe // 2
    tensor = lax.axis_index("tensor")
    dp = lax.axis_index("dp")
    pair, z_index = dp // Z, dp % Z

    weights = gather_weights(dec_weight, enc_weight, core)

    codes_in = lax.dynamic_slice_in_dim(codes_in, tensor * CHUNKS, CHUNKS, 0)
    lengths = lax.dynamic_slice_in_dim(lengths, tensor * CHUNKS, CHUNKS, 0)
    codes_in = to_local(codes_in, pair, z_index)
    codes_in = jnp.where(stage == 0, codes_in, jnp.zeros_like(codes_in))
    head = to_local(head[None], pair, z_index)
    is_last = (stage == STAGES - 1).astype(jnp.int32)[None]

    rows = codes_in.shape[1]
    blank = jnp.zeros((rows, WIDTH), bf16)
    chunks = range(CHUNKS)
    received = [blank] * CHUNKS
    codes = [[None, None] for _ in chunks]
    gated = [[None, None] for _ in chunks]
    slope = [[None, None] for _ in chunks]
    seeds = [None] * CHUNKS
    for step in range(STAGES):
        keep = step == STAGES - 1
        for m in chunks:
            first = section_forward([received[m], codes_in[m]], weights[0], keep)
            second = section_forward([first[0], first[1], core_swap(first[1])], weights[1], keep)
            across = core_swap(second[1])
            if keep:
                codes[m] = [first[0], second[0]]
                gated[m] = [first[2], second[2]]
                slope[m] = [first[3], second[3]]
                seeds[m] = reward_seed(is_last, lengths[m], second[0], second[1], across, head)
            else:
                received[m] = y_shift(add(second[0], add(second[1], across)).astype(bf16), 1)

    received = [blank] * CHUNKS
    grads = [[None] * CHUNKS, [None] * CHUNKS]
    hidden = [[None] * CHUNKS, [None] * CHUNKS]
    through = [[None] * CHUNKS, [None] * CHUNKS]
    for step in range(STAGES):
        keep = step == STAGES - 1
        for m in chunks:
            second = section_backward([received[m], seeds[m]], slope[m][1], weights[1], keep)
            second_across = core_swap(second[1])
            first = section_backward(
                [second[0], codes[m][1], second[1], second_across], slope[m][0], weights[0], keep
            )
            first_across = core_swap(first[1])
            passed = norm_grad(
                first[0], codes[m][0], first[1], first_across, f32 if keep else bf16
            )
            if keep:
                grads[0][m], grads[1][m] = first[0], second[0]
                hidden[0][m], hidden[1][m] = first[2], second[2]
                through[0][m], through[1][m] = passed, first[3]
            else:
                received[m] = y_shift(passed, -1)

    held = ()
    for section in (1, 0):
        held = weight_grads(
            section,
            grads[section],
            [codes[m][section] for m in chunks],
            [gated[m][section] for m in chunks],
            hidden[section],
            held,
        )

    code_grads = jnp.where(core == 0, jnp.stack(through[0]), jnp.stack(through[1]))
    code_grads = to_global(code_grads, pair, z_index)
    share = rows // 2
    kept = lax.dynamic_slice_in_dim(code_grads, tensor * share, share, 1)
    sent = lax.dynamic_slice_in_dim(code_grads, (1 - tensor) * share, share, 1)
    got = lax.ppermute(sent.astype(bf16), "tensor", [(0, 1), (1, 0)])
    summed = reduce_weights(*held, (got,))
    got = got.astype(f32)
    code_out = jnp.where(
        tensor == 0, jnp.concatenate([kept, got], axis=0), jnp.concatenate([got, kept], axis=0)
    )

    mine = lax.dynamic_index_in_dim(summed, core, 0, keepdims=False)
    other = core_swap(lax.dynamic_index_in_dim(summed, 1 - core, 0, keepdims=False))
    full = jnp.where(
        core == 0,
        jnp.concatenate([mine, other], axis=-1),
        jnp.concatenate([other, mine], axis=-1),
    )
    return (code_out[None], full[0][None], full[1][None])


def solution(mesh):
    in_specs = (
        P(None, "dp", None),
        P(None, "dp"),
        P("pipe", "dp", "tensor"),
        P("pipe", "dp", "tensor"),
        P(),
    )
    out_specs = (
        P("pipe", None, ("dp", "tensor"), None),
        P("pipe", "dp", "tensor"),
        P("pipe", "dp", "tensor"),
    )
    return jax.shard_map(
        on_device, mesh=mesh, in_specs=in_specs, out_specs=out_specs, check_vma=False
    )
```

time: 1120 us -> 544 us (0.49)
  Pallas kernels: 660 us -> 116 us
  waiting for transfers between devices: 185 us -> 161 us
  other arithmetic: 38.9 us -> 15.5 us
  starting transfers between devices: 124 us -> 144 us
    pallas_call x34 -> x35, Pallas kernels: 641 us -> 96.8 us  [the longest x16 39.3 us: section_backward(): pl.pallas_call(functools.partial(backward_kernel, len(terms), keep), out_...]
    ppermute x10 -> x12, waiting for transfers between devices: 58.7 us -> 15.1 us  [swap_b(): return lax.ppermute(value, ('dp', 'tensor'), pairs)]
    ppermute x32, waiting for transfers between devices: 79.3 us -> 121 us  [z_shift(): lax.ppermute(value, 'dp', [(x * Z + z, x * Z + (z + steps) % Z) for x in...]
    ppermute x34, starting transfers between devices: 32 us -> 49.3 us  [core_swap(): return lax.ppermute(value, 'pipe', [(i, i ^ 1) for i in range(8)])]
    ppermute x10 -> x12, waiting for transfers between devices: 25.3 us -> 8.53 us  [swap_a(): lax.ppermute(value, 'dp', [(x * Z + z, (1 - x) * Z + z) for x in range(2)...]
    ppermute x32, starting transfers between devices: 48 us -> 35.9 us  [z_shift(): lax.ppermute(value, 'dp', [(x * Z + z, x * Z + (z + steps) % Z) for x in...]
    another operation x17 -> x7, other arithmetic: 12.2 us -> 0.4 us  [the longest x3 0.2 us: gather_weights(): jnp.stack([jnp.stack([part_x, a]), jnp.stack([jnp.concatenate([da, db], a...]
    unnamed x141 -> x228, local copies, waits for them, and re-layouts: 74 us -> 68 us
  transfers between devices with their start and end apart: 99 -> 103, of which waited for: 28 -> 32; matrix products, arithmetic and copies ran while one was open for 5% -> 6% of each run, Pallas kernels for 12% -> 20%
where the time goes in v2:
time: 544 us; the launch traced here: 534 us
  waiting for transfers between devices  161 us (30%)
  starting transfers between devices  144 us (26%)
  Pallas kernels  116 us (21%)
  local copies, waits for them, and re-layouts  94.4 us (17%)
  other arithmetic  15.5 us (3%)
    ppermute x32, waiting for transfers between devices, z_shift(): lax.ppermute(value, 'dp', [(x * Z + z, x * Z + (z + steps) % Z) for x in...  121 us
    unnamed x228, local copies, waits for them, and re-layouts  68 us
    ppermute x34, starting transfers between devices, core_swap(): return lax.ppermute(value, 'pipe', [(i, i ^ 1) for i in range(8)])  49.3 us
    pallas_call x16, Pallas kernels, section_backward(): pl.pallas_call(functools.partial(backward_kernel, len(terms), keep), out_...  39.3 us
    pallas_call x16, Pallas kernels, section_forward(): pl.pallas_call(functools.partial(forward_kernel, len(terms), keep), out_s...  39.1 us
    ppermute x32, starting transfers between devices, z_shift(): lax.ppermute(value, 'dp', [(x * Z + z, x * Z + (z + steps) % Z) for x in...  35.9 us
    ppermute x12, starting transfers between devices, y_shift(): lax.ppermute(value, 'pipe', [(i, i + 2 * steps) for i in range(8) if 0 <=...  28.3 us
    ppermute x12, starting transfers between devices, swap_b(): return lax.ppermute(value, ('dp', 'tensor'), pairs)  20.5 us
  transfers between devices with their start and end apart: 103, of which 32 were waited for; matrix products, arithmetic and copies ran while one was open for 6% of the time, Pallas kernels for 20%

profile of v2, /device:TPU:1, one launch (start us, length us, event | category | flops | bytes accessed | tf_op | source)
XLA Modules:
  0.0 533.8 jit_solution(9767534282429381190)
XLA Ops:
  7.5 3.9 collective-permute-start.4
  14.5 3.5 collective-permute-done.1
  35.5 20.4 %collective-permute-done.14 = bf16[2,2,32,1152]{3,2,1,0:T(8,128)(2,1)S(1)} collective-permute-done((bf16[2,2,32,1152]{3,2,1,0:T(8,128)(2,1)S(1)}, bf16[2,2,32,1152]{3,2,1,0:T(8,128)(2,1)S(1)}, u32[]{:S(2)}, u32[]{:S(2)}) %collective-permute-start.14) | collective-permute-done | bytes 294944 | tf_op jit(solution)/shard_map/ppermute | solution.py:41
  55.9 7.1 %collective-permute-done.13 = bf16[2,2,32,1152]{3,2,1,0:T(8,128)(2,1)S(1)} collective-permute-done((bf16[2,2,32,1152]{3,2,1,0:T(8,128)(2,1)S(1)}, bf16[2,2,32,1152]{3,2,1,0:T(8,128)(2,1)S(1)}, u32[]{:S(2)}, u32[]{:S(2)}) %collective-permute-start.13) | collective-permute-done | bytes 294944 | tf_op jit(solution)/shard_map/ppermute | solution.py:41
  71.8 9.8 %collective-permute-done.20 = bf16[1,2,32,1152]{3,2,1,0:T(8,128)(2,1)S(1)} collective-permute-done((bf16[1,2,32,1152]{3,2,1,0:T(8,128)(2,1)S(1)}, bf16[1,2,32,1152]{3,2,1,0:T(8,128)(2,1)S(1)}, u32[]{:S(2)}, u32[]{:S(2)}) %collective-permute-start.20) | collective-permute-done | bytes 147488 | tf_op jit(solution)/shard_map/ppermute | solution.py:41
  81.6 3.4 collective-permute-start.19
  85.0 4.4 collective-permute-done.19
  95.7 10.2 %collective-permute-done.22.refs_7_ = bf16[3,2,2,32,1152]{4,3,2,1,0:T(8,128)(2,1)} collective-permute-done((bf16[3,2,2,32,1152]{4,3,2,1,0:T(8,128)(2,1)S(1)}, bf16[3,2,2,32,1152]{4,3,2,1,0:T(8,128)(2,1)}, u32[]{:S(2)}, u32[]{:S(2)}) %collective-permute-start.22) | collective-permute-done | bytes 884768 | tf_op jit(solution)/shard_map/ppermute | solution.py:57
  133.8 8.7 %shard_map.76 = (bf16[2,512,4096]{2,1,0:T(8,128)(2,1)S(1)}, bf16[2,512,4096]{2,1,0:T(8,128)(2,1)}) custom-call(bf16[5,2,2,32,1152]{4,3,2,1,0:T(8,128)(2,1)S(1)} %copy-done.42, bf16[5,2,2,32,1152]{4,3,2,1,0:T(8,128)(2,1)S(1)} %copy-done.32, bf16[5,2,2,32,1152]{4,3,2,1,0:T(8,128)(2,1)S(1)} %copy-done.30, bf16[5,1,2,32,1152]{4,3,2,1,0:T(8,128)(2,1)S(1)} %copy-done.52, ...), custom_call_target="tpu_custom_call" | custom-call | tf_op jit(solution)/shard_map/pallas_call | solution.py:79
  145.7 22.9 %collective-permute-start.29 = (bf16[128,512]{1,0:T(8,128)(2,1)S(1)}, bf16[128,512]{1,0:T(8,128)(2,1)S(1)}, u32[]{:S(2)}, u32[]{:S(2)}) collective-permute-start(bf16[128,512]{1,0:T(8,128)(2,1)S(1)} %get-tuple-element.159.refs_1_), channel_id=1, source_target_pairs={{0,32},{32,0},{64,96},{96,64},{128,160},{160,128},{192,224},{224,1... | collective-permute-start | bytes 393224 | tf_op jit(solution)/shard_map/ppermute | solution.py:31
  199.4 4.1 collective-permute-start.34
  225.4 4.1 collective-permute-start.37
  353.1 4.0 shard_map.116
  357.3 4.9 shard_map.119
  362.2 3.8 shard_map.96
  370.2 4.8 shard_map.120
  376.5 3.9 slice_bitcast_fusion.7
  412.5 11.8 %collective-permute-done.75 = bf16[2,2,2,2,32,896]{5,4,3,2,1,0:T(8,128)(2,1)S(1)} collective-permute-done((bf16[2,2,2,2,32,896]{5,4,3,2,1,0:T(8,128)(2,1)S(1)}, bf16[2,2,2,2,32,896]{5,4,3,2,1,0:T(8,128)(2,1)S(1)}, u32[]{:S(2)}, u32[]{:S(2)}) %collective-permute-start.75) | collective-permute-done | bytes 917536 | tf_op jit(solution)/shard_map/ppermute | solution.py:41
  425.6 9.5 %collective-permute-done.73 = bf16[2,64,512]{1,2,0:T(8,128)(2,1)S(1)} collective-permute-done((bf16[2,64,512]{1,2,0:T(8,128)(2,1)S(1)}, bf16[2,64,512]{1,2,0:T(8,128)(2,1)S(1)}, u32[]{:S(2)}, u32[]{:S(2)}) %collective-permute-start.73) | collective-permute-done | bytes 131104 | tf_op jit(solution)/shard_map/ppermute | solution.py:534
  443.1 17.2 %collective-permute-done.81 = bf16[2,2,2,2,32,896]{5,4,3,2,1,0:T(8,128)(2,1)S(1)} collective-permute-done((bf16[2,2,2,2,32,896]{5,4,3,2,1,0:T(8,128)(2,1)S(1)}, bf16[2,2,2,2,32,896]{5,4,3,2,1,0:T(8,128)(2,1)S(1)}, u32[]{:S(2)}, u32[]{:S(2)}) %collective-permute-start.81) | collective-permute-done | bytes 917536 | tf_op jit(solution)/shard_map/ppermute | solution.py:41
  467.7 24.3 %collective-permute-done.96 = bf16[2,2,32,1152]{3,2,1,0:T(8,128)(2,1)S(1)} collective-permute-done((bf16[2,2,32,1152]{3,2,1,0:T(8,128)(2,1)S(1)}, bf16[2,2,32,1152]{3,2,1,0:T(8,128)(2,1)S(1)}, u32[]{:S(2)}, u32[]{:S(2)}) %collective-permute-start.96) | collective-permute-done | bytes 294944 | tf_op jit(solution)/shard_map/ppermute | solution.py:41
  492.1 5.9 %collective-permute-done.97 = bf16[2,2,32,1152]{3,2,1,0:T(8,128)(2,1)S(1)} collective-permute-done((bf16[2,2,32,1152]{3,2,1,0:T(8,128)(2,1)S(1)}, bf16[2,2,32,1152]{3,2,1,0:T(8,128)(2,1)S(1)}, u32[]{:S(2)}, u32[]{:S(2)}) %collective-permute-start.97) | collective-permute-done | bytes 294944 | tf_op jit(solution)/shard_map/ppermute | solution.py:41
  513.9 6.0 %collective-permute-done.100 = bf16[2,2,32,1152]{3,2,1,0:T(8,128)(2,1)} collective-permute-done((bf16[2,2,32,1152]{3,2,1,0:T(8,128)(2,1)S(1)}, bf16[2,2,32,1152]{3,2,1,0:T(8,128)(2,1)}, u32[]{:S(2)}, u32[]{:S(2)}) %collective-permute-start.100) | collective-permute-done | bytes 294944 | tf_op jit(solution)/shard_map/ppermute | solution.py:41
  522.0 8.4 %collective-permute-start.102 = (f32[2,32,2048]{2,1,0:T(8,128)}, f32[2,32,2048]{2,1,0:T(8,128)S(1)}, u32[]{:S(2)}, u32[]{:S(2)}) collective-permute-start(f32[2,32,2048]{2,1,0:T(8,128)} %get-tuple-element.295), channel_id=1, source_target_pairs={{0,32},{32,0},{64,96},{96,64},{128,160},{160,128},{192,224},{224,1... | collective-permute-start | bytes 1572872 | tf_op jit(solution)/shard_map/ppermute | solution.py:31
  (555 shorter events, 323.6 us)
Async XLA Ops:
  30.8 32.2 %collective-permute-start.10 = (bf16[5,2,2,32,1152]{4,3,2,1,0:T(8,128)(2,1)S(1)}, bf16[5,2,2,32,1152]{4,3,2,1,0:T(8,128)(2,1)S(1)}, u32[]{:S(2)}, u32[]{:S(2)}) collective-permute-start(bf16[5,2,2,32,1152]{4,3,2,1,0:T(8,128)(2,1)S(1)} %bitcast_dynamic-update-slice_fusion.refs_0_), channel_id=1, source_target_pairs={{0,17},{1,16},{2,19},{3,18},{4,21},{5,20},{6,23},{7,22},{8,25},{9,... | collective-permute-start | bytes 4423688 | tf_op jit(solution)/shard_map/ppermute | solution.py:57
  31.7 31.4 %collective-permute-start.9 = (bf16[5,2,2,32,1152]{4,3,2,1,0:T(8,128)(2,1)S(1)}, bf16[5,2,2,32,1152]{4,3,2,1,0:T(8,128)(2,1)S(1)}, u32[]{:S(2)}, u32[]{:S(2)}) collective-permute-start(bf16[5,2,2,32,1152]{4,3,2,1,0:T(8,128)(2,1)S(1)} %bitcast_dynamic-update-slice_fusion.refs_0_), channel_id=1, source_target_pairs={{0,16},{2,18},{4,20},{6,22},{8,24},{10,26},{12,28},{14,30},{16,0},... | collective-permute-start | bytes 4423688 | tf_op jit(solution)/shard_map/ppermute | solution.py:47
  32.2 30.8 %collective-permute-start.12 = (bf16[2,2,2,2,32,896]{5,4,3,2,1,0:T(8,128)(2,1)S(1)}, bf16[2,2,2,2,32,896]{5,4,3,2,1,0:T(8,128)(2,1)S(1)}, u32[]{:S(2)}, u32[]{:S(2)}) collective-permute-start(bf16[2,2,2,2,32,896]{5,4,3,2,1,0:T(8,128)(2,1)S(1)} %pad_maximum_fusion.2.refs_10_), channel_id=1, source_target_pairs={{0,14},{2,0},{4,2},{6,4},{8,6},{10,8},{12,10},{14,12},{16,30},{18,... | collective-permute-start | bytes 2752520 | tf_op jit(solution)/shard_map/ppermute | solution.py:41
  32.9 30.2 %collective-permute-start.11 = (bf16[2,2,2,2,32,896]{5,4,3,2,1,0:T(8,128)(2,1)S(1)}, bf16[2,2,2,2,32,896]{5,4,3,2,1,0:T(8,128)(2,1)S(1)}, u32[]{:S(2)}, u32[]{:S(2)}) collective-permute-start(bf16[2,2,2,2,32,896]{5,4,3,2,1,0:T(8,128)(2,1)S(1)} %pad_maximum_fusion.2.refs_10_), channel_id=1, source_target_pairs={{0,2},{2,4},{4,6},{6,8},{8,10},{10,12},{12,14},{14,0},{16,18},{18,... | collective-permute-start | bytes 2752520 | tf_op jit(solution)/shard_map/ppermute | solution.py:41
  33.8 22.1 %collective-permute-start.14 = (bf16[2,2,32,1152]{3,2,1,0:T(8,128)(2,1)S(1)}, bf16[2,2,32,1152]{3,2,1,0:T(8,128)(2,1)S(1)}, u32[]{:S(2)}, u32[]{:S(2)}) collective-permute-start(bf16[2,2,32,1152]{3,2,1,0:T(8,128)(2,1)S(1)} %collective-permute-done.8), channel_id=1, source_target_pairs={{0,14},{2,0},{4,2},{6,4},{8,6},{10,8},{12,10},{14,12},{16,30},{18,... | collective-permute-start | bytes 884744 | tf_op jit(solution)/shard_map/ppermute | solution.py:41
  63.1 26.4 %collective-permute-start.17 = (bf16[2,2,2,2,32,896]{5,4,3,2,1,0:T(8,128)(2,1)S(1)}, bf16[2,2,2,2,32,896]{5,4,3,2,1,0:T(8,128)(2,1)}, u32[]{:S(2)}, u32[]{:S(2)}) collective-permute-start(bf16[2,2,2,2,32,896]{5,4,3,2,1,0:T(8,128)(2,1)S(1)} %collective-permute-done.11.refs_18_), channel_id=1, source_target_pairs={{0,2},{2,4},{4,6},{6,8},{8,10},{10,12},{12,14},{14,0},{16,18},{18,... | collective-permute-start | bytes 2752520 | tf_op jit(solution)/shard_map/ppermute | solution.py:41
  64.3 25.2 %collective-permute-start.18 = (bf16[2,2,2,2,32,896]{5,4,3,2,1,0:T(8,128)(2,1)S(1)}, bf16[2,2,2,2,32,896]{5,4,3,2,1,0:T(8,128)(2,1)}, u32[]{:S(2)}, u32[]{:S(2)}) collective-permute-start(bf16[2,2,2,2,32,896]{5,4,3,2,1,0:T(8,128)(2,1)S(1)} %collective-permute-done.12.refs_11_), channel_id=1, source_target_pairs={{0,14},{2,0},{4,2},{6,4},{8,6},{10,8},{12,10},{14,12},{16,30},{18,... | collective-permute-start | bytes 2752520 | tf_op jit(solution)/shard_map/ppermute | solution.py:41
  145.7 28.9 %collective-permute-start.29 = (bf16[128,512]{1,0:T(8,128)(2,1)S(1)}, bf16[128,512]{1,0:T(8,128)(2,1)S(1)}, u32[]{:S(2)}, u32[]{:S(2)}) collective-permute-start(bf16[128,512]{1,0:T(8,128)(2,1)S(1)} %get-tuple-element.159.refs_1_), channel_id=1, source_target_pairs={{0,32},{32,0},{64,96},{96,64},{128,160},{160,128},{192,224},{224,1... | collective-permute-start | bytes 393224 | tf_op jit(solution)/shard_map/ppermute | solution.py:31
  366.0 26.7 %collective-permute-start.50 = (bf16[128,512]{1,0:T(8,128)(2,1)}, bf16[128,512]{1,0:T(8,128)(2,1)}, u32[]{:S(2)}, u32[]{:S(2)}) collective-permute-start(bf16[128,512]{1,0:T(8,128)(2,1)} %get-tuple-element.192.left_ref), channel_id=1, source_target_pairs={{0,32},{32,0},{64,96},{96,64},{128,160},{160,128},{192,224},{224,1... | collective-permute-start | bytes 393224 | tf_op jit(solution)/shard_map/ppermute | solution.py:31
  370.1 26.7 %collective-permute-start.72 = (bf16[128,512]{1,0:T(8,128)(2,1)S(1)}, bf16[128,512]{1,0:T(8,128)(2,1)}, u32[]{:S(2)}, u32[]{:S(2)}) collective-permute-start(bf16[128,512]{1,0:T(8,128)(2,1)S(1)} %get-tuple-element.226.left_ref), channel_id=1, source_target_pairs={{0,32},{32,0},{64,96},{96,64},{128,160},{160,128},{192,224},{224,1... | collective-permute-start | bytes 393224 | tf_op jit(solution)/shard_map/ppermute | solution.py:31
  402.4 21.9 %collective-permute-start.75 = (bf16[2,2,2,2,32,896]{5,4,3,2,1,0:T(8,128)(2,1)S(1)}, bf16[2,2,2,2,32,896]{5,4,3,2,1,0:T(8,128)(2,1)S(1)}, u32[]{:S(2)}, u32[]{:S(2)}) collective-permute-start(bf16[2,2,2,2,32,896]{5,4,3,2,1,0:T(8,128)(2,1)S(1)} %pad_maximum_fusion.3), channel_id=1, source_target_pairs={{0,2},{2,4},{4,6},{6,8},{8,10},{10,12},{12,14},{14,0},{16,18},{18,... | collective-permute-start | bytes 2752520 | tf_op jit(solution)/shard_map/ppermute | solution.py:41
  402.9 22.1 %collective-permute-start.77 = (bf16[2,2,2,2,32,896]{5,4,3,2,1,0:T(8,128)(2,1)S(1)}, bf16[2,2,2,2,32,896]{5,4,3,2,1,0:T(8,128)(2,1)S(1)}, u32[]{:S(2)}, u32[]{:S(2)}) collective-permute-start(bf16[2,2,2,2,32,896]{5,4,3,2,1,0:T(8,128)(2,1)S(1)} %pad_maximum_fusion.4), channel_id=1, source_target_pairs={{0,14},{2,0},{4,2},{6,4},{8,6},{10,8},{12,10},{14,12},{16,30},{18,... | collective-permute-start | bytes 2752520 | tf_op jit(solution)/shard_map/ppermute | solution.py:41
  407.8 27.3 %collective-permute-start.83 = (bf16[3,2,2,32,1152]{4,3,2,1,0:T(8,128)(2,1)S(1)}, bf16[3,2,2,32,1152]{4,3,2,1,0:T(8,128)(2,1)S(1)}, u32[]{:S(2)}, u32[]{:S(2)}) collective-permute-start(bf16[3,2,2,32,1152]{4,3,2,1,0:T(8,128)(2,1)S(1)} %pad_maximum_fusion.7), channel_id=1, source_target_pairs={{0,17},{1,16},{2,19},{3,18},{4,21},{5,20},{6,23},{7,22},{8,25},{9,... | collective-permute-start | bytes 2654216 | tf_op jit(solution)/shard_map/ppermute | solution.py:57
  408.5 26.6 %collective-permute-start.82 = (bf16[3,2,2,32,1152]{4,3,2,1,0:T(8,128)(2,1)S(1)}, bf16[3,2,2,32,1152]{4,3,2,1,0:T(8,128)(2,1)S(1)}, u32[]{:S(2)}, u32[]{:S(2)}) collective-permute-start(bf16[3,2,2,32,1152]{4,3,2,1,0:T(8,128)(2,1)S(1)} %pad_maximum_fusion.6), channel_id=1, source_target_pairs={{0,16},{2,18},{4,20},{6,22},{8,24},{10,26},{12,28},{14,30},{16,0},... | collective-permute-start | bytes 2654216 | tf_op jit(solution)/shard_map/ppermute | solution.py:47
  410.0 25.2 %collective-permute-start.73 = (bf16[2,64,512]{1,2,0:T(8,128)(2,1)S(1)}, bf16[2,64,512]{1,2,0:T(8,128)(2,1)S(1)}, u32[]{:S(2)}, u32[]{:S(2)}) collective-permute-start(bf16[2,64,512]{1,2,0:T(8,128)(2,1)S(1)} %dynamic-slice_convert_fusion), channel_id=1, source_target_pairs={{0,1},{1,0},{2,3},{3,2},{4,5},{5,4},{6,7},{7,6},{8,9},{9,8},{10,11... | collective-permute-start | bytes 393224 | tf_op jit(solution)/shard_map/ppermute | solution.py:534
  438.7 21.7 %collective-permute-start.81 = (bf16[2,2,2,2,32,896]{5,4,3,2,1,0:T(8,128)(2,1)S(1)}, bf16[2,2,2,2,32,896]{5,4,3,2,1,0:T(8,128)(2,1)S(1)}, u32[]{:S(2)}, u32[]{:S(2)}) collective-permute-start(bf16[2,2,2,2,32,896]{5,4,3,2,1,0:T(8,128)(2,1)S(1)} %get-tuple-element.272), channel_id=1, source_target_pairs={{0,14},{2,0},{4,2},{6,4},{8,6},{10,8},{12,10},{14,12},{16,30},{18,... | collective-permute-start | bytes 2752520 | tf_op jit(solution)/shard_map/ppermute | solution.py:41
  440.8 21.8 %collective-permute-start.80 = (bf16[2,2,2,2,32,896]{5,4,3,2,1,0:T(8,128)(2,1)S(1)}, bf16[2,2,2,2,32,896]{5,4,3,2,1,0:T(8,128)(2,1)S(1)}, u32[]{:S(2)}, u32[]{:S(2)}) collective-permute-start(bf16[2,2,2,2,32,896]{5,4,3,2,1,0:T(8,128)(2,1)S(1)} %get-tuple-element.273), channel_id=1, source_target_pairs={{0,2},{2,4},{4,6},{6,8},{8,10},{10,12},{12,14},{14,0},{16,18},{18,... | collective-permute-start | bytes 2752520 | tf_op jit(solution)/shard_map/ppermute | solution.py:41
  440.8 22.4 %collective-permute-start.86 = (bf16[5,1,2,32,1152]{4,3,2,1,0:T(8,128)(2,1)S(1)}, bf16[5,1,2,32,1152]{4,3,2,1,0:T(8,128)(2,1)S(1)}, u32[]{:S(2)}, u32[]{:S(2)}) collective-permute-start(bf16[5,1,2,32,1152]{4,3,2,1,0:T(8,128)(2,1)S(1)} %get-tuple-element.249), channel_id=1, source_target_pairs={{0,16},{2,18},{4,20},{6,22},{8,24},{10,26},{12,28},{14,30},{16,0},... | collective-permute-start | bytes 2211848 | tf_op jit(solution)/shard_map/ppermute | solution.py:47
  441.0 22.2 %collective-permute-start.87 = (bf16[5,1,2,32,1152]{4,3,2,1,0:T(8,128)(2,1)S(1)}, bf16[5,1,2,32,1152]{4,3,2,1,0:T(8,128)(2,1)S(1)}, u32[]{:S(2)}, u32[]{:S(2)}) collective-permute-start(bf16[5,1,2,32,1152]{4,3,2,1,0:T(8,128)(2,1)S(1)} %get-tuple-element.250), channel_id=1, source_target_pairs={{0,17},{1,16},{2,19},{3,18},{4,21},{5,20},{6,23},{7,22},{8,25},{9,... | collective-permute-start | bytes 2211848 | tf_op jit(solution)/shard_map/ppermute | solution.py:57
  463.8 36.9 %collective-permute-start.94 = (bf16[5,2,2,32,1152]{4,3,2,1,0:T(8,128)(2,1)S(1)}, bf16[5,2,2,32,1152]{4,3,2,1,0:T(8,128)(2,1)S(1)}, u32[]{:S(2)}, u32[]{:S(2)}) collective-permute-start(bf16[5,2,2,32,1152]{4,3,2,1,0:T(8,128)(2,1)S(1)} %pad_maximum_fusion), channel_id=1, source_target_pairs={{0,16},{2,18},{4,20},{6,22},{8,24},{10,26},{12,28},{14,30},{16,0},... | collective-permute-start | bytes 4423688 | tf_op jit(solution)/shard_map/ppermute | solution.py:47
  464.4 36.3 %collective-permute-start.95 = (bf16[5,2,2,32,1152]{4,3,2,1,0:T(8,128)(2,1)S(1)}, bf16[5,2,2,32,1152]{4,3,2,1,0:T(8,128)(2,1)S(1)}, u32[]{:S(2)}, u32[]{:S(2)}) collective-permute-start(bf16[5,2,2,32,1152]{4,3,2,1,0:T(8,128)(2,1)S(1)} %pad_maximum_fusion.1), channel_id=1, source_target_pairs={{0,17},{1,16},{2,19},{3,18},{4,21},{5,20},{6,23},{7,22},{8,25},{9,... | collective-permute-start | bytes 4423688 | tf_op jit(solution)/shard_map/ppermute | solution.py:57
  466.2 31.7 %collective-permute-start.85 = (bf16[2,2,2,2,32,896]{5,4,3,2,1,0:T(8,128)(2,1)S(1)}, bf16[2,2,2,2,32,896]{5,4,3,2,1,0:T(8,128)(2,1)S(1)}, u32[]{:S(2)}, u32[]{:S(2)}) collective-permute-start(bf16[2,2,2,2,32,896]{5,4,3,2,1,0:T(8,128)(2,1)S(1)} %get-tuple-element.270), channel_id=1, source_target_pairs={{0,14},{2,0},{4,2},{6,4},{8,6},{10,8},{12,10},{14,12},{16,30},{18,... | collective-permute-start | bytes 2752520 | tf_op jit(solution)/shard_map/ppermute | solution.py:41
  466.5 31.4 %collective-permute-start.84 = (bf16[2,2,2,2,32,896]{5,4,3,2,1,0:T(8,128)(2,1)S(1)}, bf16[2,2,2,2,32,896]{5,4,3,2,1,0:T(8,128)(2,1)S(1)}, u32[]{:S(2)}, u32[]{:S(2)}) collective-permute-start(bf16[2,2,2,2,32,896]{5,4,3,2,1,0:T(8,128)(2,1)S(1)} %get-tuple-element.271), channel_id=1, source_target_pairs={{0,2},{2,4},{4,6},{6,8},{8,10},{10,12},{12,14},{14,0},{16,18},{18,... | collective-permute-start | bytes 2752520 | tf_op jit(solution)/shard_map/ppermute | solution.py:41
  467.7 24.4 %collective-permute-start.96 = (bf16[2,2,32,1152]{3,2,1,0:T(8,128)(2,1)S(1)}, bf16[2,2,32,1152]{3,2,1,0:T(8,128)(2,1)S(1)}, u32[]{:S(2)}, u32[]{:S(2)}) collective-permute-start(bf16[2,2,32,1152]{3,2,1,0:T(8,128)(2,1)S(1)} %pad_maximum_fusion.8), channel_id=1, source_target_pairs={{0,2},{2,4},{4,6},{6,8},{8,10},{10,12},{12,14},{14,0},{16,18},{18,... | collective-permute-start | bytes 884744 | tf_op jit(solution)/shard_map/ppermute | solution.py:41
  (190 other events, 1228.4 us)

commit v3 on v2

v3 whole, which is shorter than its diff:
```python
import functools

import jax
import jax.numpy as jnp
from jax import lax
from jax.experimental import pallas as pl
from jax.experimental.pallas import tpu as pltpu
from jax.sharding import PartitionSpec as P

eps = 1e-05
loss_scale = 512.0
f32 = jnp.float32
bf16 = jnp.bfloat16

Z = 8
SUB = 32
WIDTH = 512
SPAN = 2048
COLS = 4096
XPART = 896
ZPART = SPAN - XPART
TILE = 1024
NEAR = (0, 1, 2, 6, 7)
FAR = (3, 4, 5)
CLOSE = (0, 1, 7)
DISTANT = (2, 3, 4, 5, 6)
MIB = 1024 * 1024
CHUNKS = 2
STAGES = 4


def core_swap(value):
    return lax.ppermute(value, "pipe", [(i, i ^ 1) for i in range(8)])


def y_shift(value, steps):
    return lax.ppermute(
        value, "pipe", [(i, i + 2 * steps) for i in range(8) if 0 <= i + 2 * steps < 8]
    )


def z_shift(value, steps):
    return lax.ppermute(
        value, "dp", [(x * Z + z, x * Z + (z + steps) % Z) for x in range(2) for z in range(Z)]
    )


def swap_a(value):
    return lax.ppermute(value, "dp", [(x * Z + z, (1 - x) * Z + z) for x in range(2) for z in range(Z)])


def swap_b(value):
    pairs = [
        ((x * Z + z) * 2 + t, ((1 - x) * Z + z) * 2 + 1 - t)
        for x in range(2)
        for z in range(Z)
        for t in range(2)
    ]
    return lax.ppermute(value, ("dp", "tensor"), pairs)


def fenced(*values):
    return lax.optimization_barrier(values)


def copy_kernel(moves, n_in, *refs):
    sources, targets, sems = refs[:n_in], refs[-5:-1], refs[-1]
    copies = []
    for k, (which, src, target, dst) in enumerate(moves):
        copy = pltpu.make_async_copy(
            sources[which].at[src], targets[target].at[dst], sems.at[k]
        )
        copy.start()
        copies.append(copy)
    for copy in copies:
        copy.wait()


def place(pieces, moves, held):
    vmem = pl.BlockSpec(memory_space=pltpu.VMEM)
    n_in = len(pieces)
    return pl.pallas_call(
        functools.partial(copy_kernel, moves, n_in),
        out_shape=[jax.ShapeDtypeStruct((WIDTH, COLS), bf16)] * 4,
        in_specs=[pl.BlockSpec(memory_space=pl.ANY)] * n_in + [vmem] * len(held),
        out_specs=[vmem] * 4,
        scratch_shapes=[pltpu.SemaphoreType.DMA((len(moves),))],
        input_output_aliases={n_in + k: k for k in range(len(held))},
        compiler_params=pltpu.CompilerParams(vmem_limit_bytes=24 * MIB),
        cost_estimate=pl.CostEstimate(
            flops=0, bytes_accessed=8 * WIDTH * COLS, transcendentals=0
        ),
    )(*pieces, *held)


def spot(xr, dz, tr, low, high):
    row = (xr * Z + dz) * SUB
    return (slice(row, row + SUB), slice(tr * SPAN + low, tr * SPAN + high))


def narrow_moves(group, blocks, pieces, moves):
    for section in range(2):
        for (tr, xr), block in zip(((0, 0), (0, 1), (1, 1), (1, 0)), blocks[section]):
            for k, dz in enumerate(group):
                for mat in range(2):
                    moves.append(
                        (len(pieces), (k, mat), 2 * section + mat, spot(xr, dz, tr, XPART, SPAN))
                    )
            pieces.append(block)


def ring_moves(dz, halves, pieces, moves):
    for section in range(2):
        for mat in range(2):
            for tr in range(2):
                for xr in range(2):
                    which, index = (tr, 0) if len(halves) == 2 else (0, tr)
                    moves.append(
                        (
                            len(pieces) + which,
                            (index, xr, section, mat),
                            2 * section + mat,
                            spot(xr, dz, tr, 0, XPART),
                        )
                    )
    pieces.extend(halves)


def gather_weights(dec_weight, enc_weight, core):
    own = jnp.stack([dec_weight[0], enc_weight[0]])
    mine = lax.dynamic_slice_in_dim(own, core * SPAN, SPAN, 2)
    other = core_swap(lax.dynamic_slice_in_dim(own, (1 - core) * SPAN, SPAN, 2))
    first = core == 0
    block = jnp.stack([jnp.where(first, mine, other), jnp.where(first, other, mine)])
    part_x, part_z = block[..., :XPART], block[..., XPART:]

    a, b, u1, d1 = fenced(
        swap_a(part_x), swap_b(part_x), z_shift(part_z, 1), z_shift(part_z, -1)
    )
    da, db, u2, d2 = fenced(swap_a(b[:1]), swap_b(a[1:]), z_shift(u1, 1), z_shift(d1, -1))
    ring = jnp.stack(
        [jnp.stack([part_x, a]), jnp.stack([jnp.concatenate([da, db], axis=0), b])]
    )
    near = [jnp.stack([t[s] for t in (part_z, d1, d2, u2, u1)]) for s in range(2)]
    w1, v1, near_a1, near_b0, u3, d3, near_a0, near_b1 = fenced(
        z_shift(ring, 1),
        z_shift(ring, -1),
        swap_a(near[1]),
        swap_b(near[0]),
        z_shift(u2, 1),
        z_shift(d2, -1),
        swap_a(near[0]),
        swap_b(near[1]),
    )
    w2, v2, near_d0, near_d1, u4, d4 = fenced(
        z_shift(w1, 1),
        z_shift(v1, -1),
        swap_a(near_b0),
        swap_b(near_a1),
        z_shift(u3[:1], 1),
        z_shift(d3[1:], -1),
    )
    far = [jnp.stack([d3[0], u4[0], u3[0]]), jnp.stack([d3[1], d4[0], u3[1]])]
    w3, v3, far_a1, far_b0, far_a0, far_b1 = fenced(
        z_shift(w2, 1),
        z_shift(v2, -1),
        swap_a(far[1]),
        swap_b(far[0]),
        swap_a(far[0]),
        swap_b(far[1]),
    )
    w4, v4 = z_shift(w3[:1], 1), z_shift(v3[1:], -1)
    far_d0, far_d1 = swap_a(far_b0), swap_b(far_a1)

    pieces, moves = [], []
    narrow_moves(
        NEAR,
        ((near[0], near_a0, near_b0, near_d0), (near[1], near_a1, near_b1, near_d1)),
        pieces,
        moves,
    )
    for dz, piece in ((0, ring), (1, v1), (7, w1), (2, v2), (6, w2)):
        ring_moves(dz, [piece], pieces, moves)
    held = place(pieces, moves, ())
    pieces, moves = [], []
    narrow_moves(
        FAR,
        ((far[0], far_a0, far_b0, far_d0), (far[1], far_a1, far_b1, far_d1)),
        pieces,
        moves,
    )
    ring_moves(3, [v3], pieces, moves)
    ring_moves(5, [w3], pieces, moves)
    ring_moves(4, [w4, v4], pieces, moves)
    dec_0, enc_0, dec_1, enc_1 = place(pieces, moves, held)
    return ((dec_0, enc_0), (dec_1, enc_1))


def add(*terms):
    return functools.reduce(lambda a, b: a + b, [t.astype(f32) for t in terms])


def add16(*terms):
    return add(*terms).astype(bf16)


def couple(results, others):
    return lax.optimization_barrier((tuple(results), tuple(others)))[0]


CHAINS = {(0, 1): (4, 3, 2, 1), (0, -1): (5, 6, 7), (1, 1): (3, 2, 1), (1, -1): (4, 5, 6, 7)}


def first_swap(section, value):
    return swap_a(value) if section == 0 else swap_b(value)


def second_swap(section, value):
    return swap_b(value) if section == 0 else swap_a(value)


class ZChain:
    def __init__(self, piece):
        self.piece = piece
        self.step = 0
        self.done = {}
        self.send = {key: piece(key[0], dzs[0]) for key, dzs in CHAINS.items()}

    def shift(self):
        self.result = {key: z_shift(value, key[1]) for key, value in self.send.items()}

    def merge(self):
        self.step += 1
        self.send = {}
        for key, value in self.result.items():
            if self.step < len(CHAINS[key]):
                self.send[key] = add16(self.piece(key[0], CHAINS[key][self.step]), value)
            else:
                self.done[key] = value
        return tuple(self.send.values())


def reduce_weights(parts, code_exchange):
    sections = (0, 1)
    ring = [part[:Z] for part in parts]
    far = [part[Z : Z + 3] for part in parts]
    near = [part[Z + 3 :] for part in parts]

    wide = ZChain(lambda s, dz: ring[s][dz])
    wide.shift()
    far_1 = [first_swap(s, far[s][0]) for s in sections]
    made = wide.merge()
    far_1 = couple(far_1, made)
    far_send = [add16(far[s][1], far_1[s][0]) for s in sections]

    wide.shift()
    far_2 = [second_swap(s, far_send[s]) for s in sections]
    near_1 = [first_swap(s, near[s][0]) for s in sections]
    made = wide.merge()
    far_2 = couple(far_2, made)
    near_2 = None
    near_sums = {}

    def narrow_piece(s, dz):
        if dz in DISTANT:
            k = DISTANT.index(dz)
            return add16(far[s][2][k], far_1[s][1, k], far_2[s][k])
        k = CLOSE.index(dz)
        return add16(near[s][2][k], near_1[s][1, k], near_2[s][k])

    narrow = ZChain(narrow_piece)
    wide.shift()
    narrow.shift()
    made = wide.merge()
    near_1 = couple(near_1, made)
    near_send = [add16(near[s][1], near_1[s][0]) for s in sections]
    near_2 = [second_swap(s, near_send[s]) for s in sections]
    made = narrow.merge()
    near_2 = couple(near_2, made)

    wide.shift()
    narrow.shift()
    wide.merge()

    def ring_sum(s, span, *more):
        return add(ring[s][0][span], wide.done[s, 1][span], wide.done[s, -1][span], *more)

    ring_first = [ring_sum(s, slice(0, 2)).astype(bf16) for s in sections]
    ring_1 = [first_swap(s, ring_first[s]) for s in sections]
    made = narrow.merge()
    narrow.shift()
    got = code_exchange(made)
    ring_1 = couple(ring_1, made)
    ring_send = [ring_sum(s, 2, ring_1[s][0]).astype(bf16) for s in sections]
    ring_2 = [second_swap(s, ring_send[s]) for s in sections]
    narrow.merge()
    narrow.shift()
    narrow.merge()
    sums = []
    for s in sections:
        k = CLOSE.index(0)
        last = add(
            near[s][2][k], near_1[s][1, k], near_2[s][k], narrow.done[s, 1], narrow.done[s, -1]
        )
        sums.append(jnp.concatenate([ring_sum(s, 3, ring_1[s][1], ring_2[s]), last], axis=-1))
    return sums, got


def norm_of(codes):
    values = codes.astype(f32)
    scales = lax.rsqrt(jnp.mean(values * values, axis=-1, keepdims=True) + eps)
    return values, scales


def grad_through_norm(grad_out, codes, left, right):
    values, scales = norm_of(codes)
    summed = left.astype(f32) + right.astype(f32)
    inner = jnp.mean(summed * values, axis=-1, keepdims=True)
    return (
        grad_out.astype(f32) + scales * summed - values * (scales * scales * scales) * inner
    )


def dot_rows(left, right):
    return lax.dot_general(left, right, (((1,), (0,)), ((), ())), preferred_element_type=f32)


def dot_last(left, right):
    return lax.dot_general(left, right, (((1,), (1,)), ((), ())), preferred_element_type=f32)


def dot_first(left, right):
    return lax.dot_general(left, right, (((0,), (0,)), ((), ())), preferred_element_type=f32)


def start_tiles(source, target, sems):
    copies = []
    for k, low in enumerate(range(0, COLS, TILE)):
        span = slice(low, low + TILE)
        copy = pltpu.make_async_copy(source.at[:, span], target.at[:, span], sems.at[k])
        copy.start()
        copies.append(copy)
    return copies


def forward_kernel(n_terms, keep, *refs):
    terms, (dec_ref, enc_hbm), outs = refs[:n_terms], refs[n_terms : n_terms + 2], refs[n_terms + 2 :]
    enc_ref, enc_sems = outs[-2:]
    enc_copies = start_tiles(enc_hbm, enc_ref, enc_sems)
    code_ref, part_ref = outs[:2]
    codes = terms[1][...].astype(f32)
    if n_terms == 3:
        codes = codes + terms[2][...].astype(f32)
    codes = (terms[0][...].astype(f32) + codes).astype(bf16)
    code_ref[...] = codes
    values, scales = norm_of(codes)
    normed = (values * scales).astype(bf16)
    total = None
    for k, low in enumerate(range(0, COLS, TILE)):
        span = slice(low, low + TILE)
        half = 0.5 * dot_rows(normed, dec_ref[:, span])
        bend = jnp.tanh(half)
        gated = (half + half * bend).astype(bf16)
        if keep:
            outs[2][:, span] = gated
            outs[3][:, span] = (0.5 * (1.0 + bend) * (1.0 + half * (1.0 - bend))).astype(bf16)
        enc_copies[k].wait()
        part = dot_last(gated, enc_ref[:, span])
        total = part if total is None else total + part
    part_ref[...] = total.astype(bf16)


def section_cost(rows):
    return pl.CostEstimate(
        flops=4 * rows * WIDTH * COLS,
        bytes_accessed=4 * WIDTH * COLS + 8 * rows * WIDTH,
        transcendentals=rows * COLS,
    )


def tile_scratch(rows):
    return [pltpu.VMEM((rows, COLS), bf16), pltpu.SemaphoreType.DMA((COLS // TILE,))]


def section_forward(terms, weights, keep):
    rows = terms[0].shape[0]
    vmem, hbm = pl.BlockSpec(memory_space=pltpu.VMEM), pl.BlockSpec(memory_space=pl.ANY)
    out_shape = [jax.ShapeDtypeStruct((rows, WIDTH), bf16)] * 2
    if keep:
        out_shape += [jax.ShapeDtypeStruct((rows, COLS), bf16)] * 2
    return pl.pallas_call(
        functools.partial(forward_kernel, len(terms), keep),
        in_specs=[vmem] * (len(terms) + 1) + [hbm],
        out_specs=[vmem] * len(out_shape),
        out_shape=out_shape,
        scratch_shapes=tile_scratch(WIDTH),
        compiler_params=pltpu.CompilerParams(vmem_limit_bytes=24 * MIB),
        cost_estimate=section_cost(rows),
    )(*terms, *weights)


def backward_kernel(n_terms, keep, *refs):
    terms, (dec_ref, enc_hbm, slope_hbm) = refs[:n_terms], refs[n_terms : n_terms + 3]
    outs = refs[n_terms + 3 :]
    enc_ref, enc_sems, slope_ref, slope_sems = outs[-4:]
    enc_copies = start_tiles(enc_hbm, enc_ref, enc_sems)
    slope_copies = start_tiles(slope_hbm, slope_ref, slope_sems)
    grad_ref, part_ref = outs[:2]
    if n_terms == 2:
        grad = terms[0][...].astype(f32) + terms[1][...].astype(f32)
    else:
        grad = grad_through_norm(*[t[...] for t in terms])
        if keep:
            outs[3][...] = grad
    grad = grad.astype(bf16)
    grad_ref[...] = grad
    total = None
    for k, low in enumerate(range(0, COLS, TILE)):
        span = slice(low, low + TILE)
        enc_copies[k].wait()
        gated_grad = dot_rows(grad, enc_ref[:, span])
        slope_copies[k].wait()
        hidden_grad = (gated_grad * slope_ref[:, span].astype(f32)).astype(bf16)
        if keep:
            outs[2][:, span] = hidden_grad
        part = dot_last(hidden_grad, dec_ref[:, span])
        total = part if total is None else total + part
    part_ref[...] = total.astype(bf16)


def section_backward(terms, slope, weights, keep):
    rows = terms[0].shape[0]
    vmem, hbm = pl.BlockSpec(memory_space=pltpu.VMEM), pl.BlockSpec(memory_space=pl.ANY)
    out_shape = [jax.ShapeDtypeStruct((rows, WIDTH), bf16)] * 2
    if keep:
        out_shape += [jax.ShapeDtypeStruct((rows, COLS), bf16)]
        if len(terms) > 2:
            out_shape += [jax.ShapeDtypeStruct((rows, WIDTH), f32)]
    return pl.pallas_call(
        functools.partial(backward_kernel, len(terms), keep),
        in_specs=[vmem] * (len(terms) + 1) + [hbm, hbm],
        out_specs=[vmem] * len(out_shape),
        out_shape=out_shape,
        scratch_shapes=tile_scratch(WIDTH) + tile_scratch(rows),
        compiler_params=pltpu.CompilerParams(vmem_limit_bytes=24 * MIB),
        cost_estimate=section_cost(rows),
    )(*terms, *weights, slope)


def norm_grad_kernel(grad_ref, code_ref, left_ref, right_ref, out_ref):
    out_ref[...] = grad_through_norm(
        grad_ref[...], code_ref[...], left_ref[...], right_ref[...]
    ).astype(out_ref.dtype)


def norm_grad(grad, codes, left, right, dtype):
    return pl.pallas_call(
        norm_grad_kernel, out_shape=jax.ShapeDtypeStruct(grad.shape, dtype)
    )(grad, codes, left, right)


def seed_kernel(flag_ref, lengths_ref, code_ref, left_ref, right_ref, head_ref, out_ref):
    codes = (
        code_ref[...].astype(f32) + (left_ref[...].astype(f32) + right_ref[...].astype(f32))
    ).astype(bf16)
    head = head_ref[...].astype(f32)
    scores = jnp.sum(codes.astype(f32) * head, axis=-1, keepdims=True)
    rows = scores.shape[0]
    seq_len = rows // 2
    position = lax.broadcasted_iota(jnp.int32, (rows, 1), 0)
    chosen_length, other_length = lengths_ref[0], lengths_ref[1]
    chosen = jnp.where(position < seq_len, 1.0, 0.0)
    limit = jnp.where(position < seq_len, chosen_length, other_length + seq_len)
    valid = jnp.where(position < limit, 1.0, 0.0)
    chosen_count = jnp.full((1, 1), chosen_length, jnp.int32).astype(f32)
    other_count = jnp.full((1, 1), other_length, jnp.int32).astype(f32)
    chosen_sum = jnp.sum(scores * valid * chosen, axis=0, keepdims=True)
    other_sum = jnp.sum(scores * valid * (1.0 - chosen), axis=0, keepdims=True)
    gap = other_sum / other_count - chosen_sum / chosen_count
    weight = loss_scale * jax.nn.sigmoid(gap)
    token = (1.0 - chosen) * (weight / other_count) - chosen * (weight / chosen_count)
    token = token * valid * jnp.full((1, 1), flag_ref[0], jnp.int32).astype(f32)
    out_ref[...] = (token * head).astype(bf16)


def reward_seed(flag, lengths, codes, left, right, head):
    vmem = pl.BlockSpec(memory_space=pltpu.VMEM)
    smem = pl.BlockSpec(memory_space=pltpu.SMEM)
    return pl.pallas_call(
        seed_kernel,
        in_specs=[smem, smem, vmem, vmem, vmem, vmem],
        out_specs=vmem,
        out_shape=jax.ShapeDtypeStruct(codes.shape, bf16),
    )(flag, lengths, codes, left, right, head)


def weight_grad_kernel(order, *refs):
    grads, codes = refs[0:CHUNKS], refs[CHUNKS : 2 * CHUNKS]
    gated, hidden = refs[2 * CHUNKS : 3 * CHUNKS], refs[3 * CHUNKS : 4 * CHUNKS]
    outs = refs[4 * CHUNKS :]
    ring_refs, far_refs, near_refs = outs[:Z], outs[Z : Z + 3], outs[Z + 3 :]

    def joined(group):
        return jnp.concatenate([ref[...] for ref in group], axis=0)

    values, scales = norm_of(joined(codes))
    normed = (values * scales).astype(bf16)
    for mat, (left, group) in enumerate(((normed, hidden), (joined(grads), gated))):
        for tr in range(2):
            for low, high in ((0, XPART), (XPART, SPAN)):
                span = slice(tr * SPAN + low, tr * SPAN + high)
                right = jnp.concatenate([ref[:, span] for ref in group], axis=0)
                result = dot_first(left, right).astype(bf16)
                for xr in range(2):
                    place_at = order.index((tr, xr))
                    for dz in range(Z):
                        row = (xr * Z + dz) * SUB
                        piece = result[row : row + SUB]
                        if low == 0:
                            ring_refs[dz][place_at, mat] = piece
                            continue
                        group_refs, k = (
                            (far_refs, DISTANT.index(dz))
                            if dz in DISTANT
                            else (near_refs, CLOSE.index(dz))
                        )
                        if place_at < 2:
                            group_refs[0][place_at, k, mat] = piece
                        else:
                            group_refs[place_at - 1][k, mat] = piece


def weight_grads(section, grads, codes, gated, hidden):
    order = ((1, 0), (0, 1), (1, 1), (0, 0)) if section == 0 else ((1, 0), (1, 1), (0, 1), (0, 0))
    rows = grads[0].shape[0]

    def group_shapes(count):
        tail = (count, 2, SUB, ZPART)
        return [jax.ShapeDtypeStruct(shape, bf16) for shape in ((2,) + tail, tail, tail)]

    return pl.pallas_call(
        functools.partial(weight_grad_kernel, order),
        out_shape=[jax.ShapeDtypeStruct((4, 2, SUB, XPART), bf16)] * Z
        + group_shapes(len(DISTANT))
        + group_shapes(len(CLOSE)),
        compiler_params=pltpu.CompilerParams(vmem_limit_bytes=40 * MIB),
        cost_estimate=pl.CostEstimate(
            flops=4 * rows * CHUNKS * WIDTH * COLS,
            bytes_accessed=4 * WIDTH * COLS,
            transcendentals=0,
        ),
    )(*grads, *codes, *gated, *hidden)


def to_local(value, pair, z_index):
    lead = value.shape[:-1]
    value = value.reshape(lead + (2, Z, SUB))
    axis = len(lead)
    value = jnp.where(pair == 0, value, jnp.flip(value, axis))
    doubled = jnp.concatenate([value, value], axis=axis + 1)
    return lax.dynamic_slice_in_dim(doubled, z_index, Z, axis + 1).reshape(lead + (WIDTH,))


def to_global(value, pair, z_index):
    return to_local(value, pair, (Z - z_index) % Z)


def on_device(codes_in, lengths, dec_weight, enc_weight, head):
    pipe = lax.axis_index("pipe")
    core, stage = pipe % 2, pipe // 2
    tensor = lax.axis_index("tensor")
    dp = lax.axis_index("dp")
    pair, z_index = dp // Z, dp % Z

    weights = gather_weights(dec_weight, enc_weight, core)

    codes_in = lax.dynamic_slice_in_dim(codes_in, tensor * CHUNKS, CHUNKS, 0)
    lengths = lax.dynamic_slice_in_dim(lengths, tensor * CHUNKS, CHUNKS, 0)
    codes_in = to_local(codes_in, pair, z_index)
    codes_in = jnp.where(stage == 0, codes_in, jnp.zeros_like(codes_in))
    head = to_local(head[None], pair, z_index)
    is_last = (stage == STAGES - 1).astype(jnp.int32)[None]

    rows = codes_in.shape[1]
    blank = jnp.zeros((rows, WIDTH), bf16)
    chunks = range(CHUNKS)
    received = [blank] * CHUNKS
    codes = [[None, None] for _ in chunks]
    gated = [[None, None] for _ in chunks]
    slope = [[None, None] for _ in chunks]
    seeds = [None] * CHUNKS
    for step in range(STAGES):
        keep = step == STAGES - 1
        for m in chunks:
            first = section_forward([received[m], codes_in[m]], weights[0], keep)
            second = section_forward([first[0], first[1], core_swap(first[1])], weights[1], keep)
            across = core_swap(second[1])
            if keep:
                codes[m] = [first[0], second[0]]
                gated[m] = [first[2], second[2]]
                slope[m] = [first[3], second[3]]
                seeds[m] = reward_seed(is_last, lengths[m], second[0], second[1], across, head)
            else:
                received[m] = y_shift(add(second[0], add(second[1], across)).astype(bf16), 1)

    received = [blank] * CHUNKS
    grads = [[None] * CHUNKS, [None] * CHUNKS]
    hidden = [[None] * CHUNKS, [None] * CHUNKS]
    through = [[None] * CHUNKS, [None] * CHUNKS]
    for step in range(STAGES):
        keep = step == STAGES - 1
        for m in chunks:
            second = section_backward([received[m], seeds[m]], slope[m][1], weights[1], keep)
            second_across = core_swap(second[1])
            first = section_backward(
                [second[0], codes[m][1], second[1], second_across], slope[m][0], weights[0], keep
            )
            first_across = core_swap(first[1])
            passed = norm_grad(
                first[0], codes[m][0], first[1], first_across, f32 if keep else bf16
            )
            if keep:
                grads[0][m], grads[1][m] = first[0], second[0]
                hidden[0][m], hidden[1][m] = first[2], second[2]
                through[0][m], through[1][m] = passed, first[3]
            else:
                received[m] = y_shift(passed, -1)

    parts = [None, None]
    for section in (1, 0):
        parts[section] = weight_grads(
            section,
            grads[section],
            [codes[m][section] for m in chunks],
            [gated[m][section] for m in chunks],
            hidden[section],
        )

    code_grads = jnp.where(core == 0, jnp.stack(through[0]), jnp.stack(through[1]))
    code_grads = to_global(code_grads, pair, z_index)
    share = rows // 2
    kept = lax.dynamic_slice_in_dim(code_grads, tensor * share, share, 1)
    sent = lax.dynamic_slice_in_dim(code_grads, (1 - tensor) * share, share, 1).astype(bf16)

    def code_exchange(others):
        (late,) = couple((sent,), others)
        return lax.ppermute(late, "tensor", [(0, 1), (1, 0)])

    sums, got = reduce_weights(parts, code_exchange)
    got = got.astype(f32)
    code_out = jnp.where(
        tensor == 0, jnp.concatenate([kept, got], axis=0), jnp.concatenate([got, kept], axis=0)
    )

    mine = jnp.where(core == 0, sums[0], sums[1])
    other = core_swap(jnp.where(core == 0, sums[1], sums[0]))
    full = jnp.where(
        core == 0,
        jnp.concatenate([mine, other], axis=-1),
        jnp.concatenate([other, mine], axis=-1),
    )
    return (code_out[None], full[0][None], full[1][None])


def solution(mesh):
    in_specs = (
        P(None, "dp", None),
        P(None, "dp"),
        P("pipe", "dp", "tensor"),
        P("pipe", "dp", "tensor"),
        P(),
    )
    out_specs = (
        P("pipe", None, ("dp", "tensor"), None),
        P("pipe", "dp", "tensor"),
        P("pipe", "dp", "tensor"),
    )
    return jax.shard_map(
        on_device, mesh=mesh, in_specs=in_specs, out_specs=out_specs, check_vma=False
    )
```

time: 544 us -> 657 us (1.21)
  Pallas kernels: 116 us -> 180 us
  local copies, waits for them, and re-layouts: 94.4 us -> 113 us
  starting transfers between devices: 144 us -> 159 us
  waiting for transfers between devices: 161 us -> 172 us
    pallas_call x35 -> x36, Pallas kernels: 96.8 us -> 160 us  [the longest x16 77.2 us: section_backward(): pl.pallas_call(functools.partial(backward_kernel, len(terms), keep), in_s...]
    ppermute x12 -> x14, waiting for transfers between devices: 8.53 us -> 58.4 us  [swap_a(): lax.ppermute(value, 'dp', [(x * Z + z, (1 - x) * Z + z) for x in range(2)...]
    ppermute x32 -> x44, waiting for transfers between devices: 121 us -> 80.2 us  [z_shift(): lax.ppermute(value, 'dp', [(x * Z + z, x * Z + (z + steps) % Z) for x in...]
    unnamed x228 -> x321, local copies, waits for them, and re-layouts: 68 us -> 99.6 us
    ppermute x32 -> x44, starting transfers between devices: 35.9 us -> 51.2 us  [z_shift(): lax.ppermute(value, 'dp', [(x * Z + z, x * Z + (z + steps) % Z) for x in...]
    split x6 -> x0, local copies, waits for them, and re-layouts: 7.74 us -> none  [the longest x4 5.86 us: add_high(): low, high = jnp.split(whole, 2, axis)]
    ppermute x12 -> x14, waiting for transfers between devices: 15.1 us -> 17.6 us  [swap_b(): return lax.ppermute(value, ('dp', 'tensor'), pairs)]
    ppermute x12 -> x14, starting transfers between devices: 20.5 us -> 21.7 us  [swap_b(): return lax.ppermute(value, ('dp', 'tensor'), pairs)]
  transfers between devices with their start and end apart: 103 -> 119, of which waited for: 32 -> 41; matrix products, arithmetic and copies ran while one was open for 6% -> 5% of each run, Pallas kernels for 20% -> 27%
where the time goes in v3:
time: 657 us; the launch traced here: 646 us
  Pallas kernels  180 us (27%)
  waiting for transfers between devices  172 us (26%)
  starting transfers between devices  159 us (24%)
  local copies, waits for them, and re-layouts  113 us (17%)
  other arithmetic  18.5 us (3%)
    unnamed x321, local copies, waits for them, and re-layouts  99.6 us
    ppermute x44, waiting for transfers between devices, z_shift(): lax.ppermute(value, 'dp', [(x * Z + z, x * Z + (z + steps) % Z) for x in...  80.2 us
    pallas_call x16, Pallas kernels, section_backward(): pl.pallas_call(functools.partial(backward_kernel, len(terms), keep), in_s...  77.2 us
    pallas_call x16, Pallas kernels, section_forward(): pl.pallas_call(functools.partial(forward_kernel, len(terms), keep), in_sp...  67.6 us
    ppermute x14, waiting for transfers between devices, swap_a(): lax.ppermute(value, 'dp', [(x * Z + z, (1 - x) * Z + z) for x in range(2)...  58.4 us
    ppermute x34, starting transfers between devices, core_swap(): return lax.ppermute(value, 'pipe', [(i, i ^ 1) for i in range(8)])  52.7 us
    ppermute x44, starting transfers between devices, z_shift(): lax.ppermute(value, 'dp', [(x * Z + z, x * Z + (z + steps) % Z) for x in...  51.2 us
    ppermute x12, starting transfers between devices, y_shift(): lax.ppermute(value, 'pipe', [(i, i + 2 * steps) for i in range(8) if 0 <=...  27.8 us
  transfers between devices with their start and end apart: 119, of which 41 were waited for; matrix products, arithmetic and copies ran while one was open for 5% of the time, Pallas kernels for 27%

profile of v3, /device:TPU:1, one launch (start us, length us, event | category | flops | bytes accessed | tf_op | source)
XLA Modules:
  0.0 645.7 jit_solution(14859067343945596488)
XLA Ops:
  38.0 5.1 collective-permute-done.11.refs_5_
  47.3 11.5 %collective-permute-done.15.refs_1_ = bf16[5,2,32,1152]{3,2,1,0:T(8,128)(2,1)S(1)} collective-permute-done((bf16[5,2,32,1152]{3,2,1,0:T(8,128)(2,1)S(1)}, bf16[5,2,32,1152]{3,2,1,0:T(8,128)(2,1)S(1)}, u32[]{:S(2)}, u32[]{:S(2)}) %collective-permute-start.15) | collective-permute-done | bytes 737312 | tf_op jit(solution)/shard_map/ppermute | solution.py:49
  71.6 9.6 %collective-permute-done.21 = bf16[1,2,32,1152]{3,2,1,0:T(8,128)(2,1)S(1)} collective-permute-done((bf16[1,2,32,1152]{3,2,1,0:T(8,128)(2,1)S(1)}, bf16[1,2,32,1152]{3,2,1,0:T(8,128)(2,1)S(1)}, u32[]{:S(2)}, u32[]{:S(2)}) %collective-permute-start.21) | collective-permute-done | bytes 147488 | tf_op jit(solution)/shard_map/ppermute | solution.py:43
  131.7 5.4 shard_map.76
  148.5 15.0 %collective-permute-start.33 = (bf16[128,512]{1,0:T(8,128)(2,1)S(1)}, bf16[128,512]{1,0:T(8,128)(2,1)S(1)}, u32[]{:S(2)}, u32[]{:S(2)}) collective-permute-start(bf16[128,512]{1,0:T(8,128)(2,1)S(1)} %get-tuple-element.191.refs_1_), channel_id=1, source_target_pairs={{0,32},{32,0},{64,96},{96,64},{128,160},{160,128},{192,224},{224,1... | collective-permute-start | bytes 393224 | tf_op jit(solution)/shard_map/ppermute | solution.py:33
  255.1 5.2 shard_map.85
  262.5 5.2 shard_map.106
  296.9 5.3 shard_map.88
  325.2 5.1 shard_map.90
  341.0 4.9 shard_map.112
  362.6 5.1 shard_map.93
  378.4 4.9 shard_map.115
  400.1 5.0 shard_map.96
  406.7 5.8 shard_map.117
  419.6 4.9 shard_map.97
  433.1 5.9 shard_map.118
  484.2 8.5 %collective-permute-done.88 = bf16[4,2,32,896]{3,2,1,0:T(8,128)(2,1)S(1)} collective-permute-done((bf16[4,2,32,896]{3,2,1,0:T(8,128)(2,1)S(1)}, bf16[4,2,32,896]{3,2,1,0:T(8,128)(2,1)S(1)}, u32[]{:S(2)}, u32[]{:S(2)}) %collective-permute-start.88) | collective-permute-done | bytes 458784 | tf_op jit(solution)/shard_map/ppermute | solution.py:43
  503.7 9.7 %collective-permute-done.94 = bf16[4,2,32,896]{3,2,1,0:T(8,128)(2,1)S(1)} collective-permute-done((bf16[4,2,32,896]{3,2,1,0:T(8,128)(2,1)S(1)}, bf16[4,2,32,896]{3,2,1,0:T(8,128)(2,1)S(1)}, u32[]{:S(2)}, u32[]{:S(2)}) %collective-permute-start.94) | collective-permute-done | bytes 458784 | tf_op jit(solution)/shard_map/ppermute | solution.py:43
  514.5 10.3 %collective-permute-done.93 = bf16[4,2,32,896]{3,2,1,0:T(8,128)(2,1)S(1)} collective-permute-done((bf16[4,2,32,896]{3,2,1,0:T(8,128)(2,1)S(1)}, bf16[4,2,32,896]{3,2,1,0:T(8,128)(2,1)S(1)}, u32[]{:S(2)}, u32[]{:S(2)}) %collective-permute-start.93) | collective-permute-done | bytes 458784 | tf_op jit(solution)/shard_map/ppermute | solution.py:43
  527.6 22.3 %collective-permute-done.91 = bf16[2,3,2,32,1152]{4,3,2,1,0:T(8,128)(2,1)S(1)} collective-permute-done((bf16[2,3,2,32,1152]{4,3,2,1,0:T(8,128)(2,1)S(1)}, bf16[2,3,2,32,1152]{4,3,2,1,0:T(8,128)(2,1)S(1)}, u32[]{:S(2)}, u32[]{:S(2)}) %collective-permute-start.91) | collective-permute-done | bytes 884768 | tf_op jit(solution)/shard_map/ppermute | solution.py:49
  562.0 5.9 collective-permute-done.84
  588.1 5.5 collective-permute-done.98
  615.4 17.9 %collective-permute-start.118 = (f32[2,32,2048]{2,1,0:T(8,128)S(1)}, f32[2,32,2048]{2,1,0:T(8,128)S(1)}, u32[]{:S(2)}, u32[]{:S(2)}) collective-permute-start(f32[2,32,2048]{2,1,0:T(8,128)S(1)} %get-tuple-element.325), channel_id=1, source_target_pairs={{0,32},{32,0},{64,96},{96,64},{128,160},{160,128},{192,224},{224,1... | collective-permute-start | bytes 1572872 | tf_op jit(solution)/shard_map/ppermute | solution.py:33
  635.9 7.0 %collective-permute-done.103 = bf16[2,64,512]{1,2,0:T(8,128)(2,1)S(1)} collective-permute-done((bf16[2,64,512]{1,2,0:T(8,128)(2,1)S(1)}, bf16[2,64,512]{1,2,0:T(8,128)(2,1)S(1)}, u32[]{:S(2)}, u32[]{:S(2)}) %collective-permute-start.103) | collective-permute-done | bytes 131104 | tf_op jit(solution)/shard_map/ppermute | solution.py:647
  (665 shorter events, 451.8 us)
Async XLA Ops:
  31.6 31.8 %collective-permute-start.10 = (bf16[2,2,2,2,32,896]{5,4,3,2,1,0:T(8,128)(2,1)S(1)}, bf16[2,2,2,2,32,896]{5,4,3,2,1,0:T(8,128)(2,1)S(1)}, u32[]{:S(2)}, u32[]{:S(2)}) collective-permute-start(bf16[2,2,2,2,32,896]{5,4,3,2,1,0:T(8,128)(2,1)S(1)} %pad_maximum_fusion.refs_8_), channel_id=1, source_target_pairs={{0,14},{2,0},{4,2},{6,4},{8,6},{10,8},{12,10},{14,12},{16,30},{18,... | collective-permute-start | bytes 2752520 | tf_op jit(solution)/shard_map/ppermute | solution.py:43
  32.5 30.8 %collective-permute-start.9 = (bf16[2,2,2,2,32,896]{5,4,3,2,1,0:T(8,128)(2,1)S(1)}, bf16[2,2,2,2,32,896]{5,4,3,2,1,0:T(8,128)(2,1)S(1)}, u32[]{:S(2)}, u32[]{:S(2)}) collective-permute-start(bf16[2,2,2,2,32,896]{5,4,3,2,1,0:T(8,128)(2,1)S(1)} %pad_maximum_fusion.refs_8_), channel_id=1, source_target_pairs={{0,2},{2,4},{4,6},{6,8},{8,10},{10,12},{12,14},{14,0},{16,18},{18,... | collective-permute-start | bytes 2752520 | tf_op jit(solution)/shard_map/ppermute | solution.py:43
  37.3 21.5 %collective-permute-start.15 = (bf16[5,2,32,1152]{3,2,1,0:T(8,128)(2,1)S(1)}, bf16[5,2,32,1152]{3,2,1,0:T(8,128)(2,1)S(1)}, u32[]{:S(2)}, u32[]{:S(2)}) collective-permute-start(bf16[5,2,32,1152]{3,2,1,0:T(8,128)(2,1)S(1)} %get-tuple-element.332.refs_0_), channel_id=1, source_target_pairs={{0,16},{2,18},{4,20},{6,22},{8,24},{10,26},{12,28},{14,30},{16,0},... | collective-permute-start | bytes 2211848 | tf_op jit(solution)/shard_map/ppermute | solution.py:49
  63.4 26.7 %collective-permute-start.17 = (bf16[2,2,2,2,32,896]{5,4,3,2,1,0:T(8,128)(2,1)S(1)}, bf16[2,2,2,2,32,896]{5,4,3,2,1,0:T(8,128)(2,1)}, u32[]{:S(2)}, u32[]{:S(2)}) collective-permute-start(bf16[2,2,2,2,32,896]{5,4,3,2,1,0:T(8,128)(2,1)S(1)} %collective-permute-done.9.refs_10_), channel_id=1, source_target_pairs={{0,2},{2,4},{4,6},{6,8},{8,10},{10,12},{12,14},{14,0},{16,18},{18,... | collective-permute-start | bytes 2752520 | tf_op jit(solution)/shard_map/ppermute | solution.py:43
  66.2 23.8 %collective-permute-start.18 = (bf16[2,2,2,2,32,896]{5,4,3,2,1,0:T(8,128)(2,1)S(1)}, bf16[2,2,2,2,32,896]{5,4,3,2,1,0:T(8,128)(2,1)}, u32[]{:S(2)}, u32[]{:S(2)}) collective-permute-start(bf16[2,2,2,2,32,896]{5,4,3,2,1,0:T(8,128)(2,1)S(1)} %collective-permute-done.10.refs_9_), channel_id=1, source_target_pairs={{0,14},{2,0},{4,2},{6,4},{8,6},{10,8},{12,10},{14,12},{16,30},{18,... | collective-permute-start | bytes 2752520 | tf_op jit(solution)/shard_map/ppermute | solution.py:43
  90.0 22.4 %collective-permute-start.23 = (bf16[2,2,2,2,32,896]{5,4,3,2,1,0:T(8,128)(2,1)}, bf16[2,2,2,2,32,896]{5,4,3,2,1,0:T(8,128)(2,1)S(1)}, u32[]{:S(2)}, u32[]{:S(2)}) collective-permute-start(bf16[2,2,2,2,32,896]{5,4,3,2,1,0:T(8,128)(2,1)} %collective-permute-done.17.refs_12_), channel_id=1, source_target_pairs={{0,2},{2,4},{4,6},{6,8},{8,10},{10,12},{12,14},{14,0},{16,18},{18,... | collective-permute-start | bytes 2752520 | tf_op jit(solution)/shard_map/ppermute | solution.py:43
  91.0 21.5 %collective-permute-start.24 = (bf16[2,2,2,2,32,896]{5,4,3,2,1,0:T(8,128)(2,1)}, bf16[2,2,2,2,32,896]{5,4,3,2,1,0:T(8,128)(2,1)S(1)}, u32[]{:S(2)}, u32[]{:S(2)}) collective-permute-start(bf16[2,2,2,2,32,896]{5,4,3,2,1,0:T(8,128)(2,1)} %collective-permute-done.18.refs_11_), channel_id=1, source_target_pairs={{0,14},{2,0},{4,2},{6,4},{8,6},{10,8},{12,10},{14,12},{16,30},{18,... | collective-permute-start | bytes 2752520 | tf_op jit(solution)/shard_map/ppermute | solution.py:43
  113.3 23.8 %collective-permute-start.31 = (bf16[1,2,2,2,32,896]{5,4,3,2,1,0:T(8,128)(2,1)}, bf16[1,2,2,2,32,896]{5,4,3,2,1,0:T(8,128)(2,1)}, u32[]{:S(2)}, u32[]{:S(2)}) collective-permute-start(bf16[1,2,2,2,32,896]{5,4,3,2,1,0:T(8,128)(2,1)} %slice.334), channel_id=1, source_target_pairs={{0,2},{2,4},{4,6},{6,8},{8,10},{10,12},{12,14},{14,0},{16,18},{18,... | collective-permute-start | bytes 1376264 | tf_op jit(solution)/shard_map/ppermute | solution.py:43
  114.1 23.0 %collective-permute-start.32 = (bf16[1,2,2,2,32,896]{5,4,3,2,1,0:T(8,128)(2,1)}, bf16[1,2,2,2,32,896]{5,4,3,2,1,0:T(8,128)(2,1)}, u32[]{:S(2)}, u32[]{:S(2)}) collective-permute-start(bf16[1,2,2,2,32,896]{5,4,3,2,1,0:T(8,128)(2,1)} %slice.335), channel_id=1, source_target_pairs={{0,14},{2,0},{4,2},{6,4},{8,6},{10,8},{12,10},{14,12},{16,30},{18,... | collective-permute-start | bytes 1376264 | tf_op jit(solution)/shard_map/ppermute | solution.py:43
  148.5 23.6 %collective-permute-start.33 = (bf16[128,512]{1,0:T(8,128)(2,1)S(1)}, bf16[128,512]{1,0:T(8,128)(2,1)S(1)}, u32[]{:S(2)}, u32[]{:S(2)}) collective-permute-start(bf16[128,512]{1,0:T(8,128)(2,1)S(1)} %get-tuple-element.191.refs_1_), channel_id=1, source_target_pairs={{0,32},{32,0},{64,96},{96,64},{128,160},{160,128},{192,224},{224,1... | collective-permute-start | bytes 393224 | tf_op jit(solution)/shard_map/ppermute | solution.py:33
  416.9 54.5 %collective-permute-start.82 = (bf16[4,2,32,896]{3,2,1,0:T(8,128)(2,1)}, bf16[4,2,32,896]{3,2,1,0:T(8,128)(2,1)}, u32[]{:S(2)}, u32[]{:S(2)}) collective-permute-start(bf16[4,2,32,896]{3,2,1,0:T(8,128)(2,1)} %get-tuple-element.280), channel_id=1, source_target_pairs={{0,14},{2,0},{4,2},{6,4},{8,6},{10,8},{12,10},{14,12},{16,30},{18,... | collective-permute-start | bytes 1376264 | tf_op jit(solution)/shard_map/ppermute | solution.py:43
  417.2 57.5 %collective-permute-start.81 = (bf16[4,2,32,896]{3,2,1,0:T(8,128)(2,1)}, bf16[4,2,32,896]{3,2,1,0:T(8,128)(2,1)}, u32[]{:S(2)}, u32[]{:S(2)}) collective-permute-start(bf16[4,2,32,896]{3,2,1,0:T(8,128)(2,1)} %get-tuple-element.278), channel_id=1, source_target_pairs={{0,2},{2,4},{4,6},{6,8},{8,10},{10,12},{12,14},{14,0},{16,18},{18,... | collective-permute-start | bytes 1376264 | tf_op jit(solution)/shard_map/ppermute | solution.py:43
  418.5 132.6 %collective-permute-start.78 = (bf16[2,5,2,32,1152]{4,3,2,1,0:T(8,128)(2,1)}, bf16[2,5,2,32,1152]{4,3,2,1,0:T(8,128)(2,1)}, u32[]{:S(2)}, u32[]{:S(2)}) collective-permute-start(bf16[2,5,2,32,1152]{4,3,2,1,0:T(8,128)(2,1)} %get-tuple-element.272), channel_id=1, source_target_pairs={{0,17},{1,16},{2,19},{3,18},{4,21},{5,20},{6,23},{7,22},{8,25},{9,... | collective-permute-start | bytes 4423688 | tf_op jit(solution)/shard_map/ppermute | solution.py:59
  426.2 34.0 %collective-permute-start.54 = (bf16[128,512]{1,0:T(8,128)(2,1)}, bf16[128,512]{1,0:T(8,128)(2,1)}, u32[]{:S(2)}, u32[]{:S(2)}) collective-permute-start(bf16[128,512]{1,0:T(8,128)(2,1)} %get-tuple-element.225.left_ref), channel_id=1, source_target_pairs={{0,32},{32,0},{64,96},{96,64},{128,160},{160,128},{192,224},{224,1... | collective-permute-start | bytes 393224 | tf_op jit(solution)/shard_map/ppermute | solution.py:33
  440.8 24.8 %collective-permute-start.76 = (bf16[128,512]{1,0:T(8,128)(2,1)}, bf16[128,512]{1,0:T(8,128)(2,1)S(1)}, u32[]{:S(2)}, u32[]{:S(2)}) collective-permute-start(bf16[128,512]{1,0:T(8,128)(2,1)} %get-tuple-element.259.left_ref), channel_id=1, source_target_pairs={{0,32},{32,0},{64,96},{96,64},{128,160},{160,128},{192,224},{224,1... | collective-permute-start | bytes 393224 | tf_op jit(solution)/shard_map/ppermute | solution.py:33
  460.3 64.6 %collective-permute-start.92 = (bf16[2,3,2,32,1152]{4,3,2,1,0:T(8,128)(2,1)}, bf16[2,3,2,32,1152]{4,3,2,1,0:T(8,128)(2,1)}, u32[]{:S(2)}, u32[]{:S(2)}) collective-permute-start(bf16[2,3,2,32,1152]{4,3,2,1,0:T(8,128)(2,1)} %get-tuple-element.292), channel_id=1, source_target_pairs={{0,17},{1,16},{2,19},{3,18},{4,21},{5,20},{6,23},{7,22},{8,25},{9,... | collective-permute-start | bytes 2654216 | tf_op jit(solution)/shard_map/ppermute | solution.py:59
  499.8 52.8 %collective-permute-start.77 = (bf16[2,5,2,32,1152]{4,3,2,1,0:T(8,128)(2,1)S(1)}, bf16[2,5,2,32,1152]{4,3,2,1,0:T(8,128)(2,1)S(1)}, u32[]{:S(2)}, u32[]{:S(2)}) collective-permute-start(bf16[2,5,2,32,1152]{4,3,2,1,0:T(8,128)(2,1)S(1)} %copy-done.128), channel_id=1, source_target_pairs={{0,16},{2,18},{4,20},{6,22},{8,24},{10,26},{12,28},{14,30},{16,0},... | collective-permute-start | bytes 4423688 | tf_op jit(solution)/shard_map/ppermute | solution.py:49
  503.6 46.3 %collective-permute-start.91 = (bf16[2,3,2,32,1152]{4,3,2,1,0:T(8,128)(2,1)S(1)}, bf16[2,3,2,32,1152]{4,3,2,1,0:T(8,128)(2,1)S(1)}, u32[]{:S(2)}, u32[]{:S(2)}) collective-permute-start(bf16[2,3,2,32,1152]{4,3,2,1,0:T(8,128)(2,1)S(1)} %copy-done.142), channel_id=1, source_target_pairs={{0,16},{2,18},{4,20},{6,22},{8,24},{10,26},{12,28},{14,30},{16,0},... | collective-permute-start | bytes 2654216 | tf_op jit(solution)/shard_map/ppermute | solution.py:49
  524.8 29.7 %collective-permute-start.107 = (bf16[4,2,32,896]{3,2,1,0:T(8,128)(2,1)S(1)}, bf16[4,2,32,896]{3,2,1,0:T(8,128)(2,1)S(1)}, u32[]{:S(2)}, u32[]{:S(2)}) collective-permute-start(bf16[4,2,32,896]{3,2,1,0:T(8,128)(2,1)S(1)} %add_convert_fusion.3), channel_id=1, source_target_pairs={{0,2},{2,4},{4,6},{6,8},{8,10},{10,12},{12,14},{14,0},{16,18},{18,... | collective-permute-start | bytes 1376264 | tf_op jit(solution)/shard_map/ppermute | solution.py:43
  524.9 34.2 %collective-permute-start.105 = (bf16[4,2,32,896]{3,2,1,0:T(8,128)(2,1)S(1)}, bf16[4,2,32,896]{3,2,1,0:T(8,128)(2,1)S(1)}, u32[]{:S(2)}, u32[]{:S(2)}) collective-permute-start(bf16[4,2,32,896]{3,2,1,0:T(8,128)(2,1)S(1)} %add_convert_fusion.4), channel_id=1, source_target_pairs={{0,14},{2,0},{4,2},{6,4},{8,6},{10,8},{12,10},{14,12},{16,30},{18,... | collective-permute-start | bytes 1376264 | tf_op jit(solution)/shard_map/ppermute | solution.py:43
  558.4 36.2 %collective-permute-start.96 = (bf16[3,2,32,1152]{3,2,1,0:T(8,128)(2,1)S(1)}, bf16[3,2,32,1152]{3,2,1,0:T(8,128)(2,1)S(1)}, u32[]{:S(2)}, u32[]{:S(2)}) collective-permute-start(bf16[3,2,32,1152]{3,2,1,0:T(8,128)(2,1)S(1)} %fusion.2), channel_id=1, source_target_pairs={{0,16},{2,18},{4,20},{6,22},{8,24},{10,26},{12,28},{14,30},{16,0},... | collective-permute-start | bytes 1327112 | tf_op jit(solution)/shard_map/ppermute | solution.py:49
  559.1 35.6 %collective-permute-start.95 = (bf16[3,2,32,1152]{3,2,1,0:T(8,128)(2,1)S(1)}, bf16[3,2,32,1152]{3,2,1,0:T(8,128)(2,1)S(1)}, u32[]{:S(2)}, u32[]{:S(2)}) collective-permute-start(bf16[3,2,32,1152]{3,2,1,0:T(8,128)(2,1)S(1)} %fusion.3), channel_id=1, source_target_pairs={{0,17},{1,16},{2,19},{3,18},{4,21},{5,20},{6,23},{7,22},{8,25},{9,... | collective-permute-start | bytes 1327112 | tf_op jit(solution)/shard_map/ppermute | solution.py:59
  560.9 43.0 %collective-permute-start.109 = (bf16[2,2,32,896]{3,2,1,0:T(8,128)(2,1)S(1)}, bf16[2,2,32,896]{3,2,1,0:T(8,128)(2,1)S(1)}, u32[]{:S(2)}, u32[]{:S(2)}) collective-permute-start(bf16[2,2,32,896]{3,2,1,0:T(8,128)(2,1)S(1)} %add_convert_fusion.10), channel_id=1, source_target_pairs={{0,17},{1,16},{2,19},{3,18},{4,21},{5,20},{6,23},{7,22},{8,25},{9,... | collective-permute-start | bytes 688136 | tf_op jit(solution)/shard_map/ppermute | solution.py:59
  615.4 28.8 %collective-permute-start.118 = (f32[2,32,2048]{2,1,0:T(8,128)S(1)}, f32[2,32,2048]{2,1,0:T(8,128)S(1)}, u32[]{:S(2)}, u32[]{:S(2)}) collective-permute-start(f32[2,32,2048]{2,1,0:T(8,128)S(1)} %get-tuple-element.325), channel_id=1, source_target_pairs={{0,32},{32,0},{64,96},{96,64},{128,160},{160,128},{192,224},{224,1... | collective-permute-start | bytes 1572872 | tf_op jit(solution)/shard_map/ppermute | solution.py:33
  (252 other events, 1928.0 us)

commit v4 on v2

--- a/solution.py
+++ b/solution.py
@@ -22,8 +22,10 @@
 TILE = 1024
 NEAR = (0, 1, 2, 6, 7)
 FAR = (3, 4, 5)
+RING = (0, 1, 2, 3, 5, 6, 7)
 MIB = 1024 * 1024
-CHUNKS = 2
+CHUNKS = 1
+MICROS = 2
 STAGES = 4
 
 
@@ -75,20 +77,44 @@
 
 
 def place(pieces, moves):
-    vmem = pl.BlockSpec(memory_space=pltpu.VMEM)
+    vmem, hbm = pl.BlockSpec(memory_space=pltpu.VMEM), pl.BlockSpec(memory_space=pltpu.HBM)
     return pl.pallas_call(
         functools.partial(copy_kernel, moves, len(pieces)),
         out_shape=[jax.ShapeDtypeStruct((2, WIDTH, COLS), bf16)] * 2,
-        in_specs=[pl.BlockSpec(memory_space=pl.ANY)] * len(pieces),
+        in_specs=[hbm] * len(pieces),
         out_specs=[vmem, vmem],
         scratch_shapes=[pltpu.SemaphoreType.DMA((len(moves),))],
-        compiler_params=pltpu.CompilerParams(vmem_limit_bytes=24 * MIB),
+        compiler_params=pltpu.CompilerParams(vmem_limit_bytes=18 * MIB),
     )(*pieces)
 
 
 def spot(xr, dz, tr, low, high):
     row = (xr * Z + dz) * SUB
     return (slice(None), slice(row, row + SUB), slice(tr * SPAN + low, tr * SPAN + high))
+
+
+def narrow_moves(group, blocks, pieces, moves):
+    for section in range(2):
+        for (tr, xr), block in zip(((0, 0), (0, 1), (1, 1), (1, 0)), blocks[section]):
+            for k, dz in enumerate(group):
+                moves.append((len(pieces), (k,), section, spot(xr, dz, tr, XPART, SPAN)))
+            pieces.append(block)
+
+
+def ring_moves(dz, halves, pieces, moves):
+    for section in range(2):
+        for tr in range(2):
+            for xr in range(2):
+                which, index = (tr, 0) if len(halves) == 2 else (0, tr)
+                moves.append(
+                    (
+                        len(pieces) + which,
+                        (index, xr, section),
+                        section,
+                        spot(xr, dz, tr, 0, XPART),
+                    )
+                )
+    pieces.extend(halves)
 
 
 def gather_weights(dec_weight, enc_weight, core):
@@ -106,59 +132,55 @@
     ring = jnp.stack(
         [jnp.stack([part_x, a]), jnp.stack([jnp.concatenate([da, db], axis=0), b])]
     )
-    near = jnp.stack([part_z, d1, d2, u2, u1])
-    near_a, near_b, w1, v1, u3, d3 = fenced(
-        swap_a(near),
-        swap_b(near),
+    near = [jnp.stack([t[s] for t in (part_z, d1, d2, u2, u1)]) for s in range(2)]
+    w1, v1, near_a1, near_b0, u3, d3, near_a0, near_b1 = fenced(
         z_shift(ring, 1),
         z_shift(ring, -1),
+        swap_a(near[1]),
+        swap_b(near[0]),
         z_shift(u2, 1),
         z_shift(d2, -1),
-    )
-    near_da, near_db, w2, v2, u4, d4 = fenced(
-        swap_a(near_b[:, :1]),
-        swap_b(near_a[:, 1:]),
+        swap_a(near[0]),
+        swap_b(near[1]),
+    )
+    w2, v2, near_d0, near_d1, u4, d4 = fenced(
         z_shift(w1, 1),
         z_shift(v1, -1),
+        swap_a(near_b0),
+        swap_b(near_a1),
         z_shift(u3[:1], 1),
         z_shift(d3[1:], -1),
     )
-    far = jnp.stack([d3, jnp.concatenate([u4, d4], axis=0), u3])
-    far_a, far_b, w3, v3 = fenced(
-        swap_a(far), swap_b(far), z_shift(w2, 1), z_shift(v2, -1)
-    )
-    far_da, far_db, w4, v4 = (
-        swap_a(far_b[:, :1]),
-        swap_b(far_a[:, 1:]),
-        z_shift(w3[:1], 1),
-        z_shift(v3[1:], -1),
-    )
+    far = [jnp.stack([d3[0], u4[0], u3[0]]), jnp.stack([d3[1], d4[0], u3[1]])]
+    w3, v3, far_a1, far_b0, far_a0, far_b1 = fenced(
+        z_shift(w2, 1),
+        z_shift(v2, -1),
+        swap_a(far[1]),
+        swap_b(far[0]),
+        swap_a(far[0]),
+        swap_b(far[1]),
+    )
+    w4, v4 = z_shift(w3[:1], 1), z_shift(v3[1:], -1)
+    far_d0, far_d1 = swap_a(far_b0), swap_b(far_a1)
 
     pieces, moves = [], []
-    for group, own_part, to_a, to_b, half_a, half_b in (
-        (NEAR, near, near_a, near_b, near_da, near_db),
-        (FAR, far, far_a, far_b, far_da, far_db),
-    ):
-        for k, dz in enumerate(group):
-            for section in range(2):
-                for n, (tr, xr) in enumerate(((0, 0), (0, 1), (1, 1))):
-                    moves.append(
-                        (len(pieces) + n, (k, section), section, spot(xr, dz, tr, XPART, SPAN))
-                    )
-                moves.append(
-                    (len(pieces) + 3 + section, (k, 0), section, spot(0, dz, 1, XPART, SPAN))
-                )
-        pieces += [own_part, to_a, to_b, half_a, half_b]
-    rings = {0: ring, 1: v1, 2: v2, 3: v3, 5: w3, 6: w2, 7: w1}
-    for dz in range(Z):
-        for section in range(2):
-            for tr in range(2):
-                for xr in range(2):
-                    which, index = (len(pieces) + tr, 0) if dz == 4 else (len(pieces), tr)
-                    moves.append(
-                        (which, (index, xr, section), section, spot(xr, dz, tr, 0, XPART))
-                    )
-        pieces += [w4, v4] if dz == 4 else [rings[dz]]
+    narrow_moves(
+        NEAR,
+        ((near[0], near_a0, near_b0, near_d0), (near[1], near_a1, near_b1, near_d1)),
+        pieces,
+        moves,
+    )
+    for dz, piece in ((0, ring), (1, v1), (7, w1), (2, v2), (6, w2)):
+        ring_moves(dz, [piece], pieces, moves)
+    narrow_moves(
+        FAR,
+        ((far[0], far_a0, far_b0, far_d0), (far[1], far_a1, far_b1, far_d1)),
+        pieces,
+        moves,
+    )
+    ring_moves(3, [v3], pieces, moves)
+    ring_moves(5, [w3], pieces, moves)
+    ring_moves(4, [w4, v4], pieces, moves)
     return place(pieces, moves)
 
 
@@ -180,27 +202,33 @@
     return lax.optimization_barrier((tuple(results), tuple(others)))[0]
 
 
-def reduce_weights(ring, near, far, extra):
-    z_res = (z_shift(ring[4, :1], 1), z_shift(ring[4, 1:], -1))
-    x_res = (swap_a(far[1, 0, :, :1]), swap_b(far[1, 0, :, 1:]))
-    w, v = z_res
-    z_send = (add_low(ring[3], w, 0), add_high(ring[5], v, 0))
+def reduce_weights(ring, near, far, corners, code_exchange):
+    (ring_40, near_0, far_0), (ring_41, near_1, far_1) = corners
+    ring = {dz: ring[k] for k, dz in enumerate(RING)}
+    z_res = (z_shift(ring_40, 1), z_shift(ring_41, -1))
+    x_res = (swap_a(far_0[0]), swap_b(far_1[0]))
+    z_send = (add_low(ring[3], z_res[0][:, :, None], 2), add_high(ring[5], z_res[1][:, :, None], 2))
     x_res = couple(x_res, z_send)
-    x_send = (add_high(far[0, 1], x_res[1], 1), add_low(far[1, 1], x_res[0], 1))
+    x_send = (
+        add_high(far[0, 1], x_res[1][:, None], 1),
+        add_low(far[1, 1], x_res[0][:, None], 1),
+    )
     z_res = couple((z_shift(z_send[0], 1), z_shift(z_send[1], -1)), x_send)
     x_res = (swap_a(x_send[0]), swap_b(x_send[1]))
     z_send = (add(ring[2], z_res[0]).astype(bf16), add(ring[6], z_res[1]).astype(bf16))
-    x_res = couple(x_res, z_send + tuple(extra))
+    x_res = couple(x_res, z_send)
     far_sum = add(far[0, 0], *x_res).astype(bf16)
-    x_send = (near[1, 0, :, :1], near[1, 0, :, 1:])
-    x_send = couple(x_send, (far_sum,))
+    x_send = couple((near_0[0], near_1[0]), (far_sum,))
     z_res = couple((z_shift(z_send[0], 1), z_shift(z_send[1], -1)), x_send)
     n_res = (z_shift(far_sum[1, :1], 1), z_shift(far_sum[1, 1:], -1))
     x_res = (swap_a(x_send[0]), swap_b(x_send[1]))
     z_send = (add(ring[1], z_res[0]).astype(bf16), add(ring[7], z_res[1]).astype(bf16))
     n_send = (add_low(far_sum[0], n_res[0], 0), add_high(far_sum[2], n_res[1], 0))
     x_res = couple(x_res, z_send + n_send)
-    x_send = (add_high(near[0, 1], x_res[1], 1), add_low(near[1, 1], x_res[0], 1))
+    x_send = (
+        add_high(near[0, 1], x_res[1][:, None], 1),
+        add_low(near[1, 1], x_res[0][:, None], 1),
+    )
     z_res = couple((z_shift(z_send[0], 1), z_shift(z_send[1], -1)), x_send)
     n_res = couple((z_shift(n_send[0], 1), z_shift(n_send[1], -1)), x_send)
     x_res = (swap_a(x_send[0]), swap_b(x_send[1]))
@@ -210,13 +238,15 @@
     n_send = (add(near_sum[2], n_res[0]).astype(bf16), add(near_sum[3], n_res[1]).astype(bf16))
     n_res = (z_shift(n_send[0], 1), z_shift(n_send[1], -1))
     x_res = (swap_a(ring_sum[1, 0, :1]), swap_b(ring_sum[1, 0, 1:]))
+    got = code_exchange(n_send)
     x_send = (add_high(ring_sum[0, 1], x_res[1], 0), add_low(ring_sum[1, 1], x_res[0], 0))
     n_res = couple(n_res, x_send)
     n_send = (add(near_sum[1], n_res[0]).astype(bf16), add(near_sum[4], n_res[1]).astype(bf16))
     x_res = (swap_a(x_send[0]), swap_b(x_send[1]))
     n_res = (z_shift(n_send[0], 1), z_shift(n_send[1], -1))
-    return jnp.concatenate(
-        [add(ring_sum[0, 0], *x_res), add(near_sum[0], *n_res)], axis=-1
+    return (
+        jnp.concatenate([add(ring_sum[0, 0], *x_res), add(near_sum[0], *n_res)], axis=-1),
+        got,
     )
 
 
@@ -287,7 +317,7 @@
     return pl.pallas_call(
         functools.partial(forward_kernel, len(terms), keep),
         out_shape=out_shape,
-        compiler_params=pltpu.CompilerParams(vmem_limit_bytes=24 * MIB),
+        compiler_params=pltpu.CompilerParams(vmem_limit_bytes=16 * MIB),
         cost_estimate=section_cost(rows),
     )(*terms, weights)
 
@@ -326,7 +356,7 @@
     return pl.pallas_call(
         functools.partial(backward_kernel, len(terms), keep),
         out_shape=out_shape,
-        compiler_params=pltpu.CompilerParams(vmem_limit_bytes=24 * MIB),
+        compiler_params=pltpu.CompilerParams(vmem_limit_bytes=16 * MIB),
         cost_estimate=section_cost(rows),
     )(*terms, slope, weights)
 
@@ -348,23 +378,26 @@
         code_ref[...].astype(f32) + (left_ref[...].astype(f32) + right_ref[...].astype(f32))
     ).astype(bf16)
     head = head_ref[...].astype(f32)
-    scores = jnp.sum(codes.astype(f32) * head, axis=-1, keepdims=True)
-    rows = scores.shape[0]
+    all_scores = jnp.sum(codes.astype(f32) * head, axis=-1, keepdims=True)
+    flag = jnp.full((1, 1), flag_ref[0], jnp.int32).astype(f32)
+    rows = all_scores.shape[0] // MICROS
     seq_len = rows // 2
-    position = lax.broadcasted_iota(jnp.int32, (rows, 1), 0)
-    chosen_length, other_length = lengths_ref[0], lengths_ref[1]
-    chosen = jnp.where(position < seq_len, 1.0, 0.0)
-    limit = jnp.where(position < seq_len, chosen_length, other_length + seq_len)
-    valid = jnp.where(position < limit, 1.0, 0.0)
-    chosen_count = jnp.full((1, 1), chosen_length, jnp.int32).astype(f32)
-    other_count = jnp.full((1, 1), other_length, jnp.int32).astype(f32)
-    chosen_sum = jnp.sum(scores * valid * chosen, axis=0, keepdims=True)
-    other_sum = jnp.sum(scores * valid * (1.0 - chosen), axis=0, keepdims=True)
-    gap = other_sum / other_count - chosen_sum / chosen_count
-    weight = loss_scale * jax.nn.sigmoid(gap)
-    token = (1.0 - chosen) * (weight / other_count) - chosen * (weight / chosen_count)
-    token = token * valid * jnp.full((1, 1), flag_ref[0], jnp.int32).astype(f32)
-    out_ref[...] = (token * head).astype(bf16)
+    for micro in range(MICROS):
+        scores = all_scores[micro * rows : (micro + 1) * rows]
+        position = lax.broadcasted_iota(jnp.int32, (rows, 1), 0)
+        chosen_length, other_length = lengths_ref[micro, 0], lengths_ref[micro, 1]
+        chosen = jnp.where(position < seq_len, 1.0, 0.0)
+        limit = jnp.where(position < seq_len, chosen_length, other_length + seq_len)
+        valid = jnp.where(position < limit, 1.0, 0.0)
+        chosen_count = jnp.full((1, 1), chosen_length, jnp.int32).astype(f32)
+        other_count = jnp.full((1, 1), other_length, jnp.int32).astype(f32)
+        chosen_sum = jnp.sum(scores * valid * chosen, axis=0, keepdims=True)
+        other_sum = jnp.sum(scores * valid * (1.0 - chosen), axis=0, keepdims=True)
+        gap = other_sum / other_count - chosen_sum / chosen_count
+        weight = loss_scale * jax.nn.sigmoid(gap)
+        token = (1.0 - chosen) * (weight / other_count) - chosen * (weight / chosen_count)
+        token = token * valid * flag
+        out_ref[micro * rows : (micro + 1) * rows, :] = (token * head).astype(bf16)
 
 
 def reward_seed(flag, lengths, codes, left, right, head):
@@ -381,7 +414,7 @@
 def weight_grad_kernel(*refs):
     grads, codes = refs[0:CHUNKS], refs[CHUNKS : 2 * CHUNKS]
     gated, hidden = refs[2 * CHUNKS : 3 * CHUNKS], refs[3 * CHUNKS : 4 * CHUNKS]
-    ring_ref, near_ref, far_ref = refs[-3:]
+    ring_ref, near_ref, far_ref, ring_4, near_corner, far_corner = refs[-6:]
 
     def joined(group):
         return jnp.concatenate([ref[...] for ref in group], axis=0)
@@ -396,12 +429,20 @@
                 for dz in range(Z):
                     row = (xr * Z + dz) * SUB
                     piece = result[row : row + SUB]
-                    if low == 0:
-                        ring_ref[dz, 0, xr, 0, mat] = piece
+                    if low == 0 and dz == 4:
+                        ring_4[0, xr, mat] = piece
+                    elif low == 0:
+                        ring_ref[RING.index(dz), 0, xr, 0, mat] = piece
                     elif dz in NEAR:
-                        near_ref[0, xr, NEAR.index(dz), 0, mat] = piece
+                        k = NEAR.index(dz)
+                        near_ref[0, xr, k, 0, mat] = piece
+                        if xr == 0:
+                            near_corner[0, k, mat] = piece
                     else:
-                        far_ref[0, xr, FAR.index(dz), 0, mat] = piece
+                        k = FAR.index(dz)
+                        far_ref[0, xr, k, 0, mat] = piece
+                        if xr == 0:
+                            far_corner[0, k, mat] = piece
 
 
 def weight_grads(section, grads, codes, gated, hidden, held):
@@ -414,6 +455,9 @@
         return pl.BlockSpec(
             (1, 2, count, 1, 2, SUB, ZPART), lambda t: (t, 0, 0, section, 0, 0, 0)
         )
+
+    def corner_spec(count):
+        return pl.BlockSpec((1, count, 2, SUB, ZPART), lambda t: (0, 0, 0, 0, 0))
 
     return pl.pallas_call(
         weight_grad_kernel,
@@ -422,17 +466,25 @@
         + [wide] * (2 * CHUNKS)
         + [pl.BlockSpec(memory_space=pl.ANY)] * len(held),
         out_specs=[
-            pl.BlockSpec((Z, 1, 2, 1, 2, SUB, XPART), lambda t: (0, t, 0, section, 0, 0, 0)),
+            pl.BlockSpec(
+                (len(RING), 1, 2, 1, 2, SUB, XPART), lambda t: (0, t, 0, section, 0, 0, 0)
+            ),
             group_spec(len(NEAR)),
             group_spec(len(FAR)),
+            pl.BlockSpec((1, 2, 2, SUB, XPART), lambda t: (t, 0, 0, 0, 0)),
+            corner_spec(len(NEAR)),
+            corner_spec(len(FAR)),
         ],
         out_shape=[
-            jax.ShapeDtypeStruct((Z, 2, 2, 2, 2, SUB, XPART), bf16),
+            jax.ShapeDtypeStruct((len(RING), 2, 2, 2, 2, SUB, XPART), bf16),
             jax.ShapeDtypeStruct((2, 2, len(NEAR), 2, 2, SUB, ZPART), bf16),
             jax.ShapeDtypeStruct((2, 2, len(FAR), 2, 2, SUB, ZPART), bf16),
+            jax.ShapeDtypeStruct((2, 2, 2, SUB, XPART), bf16),
+            jax.ShapeDtypeStruct((1, len(NEAR), 2, SUB, ZPART), bf16),
+            jax.ShapeDtypeStruct((1, len(FAR), 2, SUB, ZPART), bf16),
         ],
         input_output_aliases={n_in + k: k for k in range(len(held))},
-        compiler_params=pltpu.CompilerParams(vmem_limit_bytes=40 * MIB),
+        compiler_params=pltpu.CompilerParams(vmem_limit_bytes=30 * MIB),
         cost_estimate=pl.CostEstimate(
             flops=8 * rows * CHUNKS * WIDTH * COLS // 2,
             bytes_accessed=4 * WIDTH * COLS,
@@ -463,9 +515,10 @@
 
     weights = gather_weights(dec_weight, enc_weight, core)
 
-    codes_in = lax.dynamic_slice_in_dim(codes_in, tensor * CHUNKS, CHUNKS, 0)
-    lengths = lax.dynamic_slice_in_dim(lengths, tensor * CHUNKS, CHUNKS, 0)
-    codes_in = to_local(codes_in, pair, z_index)
+    codes_in = lax.dynamic_slice_in_dim(codes_in, tensor * MICROS, MICROS, 0)
+    lengths = lax.dynamic_slice_in_dim(lengths, tensor * MICROS, MICROS, 0)
+    lengths = lengths.reshape(CHUNKS, MICROS // CHUNKS, 2)
+    codes_in = to_local(codes_in, pair, z_index).reshape(CHUNKS, -1, WIDTH)
     codes_in = jnp.where(stage == 0, codes_in, jnp.zeros_like(codes_in))
     head = to_local(head[None], pair, z_index)
     is_last = (stage == STAGES - 1).astype(jnp.int32)[None]
@@ -515,9 +568,9 @@
             else:
                 received[m] = y_shift(passed, -1)
 
-    held = ()
+    held, corners = (), [None, None]
     for section in (1, 0):
-        held = weight_grads(
+        made = weight_grads(
             section,
             grads[section],
             [codes[m][section] for m in chunks],
@@ -525,14 +578,19 @@
             hidden[section],
             held,
         )
+        held, corners[section] = made[:3], made[3:]
 
     code_grads = jnp.where(core == 0, jnp.stack(through[0]), jnp.stack(through[1]))
-    code_grads = to_global(code_grads, pair, z_index)
-    share = rows // 2
+    code_grads = to_global(code_grads.reshape(MICROS, -1, WIDTH), pair, z_index)
+    share = code_grads.shape[1] // 2
     kept = lax.dynamic_slice_in_dim(code_grads, tensor * share, share, 1)
-    sent = lax.dynamic_slice_in_dim(code_grads, (1 - tensor) * share, share, 1)
-    got = lax.ppermute(sent.astype(bf16), "tensor", [(0, 1), (1, 0)])
-    summed = reduce_weights(*held, (got,))
+    sent = lax.dynamic_slice_in_dim(code_grads, (1 - tensor) * share, share, 1).astype(bf16)
+
+    def code_exchange(others):
+        (late,) = couple((sent,), others)
+        return lax.ppermute(late, "tensor", [(0, 1), (1, 0)])
+
+    summed, got = reduce_weights(*held, corners, code_exchange)
     got = got.astype(f32)
     code_out = jnp.where(
         tensor == 0, jnp.concatenate([kept, got], axis=0), jnp.concatenate([got, kept], axis=0)

time: 544 us -> 527 us (0.969)
  waiting for transfers between devices: 161 us -> 219 us
  Pallas kernels: 116 us -> 68.4 us
  local copies, waits for them, and re-layouts: 94.4 us -> 80.2 us
  starting transfers between devices: 144 us -> 131 us
    ppermute x12 -> x6, waiting for transfers between devices: 5.4 us -> 41.9 us  [y_shift(): lax.ppermute(value, 'pipe', [(i, i + 2 * steps) for i in range(8) if 0 <=...]
    pallas_call x16 -> x8, Pallas kernels: 39.3 us -> 19.5 us  [section_backward(): pl.pallas_call(functools.partial(backward_kernel, len(terms), keep), out_...]
    ppermute x34 -> x18, waiting for transfers between devices: 1.55 us -> 16.4 us  [core_swap(): return lax.ppermute(value, 'pipe', [(i, i ^ 1) for i in range(8)])]
    pallas_call x16 -> x8, Pallas kernels: 39.1 us -> 24.3 us  [section_forward(): pl.pallas_call(functools.partial(forward_kernel, len(terms), keep), out_s...]
    ppermute x12 -> x6, starting transfers between devices: 28.3 us -> 15.5 us  [y_shift(): lax.ppermute(value, 'pipe', [(i, i + 2 * steps) for i in range(8) if 0 <=...]
    ppermute x12 -> x14, waiting for transfers between devices: 8.53 us -> 17.9 us  [swap_a(): lax.ppermute(value, 'dp', [(x * Z + z, (1 - x) * Z + z) for x in range(2)...]
    pallas_call x8 -> x4, Pallas kernels: 15.4 us -> 8.7 us  [norm_grad(): pl.pallas_call(norm_grad_kernel, out_shape=jax.ShapeDtypeStruct(grad.shap...]
    ppermute x32, waiting for transfers between devices: 121 us -> 115 us  [z_shift(): lax.ppermute(value, 'dp', [(x * Z + z, x * Z + (z + steps) % Z) for x in...]
  transfers between devices with their start and end apart: 103 -> 85, of which waited for: 32 -> 49; matrix products, arithmetic and copies ran while one was open for 6% -> 4% of each run, Pallas kernels for 20% -> 2%
where the time goes in v4:
time: 527 us; the launch traced here: 517 us
  waiting for transfers between devices  219 us (42%)
  starting transfers between devices  131 us (25%)
  local copies, waits for them, and re-layouts  80.2 us (15%)
  Pallas kernels  68.4 us (13%)
  other arithmetic  16.9 us (3%)
    ppermute x32, waiting for transfers between devices, z_shift(): lax.ppermute(value, 'dp', [(x * Z + z, x * Z + (z + steps) % Z) for x in...  115 us
    unnamed x165, local copies, waits for them, and re-layouts  73.5 us
    ppermute x18, starting transfers between devices, core_swap(): return lax.ppermute(value, 'pipe', [(i, i ^ 1) for i in range(8)])  46.5 us
    ppermute x6, waiting for transfers between devices, y_shift(): lax.ppermute(value, 'pipe', [(i, i + 2 * steps) for i in range(8) if 0 <=...  41.9 us
    ppermute x32, starting transfers between devices, z_shift(): lax.ppermute(value, 'dp', [(x * Z + z, x * Z + (z + steps) % Z) for x in...  36.8 us
    pallas_call x8, Pallas kernels, section_forward(): pl.pallas_call(functools.partial(forward_kernel, len(terms), keep), out_s...  24.3 us
    ppermute x14, starting transfers between devices, swap_b(): return lax.ppermute(value, ('dp', 'tensor'), pairs)  23.6 us
    ppermute x14, waiting for transfers between devices, swap_b(): return lax.ppermute(value, ('dp', 'tensor'), pairs)  20 us
  transfers between devices with their start and end apart: 85, of which 49 were waited for; matrix products, arithmetic and copies ran while one was open for 4% of the time, Pallas kernels for 2%

profile of v4, /device:TPU:1, one launch (start us, length us, event | category | flops | bytes accessed | tf_op | source)
XLA Modules:
  0.0 517.1 jit_solution(7148103219964298812)
XLA Ops:
  15.5 4.9 collective-permute-done.3
  41.1 6.6 %collective-permute-done.16.refs_6_ = bf16[5,2,32,1152]{3,2,1,0:T(8,128)(2,1)S(1)} collective-permute-done((bf16[5,2,32,1152]{3,2,1,0:T(8,128)(2,1)S(1)}, bf16[5,2,32,1152]{3,2,1,0:T(8,128)(2,1)S(1)}, u32[]{:S(2)}, u32[]{:S(2)}) %collective-permute-start.16) | collective-permute-done | bytes 737312 | tf_op jit(solution)/shard_map/ppermute | solution.py:59
  49.7 14.7 %collective-permute-done.15.refs_1_ = bf16[5,2,32,1152]{3,2,1,0:T(8,128)(2,1)S(1)} collective-permute-done((bf16[5,2,32,1152]{3,2,1,0:T(8,128)(2,1)S(1)}, bf16[5,2,32,1152]{3,2,1,0:T(8,128)(2,1)S(1)}, u32[]{:S(2)}, u32[]{:S(2)}) %collective-permute-start.15) | collective-permute-done | bytes 737312 | tf_op jit(solution)/shard_map/ppermute | solution.py:49
  73.0 11.3 %collective-permute-done.21 = bf16[1,2,32,1152]{3,2,1,0:T(8,128)(2,1)S(1)} collective-permute-done((bf16[1,2,32,1152]{3,2,1,0:T(8,128)(2,1)S(1)}, bf16[1,2,32,1152]{3,2,1,0:T(8,128)(2,1)S(1)}, u32[]{:S(2)}, u32[]{:S(2)}) %collective-permute-start.21) | collective-permute-done | bytes 147488 | tf_op jit(solution)/shard_map/ppermute | solution.py:43
  85.7 4.2 collective-permute-done.22
  124.9 5.8 %collective-permute-done.31.refs_23_ = bf16[1,2,2,2,32,896]{5,4,3,2,1,0:T(8,128)(2,1)} collective-permute-done((bf16[1,2,2,2,32,896]{5,4,3,2,1,0:T(8,128)(2,1)}, bf16[1,2,2,2,32,896]{5,4,3,2,1,0:T(8,128)(2,1)}, u32[]{:S(2)}, u32[]{:S(2)}) %collective-permute-start.31) | collective-permute-done | bytes 458784 | tf_op jit(solution)/shard_map/ppermute | solution.py:43
  144.3 5.7 %shard_map.76 = (bf16[2,512,4096]{2,1,0:T(8,128)(2,1)S(1)}, bf16[2,512,4096]{2,1,0:T(8,128)(2,1)S(1)}) custom-call(bf16[5,2,32,1152]{3,2,1,0:T(8,128)(2,1)S(1)} %copy-done.33, bf16[5,2,32,1152]{3,2,1,0:T(8,128)(2,1)S(1)} %copy-done.44, bf16[5,2,32,1152]{3,2,1,0:T(8,128)(2,1)S(1)} %copy-done.46, bf16[5,2,32,1152]{3,2,1,0:T(8,128)(2,1)S(1)} %copy-done.48, ...), custom_call_target="tpu_custom_call" | custom-call | tf_op jit(solution)/shard_map/pallas_call | solution.py:81
  152.9 21.2 %collective-permute-start.33 = (bf16[256,512]{1,0:T(8,128)(2,1)S(1)}, bf16[256,512]{1,0:T(8,128)(2,1)S(1)}, u32[]{:S(2)}, u32[]{:S(2)}) collective-permute-start(bf16[256,512]{1,0:T(8,128)(2,1)S(1)} %get-tuple-element.135.refs_1_), channel_id=1, source_target_pairs={{0,32},{32,0},{64,96},{96,64},{128,160},{160,128},{192,224},{224,1... | collective-permute-start | bytes 786440 | tf_op jit(solution)/shard_map/ppermute | solution.py:33
  183.0 5.3 %collective-permute-done.35.refs_0_ = bf16[256,512]{1,0:T(8,128)(2,1)S(1)} collective-permute-done((bf16[256,512]{1,0:T(8,128)(2,1)S(1)}, bf16[256,512]{1,0:T(8,128)(2,1)S(1)}, u32[]{:S(2)}, u32[]{:S(2)}) %collective-permute-start.35) | collective-permute-done | bytes 262176 | tf_op jit(solution)/shard_map/ppermute | solution.py:37
  202.7 5.3 %collective-permute-done.38.refs_0_ = bf16[256,512]{1,0:T(8,128)(2,1)S(1)} collective-permute-done((bf16[256,512]{1,0:T(8,128)(2,1)S(1)}, bf16[256,512]{1,0:T(8,128)(2,1)S(1)}, u32[]{:S(2)}, u32[]{:S(2)}) %collective-permute-start.38) | collective-permute-done | bytes 262176 | tf_op jit(solution)/shard_map/ppermute | solution.py:37
  217.9 4.3 collective-permute-start.41
  222.2 5.1 collective-permute-done.41.refs_0_
  271.6 9.5 %collective-permute-done.46.refs_0_ = bf16[256,512]{1,0:T(8,128)(2,1)S(1)} collective-permute-done((bf16[256,512]{1,0:T(8,128)(2,1)}, bf16[256,512]{1,0:T(8,128)(2,1)S(1)}, u32[]{:S(2)}, u32[]{:S(2)}) %collective-permute-start.46) | collective-permute-done | bytes 262176 | tf_op jit(solution)/shard_map/ppermute | solution.py:37
  302.7 8.3 %collective-permute-done.49.refs_0_ = bf16[256,512]{1,0:T(8,128)(2,1)S(1)} collective-permute-done((bf16[256,512]{1,0:T(8,128)(2,1)}, bf16[256,512]{1,0:T(8,128)(2,1)S(1)}, u32[]{:S(2)}, u32[]{:S(2)}) %collective-permute-start.49) | collective-permute-done | bytes 262176 | tf_op jit(solution)/shard_map/ppermute | solution.py:37
  333.6 8.3 %collective-permute-done.52.refs_0_ = bf16[256,512]{1,0:T(8,128)(2,1)S(1)} collective-permute-done((bf16[256,512]{1,0:T(8,128)(2,1)}, bf16[256,512]{1,0:T(8,128)(2,1)S(1)}, u32[]{:S(2)}, u32[]{:S(2)}) %collective-permute-start.52) | collective-permute-done | bytes 262176 | tf_op jit(solution)/shard_map/ppermute | solution.py:37
  373.4 9.2 %collective-permute-done.57 = bf16[2,2,2,32,896]{4,3,2,1,0:T(8,128)(2,1)S(1)} collective-permute-done((bf16[2,2,2,32,896]{4,3,2,1,0:T(8,128)(2,1)S(1)}, bf16[2,2,2,32,896]{4,3,2,1,0:T(8,128)(2,1)S(1)}, u32[]{:S(2)}, u32[]{:S(2)}) %collective-permute-start.57) | collective-permute-done | bytes 458784 | tf_op jit(solution)/shard_map/ppermute | solution.py:43
  388.0 4.2 collective-permute-done.62
  392.2 12.3 %collective-permute-done.61 = bf16[2,2,2,2,32,896]{5,4,3,2,1,0:T(8,128)(2,1)S(1)} collective-permute-done((bf16[2,2,2,2,32,896]{5,4,3,2,1,0:T(8,128)(2,1)S(1)}, bf16[2,2,2,2,32,896]{5,4,3,2,1,0:T(8,128)(2,1)S(1)}, u32[]{:S(2)}, u32[]{:S(2)}) %collective-permute-start.61) | collective-permute-done | bytes 917536 | tf_op jit(solution)/shard_map/ppermute | solution.py:43
  414.7 15.9 %collective-permute-done.66 = bf16[2,2,2,2,32,896]{5,4,3,2,1,0:T(8,128)(2,1)S(1)} collective-permute-done((bf16[2,2,2,2,32,896]{5,4,3,2,1,0:T(8,128)(2,1)S(1)}, bf16[2,2,2,2,32,896]{5,4,3,2,1,0:T(8,128)(2,1)S(1)}, u32[]{:S(2)}, u32[]{:S(2)}) %collective-permute-start.66) | collective-permute-done | bytes 917536 | tf_op jit(solution)/shard_map/ppermute | solution.py:43
  443.0 20.8 %collective-permute-done.73 = bf16[2,2,32,1152]{3,2,1,0:T(8,128)(2,1)S(1)} collective-permute-done((bf16[2,2,32,1152]{3,2,1,0:T(8,128)(2,1)}, bf16[2,2,32,1152]{3,2,1,0:T(8,128)(2,1)S(1)}, u32[]{:S(2)}, u32[]{:S(2)}) %collective-permute-start.73) | collective-permute-done | bytes 294944 | tf_op jit(solution)/shard_map/ppermute | solution.py:43
  465.1 4.8 collective-permute-done.74
  488.4 7.0 %collective-permute-done.82 = bf16[2,2,32,1152]{3,2,1,0:T(8,128)(2,1)S(1)} collective-permute-done((bf16[2,2,32,1152]{3,2,1,0:T(8,128)(2,1)S(1)}, bf16[2,2,32,1152]{3,2,1,0:T(8,128)(2,1)S(1)}, u32[]{:S(2)}, u32[]{:S(2)}) %collective-permute-start.82) | collective-permute-done | bytes 294944 | tf_op jit(solution)/shard_map/ppermute | solution.py:43
  495.6 9.0 %collective-permute-start.84 = (f32[2,32,2048]{2,1,0:T(8,128)S(1)}, f32[2,32,2048]{2,1,0:T(8,128)S(1)}, u32[]{:S(2)}, u32[]{:S(2)}) collective-permute-start(f32[2,32,2048]{2,1,0:T(8,128)S(1)} %get-tuple-element.227), channel_id=1, source_target_pairs={{0,32},{32,0},{64,96},{96,64},{128,160},{160,128},{192,224},{224,1... | collective-permute-start | bytes 1572872 | tf_op jit(solution)/shard_map/ppermute | solution.py:33
  506.7 7.5 %collective-permute-done.75 = bf16[2,64,512]{1,2,0:T(8,128)(2,1)S(1)} collective-permute-done((bf16[2,64,512]{1,2,0:T(8,128)(2,1)S(1)}, bf16[2,64,512]{1,2,0:T(8,128)(2,1)S(1)}, u32[]{:S(2)}, u32[]{:S(2)}) %collective-permute-start.75) | collective-permute-done | bytes 131104 | tf_op jit(solution)/shard_map/ppermute | solution.py:591
  (419 shorter events, 303.6 us)
Async XLA Ops:
  35.2 30.1 %collective-permute-start.10 = (bf16[2,2,2,2,32,896]{5,4,3,2,1,0:T(8,128)(2,1)S(1)}, bf16[2,2,2,2,32,896]{5,4,3,2,1,0:T(8,128)(2,1)S(1)}, u32[]{:S(2)}, u32[]{:S(2)}) collective-permute-start(bf16[2,2,2,2,32,896]{5,4,3,2,1,0:T(8,128)(2,1)S(1)} %pad_maximum_fusion.2.refs_8_), channel_id=1, source_target_pairs={{0,14},{2,0},{4,2},{6,4},{8,6},{10,8},{12,10},{14,12},{16,30},{18,... | collective-permute-start | bytes 2752520 | tf_op jit(solution)/shard_map/ppermute | solution.py:43
  37.0 28.3 %collective-permute-start.9 = (bf16[2,2,2,2,32,896]{5,4,3,2,1,0:T(8,128)(2,1)S(1)}, bf16[2,2,2,2,32,896]{5,4,3,2,1,0:T(8,128)(2,1)S(1)}, u32[]{:S(2)}, u32[]{:S(2)}) collective-permute-start(bf16[2,2,2,2,32,896]{5,4,3,2,1,0:T(8,128)(2,1)S(1)} %pad_maximum_fusion.2.refs_8_), channel_id=1, source_target_pairs={{0,2},{2,4},{4,6},{6,8},{8,10},{10,12},{12,14},{14,0},{16,18},{18,... | collective-permute-start | bytes 2752520 | tf_op jit(solution)/shard_map/ppermute | solution.py:43
  41.1 23.3 %collective-permute-start.15 = (bf16[5,2,32,1152]{3,2,1,0:T(8,128)(2,1)S(1)}, bf16[5,2,32,1152]{3,2,1,0:T(8,128)(2,1)S(1)}, u32[]{:S(2)}, u32[]{:S(2)}) collective-permute-start(bf16[5,2,32,1152]{3,2,1,0:T(8,128)(2,1)S(1)} %get-tuple-element.247.refs_0_), channel_id=1, source_target_pairs={{0,16},{2,18},{4,20},{6,22},{8,24},{10,26},{12,28},{14,30},{16,0},... | collective-permute-start | bytes 2211848 | tf_op jit(solution)/shard_map/ppermute | solution.py:49
  65.3 24.5 %collective-permute-start.19 = (bf16[5,2,32,1152]{3,2,1,0:T(8,128)(2,1)S(1)}, bf16[5,2,32,1152]{3,2,1,0:T(8,128)(2,1)S(1)}, u32[]{:S(2)}, u32[]{:S(2)}) collective-permute-start(bf16[5,2,32,1152]{3,2,1,0:T(8,128)(2,1)S(1)} %collective-permute-done.12.refs_2_), channel_id=1, source_target_pairs={{0,16},{2,18},{4,20},{6,22},{8,24},{10,26},{12,28},{14,30},{16,0},... | collective-permute-start | bytes 2211848 | tf_op jit(solution)/shard_map/ppermute | solution.py:49
  67.8 22.9 %collective-permute-start.20 = (bf16[5,2,32,1152]{3,2,1,0:T(8,128)(2,1)S(1)}, bf16[5,2,32,1152]{3,2,1,0:T(8,128)(2,1)S(1)}, u32[]{:S(2)}, u32[]{:S(2)}) collective-permute-start(bf16[5,2,32,1152]{3,2,1,0:T(8,128)(2,1)S(1)} %collective-permute-done.11.refs_5_), channel_id=1, source_target_pairs={{0,17},{1,16},{2,19},{3,18},{4,21},{5,20},{6,23},{7,22},{8,25},{9,... | collective-permute-start | bytes 2211848 | tf_op jit(solution)/shard_map/ppermute | solution.py:59
  69.2 22.5 %collective-permute-start.17 = (bf16[2,2,2,2,32,896]{5,4,3,2,1,0:T(8,128)(2,1)S(1)}, bf16[2,2,2,2,32,896]{5,4,3,2,1,0:T(8,128)(2,1)}, u32[]{:S(2)}, u32[]{:S(2)}) collective-permute-start(bf16[2,2,2,2,32,896]{5,4,3,2,1,0:T(8,128)(2,1)S(1)} %collective-permute-done.9.refs_10_), channel_id=1, source_target_pairs={{0,2},{2,4},{4,6},{6,8},{8,10},{10,12},{12,14},{14,0},{16,18},{18,... | collective-permute-start | bytes 2752520 | tf_op jit(solution)/shard_map/ppermute | solution.py:43
  70.2 21.6 %collective-permute-start.18 = (bf16[2,2,2,2,32,896]{5,4,3,2,1,0:T(8,128)(2,1)S(1)}, bf16[2,2,2,2,32,896]{5,4,3,2,1,0:T(8,128)(2,1)}, u32[]{:S(2)}, u32[]{:S(2)}) collective-permute-start(bf16[2,2,2,2,32,896]{5,4,3,2,1,0:T(8,128)(2,1)S(1)} %collective-permute-done.10.refs_9_), channel_id=1, source_target_pairs={{0,14},{2,0},{4,2},{6,4},{8,6},{10,8},{12,10},{14,12},{16,30},{18,... | collective-permute-start | bytes 2752520 | tf_op jit(solution)/shard_map/ppermute | solution.py:43
  91.7 20.5 %collective-permute-start.24 = (bf16[2,2,2,2,32,896]{5,4,3,2,1,0:T(8,128)(2,1)}, bf16[2,2,2,2,32,896]{5,4,3,2,1,0:T(8,128)(2,1)S(1)}, u32[]{:S(2)}, u32[]{:S(2)}) collective-permute-start(bf16[2,2,2,2,32,896]{5,4,3,2,1,0:T(8,128)(2,1)} %collective-permute-done.18.refs_11_), channel_id=1, source_target_pairs={{0,14},{2,0},{4,2},{6,4},{8,6},{10,8},{12,10},{14,12},{16,30},{18,... | collective-permute-start | bytes 2752520 | tf_op jit(solution)/shard_map/ppermute | solution.py:43
  152.9 22.3 %collective-permute-start.33 = (bf16[256,512]{1,0:T(8,128)(2,1)S(1)}, bf16[256,512]{1,0:T(8,128)(2,1)S(1)}, u32[]{:S(2)}, u32[]{:S(2)}) collective-permute-start(bf16[256,512]{1,0:T(8,128)(2,1)S(1)} %get-tuple-element.135.refs_1_), channel_id=1, source_target_pairs={{0,32},{32,0},{64,96},{96,64},{128,160},{160,128},{192,224},{224,1... | collective-permute-start | bytes 786440 | tf_op jit(solution)/shard_map/ppermute | solution.py:33
  354.5 28.4 %collective-permute-start.56 = (bf16[3,2,32,1152]{3,2,1,0:T(8,128)(2,1)S(1)}, bf16[3,2,32,1152]{3,2,1,0:T(8,128)(2,1)S(1)}, u32[]{:S(2)}, u32[]{:S(2)}) collective-permute-start(bf16[3,2,32,1152]{3,2,1,0:T(8,128)(2,1)S(1)} %bitcast.172), channel_id=1, source_target_pairs={{0,17},{1,16},{2,19},{3,18},{4,21},{5,20},{6,23},{7,22},{8,25},{9,... | collective-permute-start | bytes 1327112 | tf_op jit(solution)/shard_map/ppermute | solution.py:59
  370.7 21.5 %collective-permute-start.62 = (bf16[2,2,2,2,32,896]{5,4,3,2,1,0:T(8,128)(2,1)S(1)}, bf16[2,2,2,2,32,896]{5,4,3,2,1,0:T(8,128)(2,1)S(1)}, u32[]{:S(2)}, u32[]{:S(2)}) collective-permute-start(bf16[2,2,2,2,32,896]{5,4,3,2,1,0:T(8,128)(2,1)S(1)} %pad_maximum_fusion.4), channel_id=1, source_target_pairs={{0,14},{2,0},{4,2},{6,4},{8,6},{10,8},{12,10},{14,12},{16,30},{18,... | collective-permute-start | bytes 2752520 | tf_op jit(solution)/shard_map/ppermute | solution.py:43
  382.8 21.7 %collective-permute-start.61 = (bf16[2,2,2,2,32,896]{5,4,3,2,1,0:T(8,128)(2,1)S(1)}, bf16[2,2,2,2,32,896]{5,4,3,2,1,0:T(8,128)(2,1)S(1)}, u32[]{:S(2)}, u32[]{:S(2)}) collective-permute-start(bf16[2,2,2,2,32,896]{5,4,3,2,1,0:T(8,128)(2,1)S(1)} %pad_maximum_fusion.3), channel_id=1, source_target_pairs={{0,2},{2,4},{4,6},{6,8},{8,10},{10,12},{12,14},{14,0},{16,18},{18,... | collective-permute-start | bytes 2752520 | tf_op jit(solution)/shard_map/ppermute | solution.py:43
  383.3 21.8 %collective-permute-start.60 = (bf16[3,2,2,32,1152]{4,3,2,0,1:T(8,128)(2,1)S(1)}, bf16[3,2,2,32,1152]{4,3,2,0,1:T(8,128)(2,1)S(1)}, u32[]{:S(2)}, u32[]{:S(2)}) collective-permute-start(bf16[3,2,2,32,1152]{4,3,2,0,1:T(8,128)(2,1)S(1)} %pad_maximum_fusion.6), channel_id=1, source_target_pairs={{0,17},{1,16},{2,19},{3,18},{4,21},{5,20},{6,23},{7,22},{8,25},{9,... | collective-permute-start | bytes 2654216 | tf_op jit(solution)/shard_map/ppermute | solution.py:59
  385.1 20.0 %collective-permute-start.59 = (bf16[3,2,2,32,1152]{4,3,2,0,1:T(8,128)(2,1)S(1)}, bf16[3,2,2,32,1152]{4,3,2,0,1:T(8,128)(2,1)S(1)}, u32[]{:S(2)}, u32[]{:S(2)}) collective-permute-start(bf16[3,2,2,32,1152]{4,3,2,0,1:T(8,128)(2,1)S(1)} %pad_maximum_fusion.5), channel_id=1, source_target_pairs={{0,16},{2,18},{4,20},{6,22},{8,24},{10,26},{12,28},{14,30},{16,0},... | collective-permute-start | bytes 2654216 | tf_op jit(solution)/shard_map/ppermute | solution.py:49
  385.6 54.4 %collective-permute-start.54 = (bf16[256,512]{1,0:T(8,128)(2,1)S(1)}, bf16[256,512]{1,0:T(8,128)(2,1)S(1)}, u32[]{:S(2)}, u32[]{:S(2)}) collective-permute-start(bf16[256,512]{1,0:T(8,128)(2,1)S(1)} %get-tuple-element.168.left_ref), channel_id=1, source_target_pairs={{0,32},{32,0},{64,96},{96,64},{128,160},{160,128},{192,224},{224,1... | collective-permute-start | bytes 786440 | tf_op jit(solution)/shard_map/ppermute | solution.py:33
  408.8 21.8 %collective-permute-start.66 = (bf16[2,2,2,2,32,896]{5,4,3,2,1,0:T(8,128)(2,1)S(1)}, bf16[2,2,2,2,32,896]{5,4,3,2,1,0:T(8,128)(2,1)S(1)}, u32[]{:S(2)}, u32[]{:S(2)}) collective-permute-start(bf16[2,2,2,2,32,896]{5,4,3,2,1,0:T(8,128)(2,1)S(1)} %get-tuple-element.212), channel_id=1, source_target_pairs={{0,14},{2,0},{4,2},{6,4},{8,6},{10,8},{12,10},{14,12},{16,30},{18,... | collective-permute-start | bytes 2752520 | tf_op jit(solution)/shard_map/ppermute | solution.py:43
  409.2 21.3 %collective-permute-start.65 = (bf16[2,2,2,2,32,896]{5,4,3,2,1,0:T(8,128)(2,1)S(1)}, bf16[2,2,2,2,32,896]{5,4,3,2,1,0:T(8,128)(2,1)S(1)}, u32[]{:S(2)}, u32[]{:S(2)}) collective-permute-start(bf16[2,2,2,2,32,896]{5,4,3,2,1,0:T(8,128)(2,1)S(1)} %get-tuple-element.213), channel_id=1, source_target_pairs={{0,2},{2,4},{4,6},{6,8},{8,10},{10,12},{12,14},{14,0},{16,18},{18,... | collective-permute-start | bytes 2752520 | tf_op jit(solution)/shard_map/ppermute | solution.py:43
  410.8 21.6 %collective-permute-start.63 = (bf16[5,2,32,1152]{3,2,1,0:T(8,128)(2,1)S(1)}, bf16[5,2,32,1152]{3,2,1,0:T(8,128)(2,1)S(1)}, u32[]{:S(2)}, u32[]{:S(2)}) collective-permute-start(bf16[5,2,32,1152]{3,2,1,0:T(8,128)(2,1)S(1)} %bitcast.171), channel_id=1, source_target_pairs={{0,16},{2,18},{4,20},{6,22},{8,24},{10,26},{12,28},{14,30},{16,0},... | collective-permute-start | bytes 2211848 | tf_op jit(solution)/shard_map/ppermute | solution.py:49
  410.8 21.6 %collective-permute-start.64 = (bf16[5,2,32,1152]{3,2,1,0:T(8,128)(2,1)S(1)}, bf16[5,2,32,1152]{3,2,1,0:T(8,128)(2,1)S(1)}, u32[]{:S(2)}, u32[]{:S(2)}) collective-permute-start(bf16[5,2,32,1152]{3,2,1,0:T(8,128)(2,1)S(1)} %bitcast.170), channel_id=1, source_target_pairs={{0,17},{1,16},{2,19},{3,18},{4,21},{5,20},{6,23},{7,22},{8,25},{9,... | collective-permute-start | bytes 2211848 | tf_op jit(solution)/shard_map/ppermute | solution.py:59
  434.1 39.6 %collective-permute-start.69 = (bf16[5,2,2,32,1152]{4,3,2,1,0:T(8,128)(2,1)}, bf16[5,2,2,32,1152]{4,3,2,1,0:T(8,128)(2,1)S(1)}, u32[]{:S(2)}, u32[]{:S(2)}) collective-permute-start(bf16[5,2,2,32,1152]{4,3,2,1,0:T(8,128)(2,1)} %pad_maximum_fusion), channel_id=1, source_target_pairs={{0,16},{2,18},{4,20},{6,22},{8,24},{10,26},{12,28},{14,30},{16,0},... | collective-permute-start | bytes 4423688 | tf_op jit(solution)/shard_map/ppermute | solution.py:49
  435.5 38.2 %collective-permute-start.70 = (bf16[5,2,2,32,1152]{4,3,2,1,0:T(8,128)(2,1)}, bf16[5,2,2,32,1152]{4,3,2,1,0:T(8,128)(2,1)}, u32[]{:S(2)}, u32[]{:S(2)}) collective-permute-start(bf16[5,2,2,32,1152]{4,3,2,1,0:T(8,128)(2,1)} %pad_maximum_fusion.1), channel_id=1, source_target_pairs={{0,17},{1,16},{2,19},{3,18},{4,21},{5,20},{6,23},{7,22},{8,25},{9,... | collective-permute-start | bytes 4423688 | tf_op jit(solution)/shard_map/ppermute | solution.py:59
  438.5 31.4 %collective-permute-start.72 = (bf16[2,2,2,2,32,896]{5,4,3,2,1,0:T(8,128)(2,1)}, bf16[2,2,2,2,32,896]{5,4,3,2,1,0:T(8,128)(2,1)S(1)}, u32[]{:S(2)}, u32[]{:S(2)}) collective-permute-start(bf16[2,2,2,2,32,896]{5,4,3,2,1,0:T(8,128)(2,1)} %get-tuple-element.210), channel_id=1, source_target_pairs={{0,14},{2,0},{4,2},{6,4},{8,6},{10,8},{12,10},{14,12},{16,30},{18,... | collective-permute-start | bytes 2752520 | tf_op jit(solution)/shard_map/ppermute | solution.py:43
  438.8 31.1 %collective-permute-start.71 = (bf16[2,2,2,2,32,896]{5,4,3,2,1,0:T(8,128)(2,1)}, bf16[2,2,2,2,32,896]{5,4,3,2,1,0:T(8,128)(2,1)}, u32[]{:S(2)}, u32[]{:S(2)}) collective-permute-start(bf16[2,2,2,2,32,896]{5,4,3,2,1,0:T(8,128)(2,1)} %get-tuple-element.211), channel_id=1, source_target_pairs={{0,2},{2,4},{4,6},{6,8},{8,10},{10,12},{12,14},{14,0},{16,18},{18,... | collective-permute-start | bytes 2752520 | tf_op jit(solution)/shard_map/ppermute | solution.py:43
  440.7 23.0 %collective-permute-start.73 = (bf16[2,2,32,1152]{3,2,1,0:T(8,128)(2,1)}, bf16[2,2,32,1152]{3,2,1,0:T(8,128)(2,1)S(1)}, u32[]{:S(2)}, u32[]{:S(2)}) collective-permute-start(bf16[2,2,32,1152]{3,2,1,0:T(8,128)(2,1)} %pad_maximum_fusion.10), channel_id=1, source_target_pairs={{0,2},{2,4},{4,6},{6,8},{8,10},{10,12},{12,14},{14,0},{16,18},{18,... | collective-permute-start | bytes 884744 | tf_op jit(solution)/shard_map/ppermute | solution.py:43
  (139 other events, 1129.5 us)
